TPU v7x, 32 devices: a whole 2x2x4 slice. The times are simulated.
32 devices in a mesh: batch: 16 (over z, y, core), head: 2 (over x).
Axes of the slice: x: 2, y: 2, z: 4, core: 2. Of those that a mesh axis runs over, the one named last changes fastest.
Arguments:
- tokens: bfloat16 [32768, 1024], P(('batch', 'head')), may hold values from -6 to 6
- first_values: bfloat16 [32768, 1024], P('batch', 'head'), may hold values from -6 to 6
- out_grad: bfloat16 [32768, 1024], P(('batch', 'head')), may hold values from -6 to 6
- lengths: int32 [16], P('batch'), may hold values from 128 to 2048, as said below
- gain_attn: float32 [1024], replicated, may hold values from 0.25 to 1.75
- gain_mlp: float32 [1024], replicated, may hold values from 0.25 to 1.75
- w_query: bfloat16 [1024, 1024], P(None, 'head'), may hold values from -0.1875 to 0.1875
- w_key: bfloat16 [1024, 1024], P(None, 'head'), may hold values from -0.1875 to 0.1875
- w_value: bfloat16 [1024, 1024], P(None, 'head'), may hold values from -0.1875 to 0.1875
- w_out: bfloat16 [1024, 1024], P('head'), may hold values from -4 to 4
- w_gate: bfloat16 [1024, 2816], P(None, 'head'), may hold values from -0.1875 to 0.1875
- w_up: bfloat16 [1024, 2816], P(None, 'head'), may hold values from -0.1875 to 0.1875
- w_down: bfloat16 [2816, 1024], P('head'), may hold values from -0.109375 to 0.109375
Outputs:
- output: bfloat16 [32768, 1024], P(('batch', 'head'))
- grad_tokens: bfloat16 [32768, 1024], P(('batch', 'head'))
- grad_first_values: bfloat16 [32768, 1024], P('batch', 'head')
- grad_gain_attn: float32 [1024], replicated
- grad_gain_mlp: float32 [1024], replicated
- grad_w_query: float32 [1024, 1024], P(None, 'head')
- grad_w_key: float32 [1024, 1024], P(None, 'head')
- grad_w_value: float32 [1024, 1024], P(None, 'head')
- grad_w_out: float32 [1024, 1024], P('head')
- grad_w_gate: float32 [1024, 2816], P(None, 'head')
- grad_w_up: float32 [1024, 2816], P(None, 'head')
- grad_w_down: float32 [2816, 1024], P('head')
Inputs may be any that keep to these rules, and one draw needn't show every extreme that they name: lengths[b] counts the valid leading places of slot b; in every draw some slot has exactly 2048 and some exactly 128.
All inputs are finite; a program needn't handle non-finite values.
Results may differ from a plain program's by a relative error of at most 0.019.
Values may be sent and summed in bfloat16 or wider, within the bound.
A program may use at most 384 MiB of HBM per device.

v0:
```python
import math

import jax
import jax.numpy as jnp
from jax import lax
from jax.sharding import PartitionSpec as P

HEAD_DIM = 64
SLOT = 2048
BLOCK = 512


EPSILON = 1e-05
NEGATIVE = -1e30


def cross(left, right):
    return lax.dot_general(
        left, right, (((0,), (0,)), ((), ())), preferred_element_type=jnp.float32
    )


def against(left, right):
    return lax.dot_general(
        left, right, (((1,), (1,)), ((), ())), preferred_element_type=jnp.float32
    )


def normalize(values, gain):
    scale = lax.rsqrt(jnp.mean(values * values, axis=-1, keepdims=True) + EPSILON)
    normed = values * scale
    return (normed, scale, normed * gain)


def norm_back(grad_result, normed, scale, gain):
    grad_normed = grad_result * gain
    inner = jnp.mean(grad_normed * normed, axis=-1, keepdims=True)
    return (scale * (grad_normed - normed * inner), jnp.sum(grad_result * normed, axis=0))


def rope_tables(count):
    half = HEAD_DIM // 2
    position = (jnp.arange(count) % SLOT).astype(jnp.float32)
    frequency = jnp.exp(
        jnp.arange(half).astype(jnp.float32) * (-2.0 * math.log(10000.0) / HEAD_DIM)
    )
    angles = position[:, None] * frequency[None, :]
    return (jnp.cos(angles)[:, None, :], jnp.sin(angles)[:, None, :])


def rotate(values, cosine, sine, direction):
    half = values.shape[-1] // 2
    first = values[..., :half]
    second = values[..., half:]
    return jnp.concatenate(
        [first * cosine - direction * second * sine, second * cosine + direction * first * sine],
        axis=-1,
    )


def block_scores(query_block, key_block, row_start, column_start, length):
    scores = jnp.einsum(
        "qhd,khd->hqk", query_block, key_block, preferred_element_type=jnp.float32
    ) * (1.0 / math.sqrt(HEAD_DIM))
    rows = row_start + jnp.arange(query_block.shape[0])
    columns = column_start + jnp.arange(key_block.shape[0])
    allowed = (columns[None, :] <= rows[:, None]) & (columns[None, :] < length)
    return jnp.where(allowed[None], scores, NEGATIVE)


def attend_slot(queries, keys, values, length):
    count = SLOT // BLOCK
    heads = queries.shape[1]
    results = []
    sums = []
    for row_block in range(count):
        query_block = queries[row_block * BLOCK : (row_block + 1) * BLOCK]
        carry = (
            jnp.full((heads, BLOCK), NEGATIVE, jnp.float32),
            jnp.zeros((heads, BLOCK), jnp.float32),
        )
        for column_block in range(row_block + 1):
            key_block = keys[column_block * BLOCK : (column_block + 1) * BLOCK]

            def statistics(
                state,
                query_block=query_block,
                key_block=key_block,
                row_block=row_block,
                column_block=column_block,
            ):
                running, total = state
                scores = block_scores(
                    query_block, key_block, row_block * BLOCK, column_block * BLOCK, length
                )
                newest = jnp.maximum(running, jnp.max(scores, axis=-1))
                total = total * jnp.exp(running - newest) + jnp.sum(
                    jnp.exp(scores - newest[..., None]), axis=-1
                )
                return (newest, total)

            carry = statistics(carry)
        logsum = carry[0] + jnp.log(carry[1])
        accumulated = jnp.zeros((BLOCK, heads, HEAD_DIM), jnp.float32)
        for column_block in range(row_block + 1):
            key_block = keys[column_block * BLOCK : (column_block + 1) * BLOCK]
            value_block = values[column_block * BLOCK : (column_block + 1) * BLOCK]

            def combine(
                state,
                query_block=query_block,
                key_block=key_block,
                value_block=value_block,
                row_block=row_block,
                column_block=column_block,
                logsum=logsum,
            ):
                scores = block_scores(
                    query_block, key_block, row_block * BLOCK, column_block * BLOCK, length
                )
                weights = jnp.exp(scores - logsum[..., None]).astype(jnp.bfloat16)
                return state + jnp.einsum(
                    "hqk,khd->qhd", weights, value_block, preferred_element_type=jnp.float32
                )

            accumulated = combine(accumulated)
        results.append(accumulated)
        sums.append(logsum)
    return (jnp.concatenate(results, axis=0), jnp.concatenate(sums, axis=1))


def attend_back(queries, keys, values, grad_attended, delta, logsum, length):
    count = SLOT // BLOCK
    heads = queries.shape[1]
    scale = 1.0 / math.sqrt(HEAD_DIM)
    grad_keys = [jnp.zeros((BLOCK, heads, HEAD_DIM), jnp.float32) for column_block in range(count)]
    grad_values = [
        jnp.zeros((BLOCK, heads, HEAD_DIM), jnp.float32) for column_block in range(count)
    ]
    grad_queries = []
    for row_block in range(count):
        rows = slice(row_block * BLOCK, (row_block + 1) * BLOCK)
        query_block = queries[rows]
        grad_block = grad_attended[rows]
        delta_block = delta[:, rows]
        logsum_block = logsum[:, rows]
        grad_query = jnp.zeros((BLOCK, heads, HEAD_DIM), jnp.float32)
        for column_block in range(row_block + 1):
            key_block = keys[column_block * BLOCK : (column_block + 1) * BLOCK]
            value_block = values[column_block * BLOCK : (column_block + 1) * BLOCK]

            def update(
                state,
                query_block=query_block,
                grad_block=grad_block,
                delta_block=delta_block,
                logsum_block=logsum_block,
                key_block=key_block,
                value_block=value_block,
                row_block=row_block,
                column_block=column_block,
            ):
                grad_query, grad_key, grad_value = state
                scores = block_scores(
                    query_block, key_block, row_block * BLOCK, column_block * BLOCK, length
                )
                probs = jnp.exp(scores - logsum_block[..., None])
                grad_probs = jnp.einsum(
                    "qhd,khd->hqk", grad_block, value_block, preferred_element_type=jnp.float32
                )
                grad_scores = (probs * (grad_probs - delta_block[..., None])).astype(jnp.bfloat16)
                grad_query = grad_query + scale * jnp.einsum(
                    "hqk,khd->qhd", grad_scores, key_block, preferred_element_type=jnp.float32
                )
                grad_key = grad_key + scale * jnp.einsum(
                    "hqk,qhd->khd", grad_scores, query_block, preferred_element_type=jnp.float32
                )
                grad_value = grad_value + jnp.einsum(
                    "hqk,qhd->khd",
                    probs.astype(jnp.bfloat16),
                    grad_block,
                    preferred_element_type=jnp.float32,
                )
                return (grad_query, grad_key, grad_value)

            grad_query, grad_keys[column_block], grad_values[column_block] = update(
                (grad_query, grad_keys[column_block], grad_values[column_block])
            )
        grad_queries.append(grad_query)
    return (
        jnp.concatenate(grad_queries, axis=0),
        jnp.concatenate(grad_keys, axis=0),
        jnp.concatenate(grad_values, axis=0),
    )


def per_device(
    tokens,
    first_values,
    out_grad,
    lengths,
    gain_attn,
    gain_mlp,
    w_query,
    w_key,
    w_value,
    w_out,
    w_gate,
    w_up,
    w_down,
):
    local_rows = tokens.shape[0]
    width_here = w_query.shape[1]
    heads_here = width_here // HEAD_DIM
    slots_here = lengths.shape[0]
    group_rows = slots_here * SLOT
    inputs = tokens.astype(jnp.float32)
    normed_one, scale_one, gained_one = normalize(inputs, gain_attn)
    gathered_one = lax.all_gather(gained_one.astype(jnp.bfloat16), "head", axis=0, tiled=True)
    w_joint = jnp.concatenate([w_query, w_key, w_value], axis=1)
    joint = jnp.dot(gathered_one, w_joint, preferred_element_type=jnp.float32)
    cosine, sine = rope_tables(group_rows)
    queries = rotate(
        joint[:, :width_here].reshape(group_rows, heads_here, HEAD_DIM), cosine, sine, 1.0
    ).astype(jnp.bfloat16)
    keys = rotate(
        joint[:, width_here : 2 * width_here].reshape(group_rows, heads_here, HEAD_DIM),
        cosine,
        sine,
        1.0,
    ).astype(jnp.bfloat16)
    mixed = (
        (0.5 * joint[:, 2 * width_here :] + 0.5 * first_values.astype(jnp.float32))
        .astype(jnp.bfloat16)
        .reshape(group_rows, heads_here, HEAD_DIM)
    )
    slot = 0
    piece, logsum = attend_slot(queries, keys, mixed, lengths[slot])
    logsums = [logsum]
    attended_wide = piece.reshape(group_rows, width_here)
    attended = attended_wide.astype(jnp.bfloat16)
    middle = inputs + lax.psum_scatter(
        jnp.dot(attended, w_out, preferred_element_type=jnp.float32).astype(jnp.bfloat16),
        "head",
        scatter_dimension=0,
        tiled=True,
    ).astype(jnp.float32)
    normed_two, scale_two, gained_two = normalize(middle, gain_mlp)
    gathered_two = lax.all_gather(gained_two.astype(jnp.bfloat16), "head", axis=0, tiled=True)
    gate = jnp.dot(gathered_two, w_gate, preferred_element_type=jnp.float32)
    upper = jnp.dot(gathered_two, w_up, preferred_element_type=jnp.float32)
    sigmoid = jax.nn.sigmoid(gate)
    silu_gate = gate * sigmoid
    hidden = (silu_gate * upper).astype(jnp.bfloat16)
    output = middle + lax.psum_scatter(
        jnp.dot(hidden, w_down, preferred_element_type=jnp.float32).astype(jnp.bfloat16),
        "head",
        scatter_dimension=0,
        tiled=True,
    ).astype(jnp.float32)
    rows_global = lax.axis_index("head") * local_rows + jnp.arange(local_rows)
    slot_of = rows_global // SLOT
    position = rows_global % SLOT
    slot_length = jnp.sum(
        jnp.where(slot_of[:, None] == jnp.arange(slots_here)[None, :], lengths[None, :], 0), axis=1
    )
    valid = (position < slot_length).astype(jnp.float32)
    grad_output = out_grad.astype(jnp.float32) * valid[:, None]
    grad_branch = lax.all_gather(grad_output.astype(jnp.bfloat16), "head", axis=0, tiled=True)
    grad_w_down = cross(hidden, grad_branch)
    grad_hidden = against(grad_branch, w_down)
    grad_gate = (grad_hidden * upper * sigmoid * (1.0 + gate * (1.0 - sigmoid))).astype(
        jnp.bfloat16
    )
    grad_up = (grad_hidden * silu_gate).astype(jnp.bfloat16)
    grad_w_gate = cross(gathered_two, grad_gate)
    grad_w_up = cross(gathered_two, grad_up)
    grad_pair = jnp.concatenate([grad_gate, grad_up], axis=1)
    w_pair = jnp.concatenate([w_gate, w_up], axis=1)
    grad_two = lax.psum_scatter(
        against(grad_pair, w_pair).astype(jnp.bfloat16), "head", scatter_dimension=0, tiled=True
    ).astype(jnp.float32)
    grad_norm_two, grad_gain_two = norm_back(grad_two, normed_two, scale_two, gain_mlp)
    grad_middle = grad_output + grad_norm_two
    grad_attn = lax.all_gather(grad_middle.astype(jnp.bfloat16), "head", axis=0, tiled=True)
    grad_w_out = cross(attended, grad_attn)
    grad_attended = against(grad_attn, w_out).astype(jnp.bfloat16)
    delta = jnp.sum(
        (grad_attended.astype(jnp.float32) * attended_wide).reshape(
            group_rows, heads_here, HEAD_DIM
        ),
        axis=-1,
    ).T
    grad_attended = grad_attended.reshape(group_rows, heads_here, HEAD_DIM)
    slot = 0
    grad_query, grad_key, grad_value = attend_back(
        queries, keys, mixed, grad_attended, delta, logsums[slot], lengths[slot]
    )
    grad_mixed = grad_value.reshape(group_rows, width_here)
    grad_q_pre = rotate(grad_query, cosine, sine, -1.0).reshape(group_rows, width_here)
    grad_k_pre = rotate(grad_key, cosine, sine, -1.0).reshape(group_rows, width_here)
    grad_first = (0.5 * grad_mixed).astype(jnp.bfloat16)
    grad_joint = jnp.concatenate([grad_q_pre, grad_k_pre, 0.5 * grad_mixed], axis=1).astype(
        jnp.bfloat16
    )
    grad_w_joint = cross(gathered_one, grad_joint)
    grad_one = lax.psum_scatter(
        against(grad_joint, w_joint).astype(jnp.bfloat16), "head", scatter_dimension=0, tiled=True
    ).astype(jnp.float32)
    grad_norm_one, grad_gain_one = norm_back(grad_one, normed_one, scale_one, gain_attn)
    grad_inputs = grad_middle + grad_norm_one
    grad_w_query = grad_w_joint[:, :width_here]
    grad_w_key = grad_w_joint[:, width_here : 2 * width_here]
    grad_w_value = grad_w_joint[:, 2 * width_here :]
    (
        grad_w_query,
        grad_w_key,
        grad_w_value,
        grad_w_out,
        grad_w_gate,
        grad_w_up,
        grad_w_down,
        grad_gain_one,
        grad_gain_two,
    ) = lax.psum(
        (
            grad_w_query,
            grad_w_key,
            grad_w_value,
            grad_w_out,
            grad_w_gate,
            grad_w_up,
            grad_w_down,
            grad_gain_one,
            grad_gain_two,
        ),
        "batch",
    )
    grad_gain_one, grad_gain_two = lax.psum((grad_gain_one, grad_gain_two), "head")
    return (
        output.astype(jnp.bfloat16),
        grad_inputs.astype(jnp.bfloat16),
        grad_first,
        grad_gain_one,
        grad_gain_two,
        grad_w_query,
        grad_w_key,
        grad_w_value,
        grad_w_out,
        grad_w_gate,
        grad_w_up,
        grad_w_down,
    )


def solution(mesh):
    placed = (
        P(("batch", "head"), None),
        P("batch", "head"),
        P(("batch", "head"), None),
        P("batch"),
        P(),
        P(),
        P(None, "head"),
        P(None, "head"),
        P(None, "head"),
        P("head", None),
        P(None, "head"),
        P(None, "head"),
        P("head", None),
    )
    return jax.shard_map(
        per_device,
        mesh=mesh,
        in_specs=placed,
        out_specs=(
            P(("batch", "head"), None),
            P(("batch", "head"), None),
            P("batch", "head"),
            P(),
            P(),
            P(None, "head"),
            P(None, "head"),
            P(None, "head"),
            P("head", None),
            P(None, "head"),
            P(None, "head"),
            P("head", None),
        ),
        check_vma=False,
    )
```

profile of v0, /device:TPU:0, one launch (start us, length us, event | category | flops | bytes accessed | tf_op | source)
XLA Modules:
  0.0 1342.1 jit_solution(9649851812444378296)
XLA Ops:
  13.7 3.9 copy.25
  29.7 42.9 %all-gather.5.cloned.1.call-done = bf16[2048,1024]{1,0:T(8,128)(2,1)} async-done(((bf16[1024,1024]{1,0:T(8,128)(2,1)}), bf16[2048,1024]{1,0:T(8,128)(2,1)}) %all-gather.5.cloned.1.call-update) | async-done | bytes 4194320 | tf_op jit(solution)/shard_map/all_gather | solution.py:219
  72.6 12.5 fusion.145
  85.0 9.3 fusion.140
  97.4 3.8 add_convert_fusion.3
  102.9 4.7 fusion.27
  107.7 4.8 fusion.30
  115.6 5.3 fusion.24
  120.9 4.7 fusion.23
  125.6 4.7 fusion.25
  130.3 5.1 exponential_reduce_fusion.8
  135.4 5.5 exponential_reduce_fusion.7
  141.0 5.6 fusion.126
  146.6 5.1 exponential_reduce_fusion.6
  151.7 5.1 exponential_reduce_fusion.4
  158.6 5.6 fusion.120
  164.2 6.8 fusion.76
  175.9 5.3 fusion.31
  182.9 5.3 exponential_reduce_fusion
  195.0 4.6 fusion.114
  199.7 3.7 convolution_add_fusion.20
  223.1 4.4 convolution_convert_fusion.2
  231.0 51.0 %reduce-scatter.5.cloned.1.call-done = bf16[1024,1024]{1,0:T(8,128)(2,1)} async-done(((bf16[2048,1024]{1,0:T(8,128)(2,1)}), bf16[1024,1024]{1,0:T(8,128)(2,1)}) %reduce-scatter.5.cloned.1.call-update) | async-done | bytes 2097168 | tf_op jit(solution)/shard_map/reduce_scatter | solution.py:242
  285.0 4.3 multiply_convert_fusion.13
  289.4 51.6 %all-gather.9.cloned.1.call-done = bf16[2048,1024]{1,0:T(8,128)(2,1)} async-done(((bf16[1024,1024]{1,0:T(8,128)(2,1)}), bf16[2048,1024]{1,0:T(8,128)(2,1)}) %all-gather.9.cloned.1.call-update) | async-done | bytes 4194320 | tf_op jit(solution)/shard_map/all_gather | solution.py:269
  341.0 11.3 fusion.147
  352.3 47.5 %all-gather.7.cloned.1.call-done = bf16[2048,1024]{1,0:T(8,128)(2,1)} async-done(((bf16[1024,1024]{1,0:T(8,128)(2,1)}), bf16[2048,1024]{1,0:T(8,128)(2,1)}) %all-gather.7.cloned.1.call-update) | async-done | bytes 4194320 | tf_op jit(solution)/shard_map/all_gather | solution.py:249
  399.8 11.5 fusion.146
  411.3 18.7 %multiply_convert_fusion.1 = (bf16[2048,1408]{0,1:T(8,128)(2,1)}, bf16[2048,1408]{0,1:T(8,128)(2,1)}, bf16[2048,1408]{0,1:T(8,128)(2,1)}) fusion(f32[2048,1408]{0,1:T(8,128)} %fusion.147, f32[2048,1408]{0,1:T(8,128)} %fusion.146, bf16[2048,1024]{1,0:T(8,128)(2,1)S(1)} %copy-done.121, bf16[1024,1408]{1,0:T(8,128)(2,1)S(1)} %copy-done.124), kind=kOutput, calls=%fused_computation.5 | convolution fusion | flops 5948833792 | bytes 47448064 | tf_op jit(solution)/shard_map/dot_general | solution.py:250
  429.9 18.5 %fusion.50 = bf16[2048,1024]{1,0:T(8,128)(2,1)} fusion(bf16[1024,1408]{1,0:T(8,128)(2,1)} %param.24, bf16[1024,1408]{1,0:T(8,128)(2,1)} %param.23, bf16[2048,1408]{0,1:T(8,128)(2,1)} %get-tuple-element.45, bf16[2048,1408]{0,1:T(8,128)(2,1)} %get-tuple-element.44), kind=kOutput, calls=%fused_computation.114 | convolution fusion | flops 11847860224 | bytes 21495808 | tf_op jit(solution)/shard_map/dot_general | solution.py:24
  448.5 54.4 %reduce-scatter.9.cloned.1.call-done = bf16[1024,1024]{1,0:T(8,128)(2,1)} async-done(((bf16[2048,1024]{1,0:T(8,128)(2,1)}), bf16[1024,1024]{1,0:T(8,128)(2,1)}) %reduce-scatter.9.cloned.1.call-update) | async-done | bytes 2097168 | tf_op jit(solution)/shard_map/reduce_scatter | solution.py:280
  502.9 5.4 fusion.41
  508.9 4.3 fusion.135
  513.2 56.9 %all-gather.11.cloned.1.call-done = bf16[2048,1024]{1,0:T(8,128)(2,1)} async-done(((bf16[1024,1024]{1,0:T(8,128)(2,1)}), bf16[2048,1024]{1,0:T(8,128)(2,1)}) %all-gather.11.cloned.1.call-update) | async-done | bytes 4194320 | tf_op jit(solution)/shard_map/all_gather | solution.py:285
  570.1 6.2 bitcast_reduce_fusion
  577.5 6.7 fusion.128
  584.2 5.5 multiply_convert_fusion.12
  596.2 4.3 multiply_convert_fusion.6
  600.5 6.8 multiply_convert_fusion.3
  610.6 4.5 multiply_convert_fusion.9
  615.1 6.3 multiply_convert_fusion.7
  621.4 6.4 multiply_convert_fusion.4
  627.9 6.6 fusion.122
  634.5 4.7 multiply_convert_fusion.11
  639.2 8.6 multiply_convert_fusion.10
  647.8 6.3 multiply_convert_fusion.8
  654.1 6.2 multiply_convert_fusion.5
  660.3 7.1 convolution_add_fusion.5
  671.6 7.1 convolution_add_fusion.4
  684.1 6.8 fusion.59
  694.0 4.7 fusion.66
  704.4 3.7 fusion.152
  732.2 10.6 convolution_convert_fusion
  742.8 11.1 convolution_convert_fusion.1
  754.0 12.1 fusion.154
  766.0 10.6 fusion.155
  776.7 10.1 fusion.156
  786.8 9.0 fusion.56
  804.6 4.1 copy.76
  812.3 33.6 %all-reduce = (f32[1024]{0:T(1024)S(1)}, f32[1024]{0:T(1024)S(1)}) all-reduce(f32[1024]{0:T(1024)S(1)} %get-tuple-element.26, f32[1024]{0:T(1024)S(1)} %copy-done.113), channel_id=1, replica_groups=mesh['batch'=16,'head'=2] {'batch'}, use_global_device_ids=true, to_apply=%region_30.31 | all-reduce | flops 2048 | bytes 16384 | tf_op jit(solution)/shard_map/psum | solution.py:325
  846.0 6.0 all-reduce.2
  854.2 7.5 fusion.37
  861.7 454.6 %all-reduce.5.cloned.1.call-done = (f32[1024,512]{1,0:T(8,128)}, f32[1024,512]{1,0:T(8,128)}, f32[1024,512]{1,0:T(8,128)}, f32[512,1024]{1,0:T(8,128)}, f32[1024...) async-done(((f32[1024,512]{1,0:T(8,128)}, f32[1024,512]{1,0:T(8,128)}, f32[1024,512]{1,0:T(8,128)}, f32[512,1024]{1,0:T(8,128)}, f32[1024,1408]{1,0:T(8,128)}, ...) | async-done | bytes 25690128 | tf_op jit(solution)/shard_map/psum | solution.py:325
  1319.5 3.7 copy.138
  (434 shorter events, 150.4 us)
Async XLA Ops:
  7.2 333.8 %copy-start = (bf16[1408,1024]{1,0:T(8,128)(2,1)S(1)}, bf16[1408,1024]{1,0:T(8,128)(2,1)}, u32[]{:S(2)}) copy-start(bf16[1408,1024]{1,0:T(8,128)(2,1)} %param.25) | copy-start | bytes 8650756
  7.2 65.4 %all-gather.5.cloned.1.call-start = ((), (), s32[]{:S(2)}) async-start(), calls=%async_computation.4 | async-start | bytes 6291456 | tf_op jit(solution)/shard_map/all_gather | solution.py:219
  9.5 10.5 copy-start.108
  13.0 269.0 %reduce-scatter.5.cloned.1.call-start = ((), (), s32[]{:S(2)}) async-start(), calls=%async_computation.5 | async-start | bytes 6291456 | tf_op jit(solution)/shard_map/reduce_scatter | solution.py:242
  26.5 70.7 %copy-start.70 = (f32[2048,32]{0,1:T(8,128)}, f32[2048,32]{0,1:T(8,128)S(1)}, u32[]{:S(2)}) copy-start(f32[2048,32]{0,1:T(8,128)S(1)} %get-tuple-element.92) | copy-start | bytes 786436
  72.6 12.5 copy-start.37
  97.2 61.4 %copy-start.87 = (bf16[512,512]{0,1:T(8,128)(2,1)}, bf16[512,512]{0,1:T(8,128)(2,1)S(1)}, u32[]{:S(2)}) copy-start(bf16[512,512]{0,1:T(8,128)(2,1)S(1)} %get-tuple-element.73) | copy-start | bytes 1572868
  97.2 73.8 %copy-start.85 = (bf16[512,512]{0,1:T(8,128)(2,1)}, bf16[512,512]{0,1:T(8,128)(2,1)S(1)}, u32[]{:S(2)}) copy-start(bf16[512,512]{0,1:T(8,128)(2,1)S(1)} %get-tuple-element.72) | copy-start | bytes 1572868
  102.8 9.6 copy-start.31
  102.8 12.7 copy-start.9
  102.9 18.0 %copy-start.33 = (bf16[512,8,64]{0,2,1:T(8,128)(2,1)}, bf16[512,8,64]{0,2,1:T(8,128)(2,1)S(1)}, u32[]{:S(2)}) copy-start(bf16[512,8,64]{0,2,1:T(8,128)(2,1)S(1)} %get-tuple-element.133) | copy-start | bytes 1572868
  102.9 22.7 %copy-start.11 = (bf16[512,8,64]{0,2,1:T(8,128)(2,1)}, bf16[512,8,64]{0,2,1:T(8,128)(2,1)S(1)}, u32[]{:S(2)}) copy-start(bf16[512,8,64]{0,2,1:T(8,128)(2,1)S(1)} %get-tuple-element.131) | copy-start | bytes 1572868
  102.9 73.0 %copy-start.3 = (bf16[512,8,64]{0,2,1:T(8,128)(2,1)}, bf16[512,8,64]{0,2,1:T(8,128)(2,1)S(1)}, u32[]{:S(2)}) copy-start(bf16[512,8,64]{0,2,1:T(8,128)(2,1)S(1)} %get-tuple-element.132) | copy-start | bytes 1572868
  114.0 57.0 %copy-start.6 = (f32[8,512,512]{1,2,0:T(8,128)}, f32[8,512,512]{1,2,0:T(8,128)S(1)}, u32[]{:S(2)}) copy-start(f32[8,512,512]{1,2,0:T(8,128)S(1)} %get-tuple-element.114) | copy-start | bytes 25165828
  115.6 84.1 %copy-start.5 = (f32[8,512,512]{1,2,0:T(8,128)}, f32[8,512,512]{1,2,0:T(8,128)S(1)}, u32[]{:S(2)}) copy-start(f32[8,512,512]{1,2,0:T(8,128)S(1)} %get-tuple-element.108) | copy-start | bytes 25165828
  141.0 23.2 %copy-start.116 = (f32[8,512]{1,0:T(8,128)}, f32[8,512]{1,0:T(8,128)S(1)}, u32[]{:S(2)}) copy-start(f32[8,512]{1,0:T(8,128)S(1)} %log_add_fusion.2) | copy-start | bytes 49156
  158.6 12.4 copy-start.114
  175.8 19.1 %copy-start.7 = (f32[8,512,512]{1,2,0:T(8,128)}, f32[8,512,512]{1,2,0:T(8,128)S(1)}, u32[]{:S(2)}) copy-start(f32[8,512,512]{1,2,0:T(8,128)S(1)} %get-tuple-element.110) | copy-start | bytes 25165828
  181.2 7.0 slice-start.4
  195.0 10.8 copy-start.118
  195.0 8.4 slice-start.12
  227.5 57.4 %copy-start.104 = (f32[1024]{0:T(1024)S(1)}, f32[1024]{0:T(1024)}, u32[]{:S(2)}) copy-start(f32[1024]{0:T(1024)} %param.18) | copy-start | bytes 12292
  227.5 113.4 %all-gather.9.cloned.1.call-start = ((), (), s32[]{:S(2)}) async-start(), calls=%async_computation.8 | async-start | bytes 6291456 | tf_op jit(solution)/shard_map/all_gather | solution.py:269
  227.6 280.7 %copy-start.106 = (f32[1024]{0:T(1024)}, f32[1024]{0:T(1024)S(1)}, u32[]{:S(2)}) copy-start(f32[1024]{0:T(1024)S(1)} %fusion.97) | copy-start | bytes 12292
  231.0 168.8 %all-gather.7.cloned.1.call-start = ((), (), s32[]{:S(2)}) async-start(), calls=%async_computation.6 | async-start | bytes 6291456 | tf_op jit(solution)/shard_map/all_gather | solution.py:249
  285.0 223.3 %copy-start.102 = (f32[1024]{0:T(1024)}, f32[1024]{0:T(1024)S(1)}, u32[]{:S(2)}) copy-start(f32[1024]{0:T(1024)S(1)} %add_rsqrt_fusion) | copy-start | bytes 12292
  289.3 213.6 %reduce-scatter.9.cloned.1.call-start = ((), (), s32[]{:S(2)}) async-start(), calls=%async_computation.9 | async-start | bytes 6291456 | tf_op jit(solution)/shard_map/reduce_scatter | solution.py:280
  399.8 11.5 copy-start.121
  399.8 11.5 copy-start.124
  448.5 121.6 %all-gather.11.cloned.1.call-start = ((), (), s32[]{:S(2)}) async-start(), calls=%async_computation.10 | async-start | bytes 6291456 | tf_op jit(solution)/shard_map/all_gather | solution.py:285
  513.2 295.5 %reduce-scatter.11.cloned.1.call-start = ((), (), s32[]{:S(2)}) async-start(), calls=%async_computation.11 | async-start | bytes 6291456 | tf_op jit(solution)/shard_map/reduce_scatter | solution.py:307
  570.1 7.4 copy-start.69
  577.4 18.7 %copy-start.95 = (bf16[512,512]{0,1:T(8,128)(2,1)}, bf16[512,512]{0,1:T(8,128)(2,1)S(1)}, u32[]{:S(2)}) copy-start(bf16[512,512]{0,1:T(8,128)(2,1)S(1)} %get-tuple-element.64) | copy-start | bytes 1572868
  577.5 15.4 %slice-start.20 = ((s8[8388608]{0:T(1024)(128)(4,1)}), s8[4194304]{0:T(1024)(128)(4,1)S(1)}, s32[]{:S(2)}) async-start(s8[8388608]{0:T(1024)(128)(4,1)} %bitcast.199), calls=%async_computation.33 | async-start | bytes 8388608
  584.2 8.7 slice-start.21
  596.2 11.1 slice-start.14
  596.2 14.4 %slice-start.8 = ((s8[8388608]{0:T(1024)(128)(4,1)}), s8[4194304]{0:T(1024)(128)(4,1)S(1)}, s32[]{:S(2)}) async-start(s8[8388608]{0:T(1024)(128)(4,1)} %bitcast.187), calls=%async_computation.21 | async-start | bytes 8388608
  600.5 10.1 slice-start.9
  610.6 10.8 slice-start.6
  615.1 19.4 %slice-start.10 = ((s8[8388608]{0:T(1024)(128)(4,1)}), s8[4194304]{0:T(1024)(128)(4,1)S(1)}, s32[]{:S(2)}) async-start(s8[8388608]{0:T(1024)(128)(4,1)} %bitcast.189), calls=%async_computation.23 | async-start | bytes 8388608
  621.4 13.0 slice-start.11
  634.5 13.3 slice-start.2
  639.2 8.6 slice-start.3
  639.2 8.6 copy-start.48
  639.2 14.9 %slice-start = ((s8[8388608]{0:T(1024)(128)(4,1)}), s8[4194304]{0:T(1024)(128)(4,1)S(1)}, s32[]{:S(2)}) async-start(s8[8388608]{0:T(1024)(128)(4,1)} %bitcast.179), calls=%async_computation.13 | async-start | bytes 8388608
  660.3 7.1 copy-start.27
  690.8 7.9 copy-start.22
  694.0 7.1 copy-start.97
  694.0 7.1 copy-start.127
  742.8 111.4 %reduce-scatter.7.cloned.1.call-start = ((), (), s32[]{:S(2)}) async-start(), calls=%async_computation.7 | async-start | bytes 6291456 | tf_op jit(solution)/shard_map/reduce_scatter | solution.py:255
  753.9 562.3 %all-reduce.5.cloned.1.call-start = ((), (), s32[]{:S(2)}) async-start(), calls=%async_computation.12 | async-start | bytes 51380224 | tf_op jit(solution)/shard_map/psum | solution.py:325
  754.0 12.1 copy-start.122
  766.0 10.6 copy-start.120
  776.7 10.1 copy-start.36
  776.7 10.1 copy-start.77
  776.7 10.2 copy-start.79
  804.5 7.8 copy-start.113
  804.6 49.6 %copy-start.103 = (f32[1024]{0:T(1024)S(1)}, f32[1024]{0:T(1024)}, u32[]{:S(2)}) copy-start(f32[1024]{0:T(1024)} %copy-done.102) | copy-start | bytes 12292
  804.6 49.6 %copy-start.105 = (f32[1024]{0:T(1024)S(1)}, f32[1024]{0:T(1024)}, u32[]{:S(2)}) copy-start(f32[1024]{0:T(1024)} %param.18) | copy-start | bytes 12292
  804.6 49.6 %copy-start.107 = (f32[1024]{0:T(1024)S(1)}, f32[1024]{0:T(1024)}, u32[]{:S(2)}) copy-start(f32[1024]{0:T(1024)} %copy-done.106) | copy-start | bytes 12292
  804.6 49.6 %copy-start.111 = (f32[1024]{0:T(1024)S(1)}, f32[1024]{0:T(1024)}, u32[]{:S(2)}) copy-start(f32[1024]{0:T(1024)} %copy-done.110) | copy-start | bytes 12292
  1316.3 8.2 copy-start.74
  1316.3 9.6 slice-start.26
  1319.5 9.3 slice-start.24
  (102 other events, 393.4 us)
Sparse Core Ops, SparseCore 0:
  13.1 59.4 all-gather.4
  227.6 54.2 reduce-scatter.4
  284.2 56.7 all-gather.8
  343.0 56.7 all-gather.6
  448.6 54.3 reduce-scatter.8
  513.3 56.7 all-gather.10
  742.9 54.2 reduce-scatter.10
  799.6 54.4 reduce-scatter.6
  861.0 455.2 all-reduce.4
where the time goes:
time: 1350 us; the launch traced here: 1340 us
  waiting for transfers between devices  761 us (56%)
  matrix products  369 us (27%)
  other arithmetic  98.7 us (7%)
  local copies, waits for them, and re-layouts  56.8 us (4%)
  blocking collectives  39.6 us (3%)
  between operations  16.6 us (1%)
    psum x1, waiting for transfers between devices, per_device(): lax.psum((grad_w_query, grad_w_key, grad_w_value, grad_w_out, grad_w_gate...  455 us
    dot_general x10, matrix products, update(): jnp.einsum('qhd,khd->hqk', grad_block, value_block, preferred_element_typ...  59.4 us
    all_gather x1, waiting for transfers between devices, per_device(): lax.all_gather(grad_middle.astype(jnp.bfloat16), 'head', axis=0, tiled=True)  56.9 us
    reduce_scatter x1, waiting for transfers between devices, per_device(): lax.psum_scatter(against(grad_pair, w_pair).astype(jnp.bfloat16), 'head',...  54.4 us
    all_gather x1, waiting for transfers between devices, per_device(): lax.all_gather(grad_output.astype(jnp.bfloat16), 'head', axis=0, tiled=True)  51.6 us
    reduce_scatter x1, waiting for transfers between devices, per_device(): lax.psum_scatter(jnp.dot(attended, w_out, preferred_element_type=jnp.floa...  51 us
    dot_general x10, matrix products, update(): jnp.einsum('hqk,qhd->khd', probs.astype(jnp.bfloat16), grad_block, prefer...  48.7 us
    all_gather x1, waiting for transfers between devices, per_device(): lax.all_gather(gained_two.astype(jnp.bfloat16), 'head', axis=0, tiled=True)  47.5 us
  transfers between devices with their start and end apart: 9, of which 8 were waited for; matrix products, arithmetic and copies ran while one was open for 8% of the time, Pallas kernels for 0%

commit v1 on v0

v1 whole, which is shorter than its diff:
```python
import functools, math
import jax, jax.numpy as jnp
from jax import lax
from jax.experimental import pallas as pl
from jax.experimental.pallas import tpu as pltpu
from jax.sharding import Mesh, PartitionSpec as P
SLOT=2048; HEAD_DIM=64
C2=math.log2(math.e)/8.0
NT=(((1,),(1,)),((),()))
TN=(((0,),(0,)),((),()))
NN=(((1,),(0,)),((),()))
def dot(a,b,dims=NN): return lax.dot_general(a,b,dims,preferred_element_type=jnp.float32)

def fwd_kernel(BQ,BK,len_ref,q_ref,k_ref,v_ref,o_ref,lse_ref,kb_ref,s_ref):
    length=len_ref[0]
    lane=lax.broadcasted_iota(jnp.int32,(SLOT,128),1)
    row=lax.broadcasted_iota(jnp.int32,(SLOT,128),0)
    k=k_ref[...]; v=v_ref[...]
    vs=[]
    for h in range(2):
        mine=(lane//64)==h
        first=lane==(64*(1-h))
        bias=jnp.where(first&(row>=length),-1e30,0.0).astype(jnp.bfloat16)
        kb_ref[h]=jnp.where(mine,k,bias)
        kb_ref[2+h]=jnp.where(mine,v,jnp.ones_like(v))
    laneq=lax.broadcasted_iota(jnp.int32,(BQ,128),1)
    for i in range(SLOT//BQ):
        rows=slice(i*BQ,(i+1)*BQ)
        q=q_ref[rows,:]
        outs=[]
        for h in range(2):
            mine=(laneq//64)==h
            qh=jnp.where(mine,q,jnp.ones_like(q))
            ext=(i+1)*BQ
            nb=(ext+BK-1)//BK
            mx=None
            for j in range(nb):
                w=min(BK,ext-j*BK)
                s=dot(qh,kb_ref[h,pl.ds(j*BK,w),:],NT)
                if j*BK+w>i*BQ+1:
                    r=lax.broadcasted_iota(jnp.int32,(BQ,w),0)+i*BQ
                    c=lax.broadcasted_iota(jnp.int32,(BQ,w),1)+j*BK
                    s=jnp.where(c<=r,s,-1e30)
                s_ref[h,:,pl.ds(j*BK,w)]=s
                m=jnp.max(s,axis=-1,keepdims=True)
                mx=m if mx is None else jnp.maximum(mx,m)
            mc=mx*C2
            acc=None
            for j in range(nb):
                w=min(BK,ext-j*BK)
                p=jnp.exp2(s_ref[h,:,pl.ds(j*BK,w)]*C2-mc).astype(jnp.bfloat16)
                a=dot(p,kb_ref[2+h,pl.ds(j*BK,w),:])
                acc=a if acc is None else acc+a
            other=64*(1-h)
            l=acc[:,other:other+1]
            outs.append((acc/l,mc+jnp.log2(l)))
        o_ref[rows,:]=jnp.where((laneq//64)==0,outs[0][0],outs[1][0]).astype(jnp.bfloat16)
        lse_ref[0,:,pl.ds(i*BQ,BQ)]=jnp.where(lax.broadcasted_iota(jnp.int32,(BQ,128),1)==0,outs[0][1],outs[1][1]).T[0:8]
def att_fwd(length,q,k,v,BQ=512,BK=512):
    W=q.shape[1]; n=W//128
    blk=pl.BlockSpec((SLOT,128),lambda p:(0,p))
    return pl.pallas_call(functools.partial(fwd_kernel,BQ,BK),grid=(n,),
        in_specs=[pl.BlockSpec(memory_space=pltpu.SMEM),blk,blk,blk],
        out_specs=[blk,pl.BlockSpec((1,8,SLOT),lambda p:(p,0,0))],
        out_shape=[jax.ShapeDtypeStruct((SLOT,W),jnp.bfloat16),jax.ShapeDtypeStruct((n,8,SLOT),jnp.float32)],
        scratch_shapes=[pltpu.VMEM((4,SLOT,128),jnp.bfloat16),pltpu.VMEM((2,BQ,SLOT),jnp.float32)],
        compiler_params=pltpu.CompilerParams(vmem_limit_bytes=56<<20),name="attfwd_%d_%d"%(BQ,BK))(length,q,k,v)

def bwd_kernel(BQ,BK,len_ref,q_ref,k_ref,v_ref,do_ref,lse_ref,dl_ref,cos_ref,sin_ref,dq_ref,dk_ref,dv_ref,qs,ks,vs,dqa):
    length=len_ref[0]
    lane=lax.broadcasted_iota(jnp.int32,(SLOT,128),1)
    row=lax.broadcasted_iota(jnp.int32,(SLOT,128),0)
    k=k_ref[0]; q=q_ref[0]; do=do_ref[...]
    for h in range(2):
        mine=(lane//64)==h
        first=lane==(64*(1-h))
        bias=jnp.where(first&(row>=length),-1e30,0.0).astype(jnp.bfloat16)
        ks[h]=jnp.where(mine,k,bias)
        ks[2+h]=jnp.where(mine,k,jnp.zeros_like(k))
        qs[h]=jnp.where(mine,q,jnp.ones_like(q))
        qs[2+h]=jnp.where(mine,q,jnp.zeros_like(q))
        vs[h]=jnp.where(mine,do,jnp.zeros_like(do))
    dqa[...]=jnp.zeros_like(dqa)
    nq=SLOT//BQ
    for j in range(SLOT//BK):
        cols=slice(j*BK,(j+1)*BK)
        v=v_ref[0,cols,:]
        dk=dv=None
        for i in range((j*BK)//BQ,nq):
            rows=slice(i*BQ,(i+1)*BQ)
            for h in range(2):
                st=dot(ks[h,cols,:],qs[h,rows,:],NT)
                if (j+1)*BK>i*BQ+1:
                    c=lax.broadcasted_iota(jnp.int32,(BK,BQ),0)+j*BK
                    r=lax.broadcasted_iota(jnp.int32,(BK,BQ),1)+i*BQ
                    st=jnp.where(c<=r,st,-1e30)
                pt=jnp.exp2(st*C2-lse_ref[0,h:h+1,rows])
                dpt=dot(v,vs[h,rows,:],NT)
                dst=(pt*(dpt-dl_ref[0,h:h+1,rows])).astype(jnp.bfloat16)
                a=dot(pt.astype(jnp.bfloat16),vs[h,rows,:])
                dv=a if dv is None else dv+a
                b=dot(dst,qs[2+h,rows,:])
                dk=b if dk is None else dk+b
                dqa[rows,:]+=dot(dst,ks[2+h,cols,:],TN)
        lf=(lax.broadcasted_iota(jnp.int32,(BK,128),1)%64)<32
        dk_ref[cols,:]=rot(dk*0.125,cos_ref[cols,:],-sin_ref[cols,:],lf).astype(dk_ref.dtype)
        dv_ref[cols,:]=(dv*0.5).astype(dv_ref.dtype)
    lf=(lax.broadcasted_iota(jnp.int32,(SLOT,128),1)%64)<32
    dq_ref[...]=rot(dqa[...]*0.125,cos_ref[...],-sin_ref[...],lf).astype(dq_ref.dtype)
def att_bwd(length,q,k,v,do,lse,delta,cos,sin,BQ=512,BK=512,odt=jnp.bfloat16):
    tab=pl.BlockSpec((SLOT,128),lambda p:(0,0),pipeline_mode=pl.Buffered(1))
    n=q.shape[0]; W=n*128
    blk=pl.BlockSpec((SLOT,128),lambda p:(0,p)); tri=pl.BlockSpec((1,SLOT,128),lambda p:(p,0,0))
    st=pl.BlockSpec((1,8,SLOT),lambda p:(p,0,0))
    return pl.pallas_call(functools.partial(bwd_kernel,BQ,BK),grid=(n,),
        in_specs=[pl.BlockSpec(memory_space=pltpu.SMEM),tri,tri,tri,blk,st,st,tab,tab],
        out_specs=[blk,blk,blk],
        out_shape=[jax.ShapeDtypeStruct((SLOT,W),odt)]*3,
        scratch_shapes=[pltpu.VMEM((4,SLOT,128),jnp.bfloat16),pltpu.VMEM((4,SLOT,128),jnp.bfloat16),pltpu.VMEM((2,SLOT,128),jnp.bfloat16),pltpu.VMEM((SLOT,128),jnp.float32)],
        compiler_params=pltpu.CompilerParams(vmem_limit_bytes=56<<20),name="attbwd_%d_%d"%(BQ,BK))(length,q,k,v,do,lse,delta,cos,sin)

EPS=1e-5
R2=256
def norm_block(x,gain):
    r=lax.rsqrt(jnp.mean(x*x,axis=-1,keepdims=True)+EPS)
    n=x*r
    return n,r
def rot(x,cos,sin,lane_first):
    up=pltpu.roll(x,96,1)
    dn=pltpu.roll(x,32,1)
    return x*cos+jnp.where(lane_first,up,dn)*sin

def qkv_kernel(R,t_ref,f_ref,g_ref,cos_ref,sin_ref,wq,wk,wv,q_ref,k_ref,m_ref):
    x=t_ref[...].astype(jnp.float32)
    n,_=norm_block(x,None)
    h=(n*g_ref[...]).astype(jnp.bfloat16)
    cos=cos_ref[...]; sin=sin_ref[...]
    lf=(lax.broadcasted_iota(jnp.int32,(R,128),1)%64)<32
    for w,o in ((wq,q_ref),(wk,k_ref)):
        y=dot(h,w[...])
        for c in range(y.shape[1]//128):
            o[:,c*128:(c+1)*128]=rot(y[:,c*128:(c+1)*128],cos,sin,lf).astype(jnp.bfloat16)
    y=dot(h,wv[...])
    m_ref[...]=(0.5*y+0.5*f_ref[...].astype(jnp.float32)).astype(jnp.bfloat16)
def qkv_fwd(t,f,gain,cos,sin,wq,wk,wv,R=256):
    N,D=t.shape; W=wq.shape[1]
    rb=lambda w:pl.BlockSpec((R,w),lambda i:(i,0))
    full=lambda a:pl.BlockSpec(a.shape,lambda i:(0,0),pipeline_mode=pl.Buffered(1))
    return pl.pallas_call(functools.partial(qkv_kernel,R),grid=(N//R,),
        in_specs=[rb(D),rb(W),full(gain),rb(128),rb(128),full(wq),full(wk),full(wv)],
        out_specs=[rb(W)]*3,out_shape=[jax.ShapeDtypeStruct((N,W),jnp.bfloat16)]*3,
        compiler_params=pltpu.CompilerParams(vmem_limit_bytes=56<<20),name="qkvfwd_%d"%R)(t,f,gain,cos,sin,wq,wk,wv)

def mlp_kernel(R,NS,FH,len_ref,t_ref,pa_ref,pb_ref,og_ref,g_ref,wg_h,wu_h,wd_h,wg_f,wu_f,wd_f,
               op_ref,gh_ref,comb_h,
               wgu,wd,agu,ad,stage,wsem,ssem):
    step=pl.program_id(0)
    D=t_ref.shape[1]
    diag=lax.axis_index("core")==lax.axis_index("head")
    load=lambda a,b,c:[pltpu.make_async_copy(a,wgu.at[:,pl.ds(0,FH)],wsem.at[0]),
         pltpu.make_async_copy(b,wgu.at[:,pl.ds(FH,FH)],wsem.at[1]),
         pltpu.make_async_copy(c,wd,wsem.at[2])]
    cps=load(wg_h,wu_h,wd_h); far=load(wg_f,wu_f,wd_f)
    @pl.when(step==0)
    def _():
        @pl.when(diag)
        def _():
            for c in cps: c.start()
        @pl.when(jnp.logical_not(diag))
        def _():
            for c in far: c.start()
        agu[...]=jnp.zeros_like(agu)
        ad[...]=jnp.zeros_like(ad)
        for c in cps: c.wait()
    x=t_ref[...].astype(jnp.float32)+(pa_ref[...].astype(jnp.float32)+pb_ref[...].astype(jnp.float32))
    n,_=norm_block(x,None)
    h=(n*g_ref[...]).astype(jnp.bfloat16)
    row=lax.broadcasted_iota(jnp.int32,(R,1),0)+step*R
    g=jnp.where(row<len_ref[0],og_ref[...],jnp.zeros((),jnp.bfloat16))
    gu=dot(h,wgu[...])
    gate=gu[:,:FH]; up=gu[:,FH:]
    gh=dot(g,wd[...],NT)
    sg=0.5*jnp.tanh(0.5*gate)+0.5
    silu=gate*sg
    hid=(silu*up).astype(jnp.bfloat16)
    gu_=(gh*silu).astype(jnp.bfloat16)
    gg_=(gh*up*(sg*(1.0+gate*(1.0-sg)))).astype(jnp.bfloat16)
    op_ref[...]=dot(hid,wd[...]).astype(jnp.bfloat16)
    gh_ref[...]=(dot(gg_,wgu[:,:FH],NT)+dot(gu_,wgu[:,FH:],NT)).astype(jnp.bfloat16)
    ad[...]+=dot(hid,g,TN)
    agu[:,:FH]+=dot(h,gg_,TN)
    agu[:,FH:]+=dot(h,gu_,TN)
    @pl.when(step==NS-1)
    def _():
        tiles=[(agu,c,c*D,D) for c in range(2*FH//128)]+[(ad,c,(2*FH//128)*D+c*FH,FH) for c in range(D//128)]
        pend=[None]*4
        for i,(a,c,off,ln) in enumerate(tiles):
            s=i%4
            if pend[s] is not None: pend[s].wait()
            stage[s,0:ln,:]=a[:,c*128:(c+1)*128].astype(jnp.bfloat16)
            cp=pltpu.make_async_copy(stage.at[s,pl.ds(0,ln)],comb_h.at[pl.ds(off,ln)],ssem.at[s])
            cp.start(); pend[s]=cp
        for p in pend: p.wait()
def mlp(length,t,pa,pb,og,gain,wg,wu,wd,wg_f,wu_f,wd_f,R=256):
    N,D=t.shape; FH=wg.shape[1]; NS=N//R
    rb=pl.BlockSpec((R,D),lambda i:(i,0))
    anyb=pl.BlockSpec(memory_space=pl.ANY)
    full=lambda a:pl.BlockSpec(a.shape,lambda i:(0,0),pipeline_mode=pl.Buffered(1))
    rows=(2*FH//128)*D+(D//128)*FH
    return pl.pallas_call(functools.partial(mlp_kernel,R,NS,FH),grid=(NS,),
        in_specs=[pl.BlockSpec(memory_space=pltpu.SMEM),rb,rb,rb,rb,full(gain)]+[anyb]*6,
        out_specs=[rb,rb,anyb],
        out_shape=[jax.ShapeDtypeStruct((N,D),jnp.bfloat16)]*2+[jax.ShapeDtypeStruct((rows,128),jnp.bfloat16)],
        scratch_shapes=[pltpu.VMEM((D,2*FH),jnp.bfloat16),pltpu.VMEM((FH,D),jnp.bfloat16),pltpu.VMEM((D,2*FH),jnp.float32),pltpu.VMEM((FH,D),jnp.float32),
            pltpu.VMEM((4,max(D,FH),128),jnp.bfloat16),pltpu.SemaphoreType.DMA((3,)),pltpu.SemaphoreType.DMA((4,))],
        compiler_params=pltpu.CompilerParams(vmem_limit_bytes=60<<20),name="mlp_%d"%R)(length,t,pa,pb,og,gain,wg,wu,wd,wg_f,wu_f,wd_f)

def mid_kernel(R,NS,len_ref,t_ref,pa_ref,pb_ref,og_ref,ga_ref,gb_ref,at_ref,g_ref,wo,
               gm_ref,gat_ref,dl_ref,gwo_ref,gg_ref,acc):
    step=pl.program_id(0)
    x=t_ref[...].astype(jnp.float32)+(pa_ref[...].astype(jnp.float32)+pb_ref[...].astype(jnp.float32))
    n,r=norm_block(x,None)
    gh2=ga_ref[...].astype(jnp.float32)+gb_ref[...].astype(jnp.float32)
    row=lax.broadcasted_iota(jnp.int32,(R,1),0)+step*R
    mg=jnp.where(row<len_ref[0],og_ref[...].astype(jnp.float32),0.0)
    gn=gh2*g_ref[...]
    inner=jnp.mean(gn*n,axis=-1,keepdims=True)
    gm=(mg+r*(gn-n*inner)).astype(jnp.bfloat16)
    gm_ref[...]=gm
    part=jnp.sum((gh2*n).reshape(R//8,8,-1),axis=0)
    at=at_ref[...]
    ga=dot(gm,wo[...],NT).astype(jnp.bfloat16)
    gat_ref[...]=ga
    xx=ga.astype(jnp.float32)*at.astype(jnp.float32)
    hi=xx.astype(jnp.bfloat16); lo=(xx-hi.astype(jnp.float32)).astype(jnp.bfloat16)
    W=at.shape[1]
    hr=lax.broadcasted_iota(jnp.int32,(8*(W//128),W),0); ln=lax.broadcasted_iota(jnp.int32,(8*(W//128),W),1)
    ind=((ln//64)==((hr//8)*2+hr%8)) & (hr%8<2)
    ind=jnp.where(ind,1.0,0.0).astype(jnp.bfloat16)
    d=dot(ind,hi,NT)+dot(ind,lo,NT)
    dl_ref[...]=d.reshape(W//128,8,R)
    w=dot(at,gm,TN)
    @pl.when(step==0)
    def _():
        acc[...]=w; gg_ref[...]=part
    @pl.when(step>0)
    def _():
        acc[...]+=w; gg_ref[...]+=part
    @pl.when(step==NS-1)
    def _():
        for c in range(acc.shape[1]//128):
            gwo_ref[c*W:(c+1)*W,:]=acc[:,c*128:(c+1)*128].astype(jnp.bfloat16)
def mid(length,t,pa,pb,og,ga,gb,at,gain,wo,R=256):
    N,D=t.shape; W=at.shape[1]; NS=N//R
    rb=lambda w:pl.BlockSpec((R,w),lambda i:(i,0))
    full=lambda a:pl.BlockSpec(a.shape,lambda i:(0,0),pipeline_mode=pl.Buffered(1))
    return pl.pallas_call(functools.partial(mid_kernel,R,NS),grid=(NS,),
        in_specs=[pl.BlockSpec(memory_space=pltpu.SMEM)]+[rb(D)]*6+[rb(W),full(gain),full(wo)],
        out_specs=[rb(D),rb(W),pl.BlockSpec((W//128,8,R),lambda i:(0,0,i)),pl.BlockSpec((W*D//128,128),lambda i:(0,0)),pl.BlockSpec((8,D),lambda i:(0,0))],
        out_shape=[jax.ShapeDtypeStruct((N,D),jnp.bfloat16),jax.ShapeDtypeStruct((N,W),jnp.bfloat16),jax.ShapeDtypeStruct((W//128,8,N),jnp.float32),
            jax.ShapeDtypeStruct((W*D//128,128),jnp.bfloat16),jax.ShapeDtypeStruct((8,D),jnp.float32)],
        scratch_shapes=[pltpu.VMEM((W,D),jnp.float32)],
        compiler_params=pltpu.CompilerParams(vmem_limit_bytes=56<<20),name="mid_%d"%R)(length,t,pa,pb,og,ga,gb,at,gain,wo)

def qkvb_kernel(R,NS,t_ref,q_ref,k_ref,v_ref,g_ref,wq,wk,wv,gh_ref,gw_ref,acc):
    step=pl.program_id(0)
    x=t_ref[...].astype(jnp.float32)
    n,_=norm_block(x,None)
    h=(n*g_ref[...]).astype(jnp.bfloat16)
    gq=q_ref[...]; gk=k_ref[...]; gv=v_ref[...]
    gh_ref[...]=(dot(gq,wq[...],NT)+dot(gk,wk[...],NT)+dot(gv,wv[...],NT)).astype(jnp.bfloat16)
    W=gq.shape[1]; D=x.shape[1]
    @pl.when(step==0)
    def _(): acc[...]=jnp.zeros_like(acc)
    for i,g in enumerate((gq,gk,gv)):
        acc[:,i*W:(i+1)*W]+=dot(h,g,TN)
    @pl.when(step==NS-1)
    def _():
        for c in range(3*W//128):
            gw_ref[c*D:(c+1)*D,:]=acc[:,c*128:(c+1)*128].astype(jnp.bfloat16)
def qkv_bwd(t,gq,gk,gv,gain,wq,wk,wv,R=256):
    N,D=t.shape; W=wq.shape[1]; NS=N//R
    rb=lambda w:pl.BlockSpec((R,w),lambda i:(i,0))
    full=lambda a:pl.BlockSpec(a.shape,lambda i:(0,0),pipeline_mode=pl.Buffered(1))
    return pl.pallas_call(functools.partial(qkvb_kernel,R,NS),grid=(NS,),
        in_specs=[rb(D),rb(W),rb(W),rb(W),full(gain),full(wq),full(wk),full(wv)],
        out_specs=[rb(D),pl.BlockSpec((3*W*D//128,128),lambda i:(0,0))],
        out_shape=[jax.ShapeDtypeStruct((N,D),jnp.bfloat16),jax.ShapeDtypeStruct((3*W*D//128,128),jnp.bfloat16)],
        scratch_shapes=[pltpu.VMEM((D,3*W),jnp.float32)],
        compiler_params=pltpu.CompilerParams(vmem_limit_bytes=56<<20),name="qkvb_%d"%R)(t,gq,gk,gv,gain,wq,wk,wv)

def unpack_kernel(b_ref,o_ref): o_ref[...]=b_ref[...].astype(jnp.float32)
def unpack(buf,off,D,W):
    o=off//D
    return pl.pallas_call(unpack_kernel,grid=(W//128,),in_specs=[pl.BlockSpec((D,128),lambda c:(o+c,0))],
       out_specs=pl.BlockSpec((D,128),lambda c:(0,c)),out_shape=jax.ShapeDtypeStruct((D,W),jnp.float32),name="unpack_%d"%W)(buf)


ALL=("zy","core","head")

class Links:
    def __init__(self,send,recv,local):
        self.send,self.recv,self.local=send,recv,local
        self.remote_count=0; self.local_count=0
    def remote(self,src,dst,device):
        at=self.remote_count; self.remote_count+=1
        return pltpu.make_async_remote_copy(src_ref=src,dst_ref=dst,send_sem=self.send.at[at],recv_sem=self.recv.at[at],
            device_id=device,device_id_type=pl.DeviceIdType.MESH)
    def copy(self,src,dst):
        at=self.local_count; self.local_count+=1
        return pltpu.make_async_copy(src,dst,self.local.at[at])

def spread_bits(groups):
    count=min(groups,8); bits=[]
    while count>1:
        count//=2; bits.append(count)
    return bits

class Spread:
    def __init__(self,links,home,full,bits,zy,swap_dev,peer):
        m=2**len(bits); rows=home.shape[0]//m
        place=0
        for level,b in enumerate(bits): place=place+((zy//b)%2)*(2**level)
        one=pl.ds(pl.multiple_of(place*rows,rows),rows)
        self.steps=[links.remote(home.at[one],full.at[one],swap_dev)]
        for level,b in enumerate(bits):
            size=2**level
            block=pl.ds(pl.multiple_of((place//size)*size*rows,size*rows),size*rows)
            self.steps.append(links.remote(full.at[block],full.at[block],peer(b)))

def front_kernel(groups,
        tok_h,fv_h,og_h,len_h,g_ref,ch_ref,sh_ref,cl_ref,sl_ref,wq_h,wk_h,wv_h,wo_h,wg_h,wu_h,wd_h,
        tok_o,og_o,len_o,q_o,k_o,m_o,att_o,lse_o,pa_o,pb_o,wq_o,wk_o,wv_o,wo_o,wg_o,wu_o,wd_o,
        tok_v,len_v,fv_v,wq_v,wk_v,wv_v,wo_v,cos_v,sin_v,qs,ks,vp,ms,kb_ref,s_ref,att_v,lse_v,pa_v,
        send_sem,recv_sem,local_sem):
    zy=lax.axis_index("zy"); core=lax.axis_index("core"); x=lax.axis_index("head")
    off=core!=x; diag=core==x
    L=Links(send_sem,recv_sem,local_sem)
    swap_dev=(zy,1-core,1-x); core_dev=(zy,1-core,x)
    bits=spread_bits(groups)
    peer=lambda b:(zy+b-2*b*((zy//b)%2),core,x)
    barrier=pltpu.get_barrier_semaphore()
    MESH=pl.DeviceIdType.MESH
    half=tok_h.shape[0]; D=tok_h.shape[1]; W=wq_h.shape[1]; NP=W//128
    CH=256; NC=half//CH
    sp={n:Spread(L,h,f,bits,zy,swap_dev,peer) for n,h,f in (("q",wq_h,wq_v),("k",wk_h,wk_v),("v",wv_h,wv_v),("o",wo_h,wo_v),("g",wg_h,wg_o),("u",wu_h,wu_o),("d",wd_h,wd_o))}
    mine=lambda k:pl.ds(pl.multiple_of(core*half+k*CH,CH),CH)
    swap_len=L.remote(len_h,len_v,swap_dev)
    there=lambda k:pl.ds(pl.multiple_of((1-core)*half+k*CH,CH),CH)
    swap_tok=[L.remote(tok_h.at[pl.ds(k*CH,CH)],tok_v.at[there(k)],swap_dev) for k in range(NC)]
    core_tok=[L.remote(tok_v.at[mine(k)],tok_v.at[mine(k)],core_dev) for k in range(NC)]
    swap_fv=[L.remote(fv_h.at[:,pl.ds(p*128,128)],fv_v.at[p],swap_dev) for p in range(NP)]
    HH=half//2
    part=lambda c,j:pl.ds(pl.multiple_of(c*half+j*HH,HH),HH)
    swap_og=[L.remote(og_h.at[pl.ds(j*HH,HH)],og_o.at[part(1-core,j)],swap_dev) for j in range(2)]
    my_half=pl.ds(pl.multiple_of(core*half,half),half)
    core_og=[L.remote(og_o.at[part(core,j)],og_o.at[part(core,j)],core_dev) for j in range(2)]
    PR=512
    core_pa=[L.remote(pa_v.at[pl.ds(r*PR,PR)],pb_o.at[pl.ds(r*PR,PR)],core_dev) for r in range(SLOT//PR)]
    out_pa=[L.copy(pa_v.at[pl.ds(r*PR,PR)],pa_o.at[pl.ds(r*PR,PR)]) for r in range(SLOT//PR)]
    own_tok=L.copy(tok_h,tok_v.at[my_half])
    own_len=L.copy(len_h,len_v)
    own_fv=[L.copy(fv_h.at[:,pl.ds(p*128,128)],fv_v.at[p]) for p in range(NP)]
    own_og=[L.copy(og_h,pa_v.at[pl.ds(0,half)]),L.copy(pa_v.at[pl.ds(0,half)],og_o.at[my_half])]
    core_og_own=[L.remote(og_h.at[pl.ds(j*HH,HH)],og_o.at[part(core,j)],core_dev) for j in range(2)]
    own_qkv=[L.copy(h,v) for h,v in ((wq_h,wq_v),(wk_h,wk_v),(wv_h,wv_v))]
    own_o=L.copy(wo_h,wo_v)
    outs=[L.copy(a,b) for a,b in ((tok_v,tok_o),(len_v,len_o),(qs,q_o),(ks,k_o),(wq_v,wq_o),(wk_v,wk_o),(wv_v,wv_o))]
    outs2=[L.copy(a,b) for a,b in ((ms,m_o),(att_v,att_o),(lse_v,lse_o),(wo_v,wo_o))]

    pl.semaphore_signal(barrier,inc=1,device_id=core_dev,device_id_type=MESH)
    @pl.when(off)
    def _():
        pl.semaphore_signal(barrier,inc=1,device_id=swap_dev,device_id_type=MESH)
        for b in bits: pl.semaphore_signal(barrier,inc=1,device_id=peer(b),device_id_type=MESH)
        pl.semaphore_wait(barrier,2+len(bits))
        for n in "qkvog": sp[n].steps[0].start()
        swap_len.start()
    @pl.when(diag)
    def _():
        pl.semaphore_wait(barrier,1)
        own_tok.start(); own_len.start()
        for c in own_qkv: c.start()
        own_tok.wait()
        for k in range(NC): core_tok[k].start()
        own_len.wait()
        for c in own_fv: c.start()
        own_o.start(); own_og[0].start()
        for c in core_og_own: c.start()
    sign=jnp.where((lax.broadcasted_iota(jnp.int32,(1,128),1)%64)<32,-1.0,1.0)
    cl=cl_ref[...]; sl=sl_ref[...]
    def table(a,_):
        rows=pl.ds(pl.multiple_of(a*32,32),32)
        ch=ch_ref[pl.ds(a,1),:]; sh=sh_ref[pl.ds(a,1),:]
        cos_v[rows,:]=ch*cl-sh*sl
        sin_v[rows,:]=(sh*cl+ch*sl)*sign
        return 0
    lax.fori_loop(0,SLOT//32,table,0)
    nl=len(bits)
    def advance(n,level):
        sp[n].steps[level].wait_recv(); sp[n].steps[level+1].start()
    @pl.when(off)
    def _():
        for level in range(nl):
            for n in ("qkvog" if level<max(nl-1,1) else "qkv"): advance(n,level)
            if level==0:
                for k in range(NC): swap_tok[k].start()
        swap_len.wait_recv()
    @pl.when(diag)
    def _():
        for c in own_qkv: c.wait()
        own_og[0].wait(); own_og[1].start()
    gain=g_ref[...]
    lf=(lax.broadcasted_iota(jnp.int32,(CH,128),1)%64)<32
    def project(block):
        rows=pl.ds(pl.multiple_of(block*CH,CH),CH)
        t=tok_v[rows,:].astype(jnp.float32)
        n,_=norm_block(t,None)
        h=(n*gain).astype(jnp.bfloat16)
        cos=cos_v[rows,:]; sin=sin_v[rows,:]
        for w,o in ((wq_v,qs),(wk_v,ks)):
            y=dot(h,w[...])
            for c in range(NP):
                o[c,rows,:]=rot(y[:,c*128:(c+1)*128],cos,sin,lf).astype(jnp.bfloat16)
        y=dot(h,wv_v[...])
        for c in range(NP): vp[c,rows,:]=y[:,c*128:(c+1)*128]
    for k in range(NC):
        if k==0:
            @pl.when(off)
            def _():
                for n in "qkv": sp[n].steps[nl].wait_recv()
        @pl.when(off)
        def _():
            core_tok[k].wait_recv()
        project(x*NC+k)
        @pl.when(off)
        def _():
            if k==0: sp["u"].steps[0].start(); swap_fv[0].start()
            if k==1 and nl>1: advance("o",nl-1)
            if k==2 and nl>1: advance("g",nl-1)
            if k==3: advance("u",0)
    for k in range(NC):
        @pl.when(off)
        def _():
            swap_tok[k].wait_recv()
            core_tok[k].start()
            if k==1: swap_fv[1].start(); sp["d"].steps[0].start()
        @pl.when(diag)
        def _():
            core_tok[k].wait_recv()
        project((1-x)*NC+k)
    @pl.when(off)
    def _():
        swap_fv[2].start(); swap_fv[3].start()
    for c in outs: c.start()
    plan={}
    todo=lambda slot,act: plan.setdefault(slot,[]).append(act)
    for level in range(1,nl): todo(4*(level-1),functools.partial(advance,"u",level))
    for level in range(nl): todo(3+4*level if level<2 else 10,functools.partial(advance,"d",level))
    todo(4,swap_og[0].start); todo(7,swap_og[1].start)
    todo(12,lambda:(swap_og[0].wait_recv(),core_og[0].start()))
    BQ,BK=512,512
    laneq=lax.broadcasted_iota(jnp.int32,(BQ,128),1)
    lane=lax.broadcasted_iota(jnp.int32,(SLOT,128),1)
    row=lax.broadcasted_iota(jnp.int32,(SLOT,128),0)
    def pair(p,_):
        for at in range(NP):
            @pl.when((p==at)&off)
            def _(): swap_fv[at].wait_recv()
            @pl.when((p==at)&diag)
            def _(): own_fv[at].wait()
        m=(0.5*vp[p]+0.5*fv_v[p].astype(jnp.float32)).astype(jnp.bfloat16)
        ms[p]=m
        k=ks[p]
        length=len_v[0:1,:]
        for h in range(2):
            own=(lane//64)==h
            first=lane==(64*(1-h))
            bias=jnp.where(first&(row>=length),-1e30,0.0).astype(jnp.bfloat16)
            kb_ref[h]=jnp.where(own,k,bias)
            kb_ref[2+h]=jnp.where(own,m,jnp.ones_like(m))
        for i in range(SLOT//BQ):
            for at in range(NP):
                acts=plan.get(at*4+i)
                if acts:
                    @pl.when((p==at)&off)
                    def _():
                        for a in acts: a()
            rows=slice(i*BQ,(i+1)*BQ)
            q=qs[p,rows,:]
            got=[]
            for h in range(2):
                own=(laneq//64)==h
                qh=jnp.where(own,q,jnp.ones_like(q))
                mx=None
                for j in range(i+1):
                    s=dot(qh,kb_ref[h,pl.ds(j*BK,BK),:],NT)
                    if j==i:
                        r=lax.broadcasted_iota(jnp.int32,(BQ,BK),0); c=lax.broadcasted_iota(jnp.int32,(BQ,BK),1)
                        s=jnp.where(c<=r,s,-1e30)
                    s_ref[h,:,pl.ds(j*BK,BK)]=s
                    m_=jnp.max(s,axis=-1,keepdims=True)
                    mx=m_ if mx is None else jnp.maximum(mx,m_)
                mc=mx*C2
                acc=None
                for j in range(i+1):
                    pr=jnp.exp2(s_ref[h,:,pl.ds(j*BK,BK)]*C2-mc).astype(jnp.bfloat16)
                    a=dot(pr,kb_ref[2+h,pl.ds(j*BK,BK),:])
                    acc=a if acc is None else acc+a
                other=64*(1-h)
                l=acc[:,other:other+1]
                got.append((acc/l,mc+jnp.log2(l)))
            att_v[rows,pl.ds(pl.multiple_of(p*128,128),128)]=jnp.where((laneq//64)==0,got[0][0],got[1][0]).astype(jnp.bfloat16)
            lse_v[p,:,i*BQ:(i+1)*BQ]=jnp.where(lax.broadcasted_iota(jnp.int32,(BQ,128),1)==0,got[0][1],got[1][1]).T[0:8]
        return 0
    lax.fori_loop(0,NP,pair,0)
    @pl.when(off)
    def _():
        sp["o"].steps[nl].wait_recv()
        swap_og[1].wait_recv(); core_og[1].start()
    @pl.when(diag)
    def _():
        own_o.wait(); own_og[1].wait()
    for c in outs2: c.start()
    for r in range(SLOT//PR):
        pa_v[r*PR:(r+1)*PR,:]=dot(att_v[r*PR:(r+1)*PR,:],wo_v[...]).astype(jnp.bfloat16)
        core_pa[r].start(); out_pa[r].start()
    for c in outs+outs2+out_pa: c.wait()
    for c in core_pa: c.wait()
    for k in range(NC): core_tok[k].wait_send()
    @pl.when(diag)
    def _():
        for c in core_og_own: c.wait_send()
        for c in core_og: c.wait_recv()
    @pl.when(off)
    def _():
        for c in core_og: c.wait_send()
        for c in core_og_own: c.wait_recv()
        for n in "gud": sp[n].steps[nl].wait_recv()
        for n in "qkvogud":
            for s in sp[n].steps: s.wait_send()
        swap_len.wait_send()
        for c in swap_tok+swap_fv+swap_og: c.wait_send()

def front(groups,tok,fv,og,length,gain,tables,ws):
    N=SLOT; D=tok.shape[1]; W=ws[0].shape[1]; NP=W//128; FH=ws[4].shape[1]
    bf=jnp.bfloat16; f32=jnp.float32
    S=jax.ShapeDtypeStruct
    outs=[S((N,D),bf),S((N,D),bf),S((8,128),jnp.int32),S((NP,N,128),bf),S((NP,N,128),bf),S((NP,N,128),bf),S((N,W),bf),S((NP,8,N),f32),S((N,D),bf),S((N,D),bf)]+[S(w.shape,bf) for w in ws]
    anyb=pl.BlockSpec(memory_space=pl.ANY); vm=pl.BlockSpec(memory_space=pltpu.VMEM)
    V=pltpu.VMEM
    scratch=[V((N,D),bf),V((8,128),jnp.int32),V((NP,N,128),bf),V((D,W),bf),V((D,W),bf),V((D,W),bf),V((W,D),bf),V((N,128),f32),V((N,128),f32),
        V((NP,N,128),bf),V((NP,N,128),bf),V((NP,N,128),f32),V((NP,N,128),bf),V((4,N,128),bf),V((2,512,N),f32),V((N,W),bf),V((NP,8,N),f32),V((N,D),bf),
        pltpu.SemaphoreType.DMA((56,)),pltpu.SemaphoreType.DMA((56,)),pltpu.SemaphoreType.DMA((32,))]
    return pl.pallas_call(functools.partial(front_kernel,groups),out_shape=outs,
        in_specs=[anyb]*4+[vm]*5+[anyb]*7,out_specs=[anyb]*len(outs),scratch_shapes=scratch,
        compiler_params=pltpu.CompilerParams(collective_id=0,has_side_effects=True,vmem_limit_bytes=58<<20),name="front")(tok,fv,og,length,gain,*tables,*ws)
def exchange(v,perm): return lax.ppermute(v,ALL,perm)
def halve(buf,perm,bit):
    half=buf.shape[0]//2
    keep=lax.dynamic_slice_in_dim(buf,bit*half,half,0)
    send=lax.dynamic_slice_in_dim(buf,(1-bit)*half,half,0)
    got=exchange(send,perm)
    return (keep.astype(jnp.float32)+got.astype(jnp.float32)).astype(jnp.bfloat16)

def per_device(groups,tokens,first_values,out_grad,lengths,gain_attn,gain_mlp,w_query,w_key,w_value,w_out,w_gate,w_up,w_down):
    bf=jnp.bfloat16; f32=jnp.float32
    n=groups
    lin=lambda i,c,x:(i*2+c)*2+x
    each=lambda fn:[(lin(i,c,x),lin(*fn(i,c,x))) for i in range(n) for c in range(2) for x in range(2)]
    swap=each(lambda i,c,x:(i,x,c))
    swap_some=[p for p in swap if p[0]!=p[1]]
    over_core=each(lambda i,c,x:(i,1-c,x))
    over_x=each(lambda i,c,x:(i,c,1-x))
    zy=lax.axis_index("zy"); core=lax.axis_index("core"); x_at=lax.axis_index("head")
    half=tokens.shape[0]
    D=tokens.shape[1]
    def mine_of(v): return lax.dynamic_slice_in_dim(v,core*half,half,0)
    def other_of(v): return lax.dynamic_slice_in_dim(v,(1-core)*half,half,0)
    def home(v):
        return jnp.where(core==x_at,v,exchange(v,swap_some))
    g1=gain_attn.reshape(1,D); g2=gain_mlp.reshape(1,D)
    lanes=jnp.arange(128)%(HEAD_DIM//2)
    frequency=jnp.exp(lanes.astype(f32)*(-2.0*math.log(10000.0)/HEAD_DIM))
    coarse=(jnp.arange(SLOT//32)*32).astype(f32)[:,None]*frequency[None,:]
    fine=jnp.arange(32).astype(f32)[:,None]*frequency[None,:]
    tables=(jnp.cos(coarse),jnp.sin(coarse),jnp.cos(fine),jnp.sin(fine))
    length8=jnp.broadcast_to(lengths.reshape(1,1),(8,128))
    (tok,og,len_full,q,k,mixed,att,lse,pa,pb,w_q,w_k,w_v,w_o,w_g,w_u,w_d)=front(n,tokens,first_values,out_grad,length8,g1,tables,(w_query,w_key,w_value,w_out,w_gate,w_up,w_down))
    length=len_full[0,:1]
    tok_half=mine_of(tok)
    angles=jnp.arange(SLOT).astype(f32)[:,None]*frequency[None,:]
    cos=jnp.cos(angles); sin=jnp.sin(angles)*jnp.where((jnp.arange(128)%64)<32,-1.0,1.0)
    op,gh2a,comb=mlp(length,tok,pa,pb,og,g2,w_gate,w_up,w_down,w_g,w_u,w_d)
    op_recv=exchange(other_of(op),over_core)
    middle=tok_half.astype(f32)+(mine_of(pa).astype(f32)+mine_of(pb).astype(f32))
    out=(middle+(mine_of(op).astype(f32)+op_recv.astype(f32))).astype(bf)
    out=home(out)
    gh2b=exchange(gh2a,over_core)
    gm,gat,delta,gwo,gg2=mid(length,tok,pa,pb,og,gh2a,gh2b,att,g2,w_o,512)
    dq,dk,dv=att_bwd(length,q,k,mixed,gat,lse,delta,cos,sin)
    grad_first=home(dv)
    gh1,gwqkv=qkv_bwd(tok,dq,dk,dv,g1,w_q,w_k,w_v,512)
    gh1_recv=exchange(other_of(gh1),over_core)
    gh1_full=mine_of(gh1).astype(f32)+gh1_recv.astype(f32)
    xt=tok_half.astype(f32)
    r1=lax.rsqrt(jnp.mean(xt*xt,axis=-1,keepdims=True)+EPS)
    n1=xt*r1
    gn=gh1_full*g1
    gt=mine_of(gm).astype(f32)+r1*(gn-n1*jnp.mean(gn*n1,axis=-1,keepdims=True))
    grad_tokens=home(gt.astype(bf))
    gg1=jnp.sum(gh1_full*n1,axis=0)
    gains=lax.psum(jnp.stack([gg1,0.5*jnp.sum(gg2,axis=0)]),ALL)
    bits=[]
    b=1
    while b<n:
        bits.append((each(lambda i,c,x,b=b:(i^b,c,x)),(zy//b)%2,b)); b*=2
    def reduce_all(buf):
        buf=halve(buf,over_x,x_at)
        for perm,bit,_ in bits: buf=halve(buf,perm,bit)
        piece=home(buf)
        got=lax.all_gather(piece,"zy",axis=0,tiled=False)
        order=[int(format(i,"0%db"%len(bits))[::-1],2) for i in range(n)]
        got=jnp.concatenate([got[o] for o in order],0)
        other=exchange(got,over_core)
        return jnp.where(core==0,jnp.concatenate([got,other],0),jnp.concatenate([other,got],0))
    FH=w_gate.shape[1]; W=w_query.shape[1]
    cut=(2*FH//128)*D
    cs=reduce_all(comb)
    os=reduce_all(jnp.concatenate([gwo,gwqkv],0))
    gwg=unpack(cs,0,D,FH); gwu=unpack(cs,cut//2,D,FH); gwd=unpack(cs[cut:],0,FH,D)
    rest=os.shape[0]-gwqkv.shape[0]
    gwo_=unpack(os,0,W,D)
    gq,gk,gv=[unpack(os,rest+j*(W//128)*D,D,W) for j in range(3)]
    return (out,grad_tokens,grad_first,gains[0],gains[1],gq,gk,gv,gwo_,gwg,gwu,gwd)

def solution(mesh):
    fine=Mesh(mesh.devices.reshape(-1,2,2),ALL)
    rows=P(ALL,None); slot=P(("zy","core"),"head"); col=P(None,"head"); row=P("head",None)
    return jax.shard_map(functools.partial(per_device,fine.devices.shape[0]),mesh=fine,
        in_specs=(rows,slot,rows,P(("zy","core")),P(),P(),col,col,col,row,col,col,row),
        out_specs=(rows,rows,slot,P(),P(),col,col,col,row,col,col,row),check_vma=False)
```

time: 1350 us -> 699 us (0.52)
  waiting for transfers between devices: 761 us -> 137 us
  matrix products: 369 us -> 0 us
  Pallas kernels: 0 us -> 340 us
  other arithmetic: 98.7 us -> 44 us
  starting transfers between devices: 0.37 us -> 22.3 us
  blocking collectives: 39.6 us -> 58.6 us
  local copies, waits for them, and re-layouts: 56.8 us -> 72.6 us
    psum x1 -> x0, waiting for transfers between devices: 455 us -> none  [per_device(): lax.psum((grad_w_query, grad_w_key, grad_w_value, grad_w_out, grad_w_gate...]
    dot_general x74 -> x0, matrix products: 369 us -> none  [the longest x10 59.4 us: update(): jnp.einsum('qhd,khd->hqk', grad_block, value_block, preferred_element_typ...]
    pallas_call x0 -> x12, Pallas kernels: none -> 340 us  [the longest x1 117 us: front(): pl.pallas_call(functools.partial(front_kernel, groups), out_shape=outs, i...]
    all_gather x4 -> x2, waiting for transfers between devices: 199 us -> 8.25 us  [reduce_all(): got = lax.all_gather(piece, 'zy', axis=0, tiled=False)]
    ppermute x0 -> x18, waiting for transfers between devices: none -> 129 us  [exchange(): return lax.ppermute(v, ALL, perm)]
    reduce_scatter x4 -> x0, waiting for transfers between devices: 108 us -> none  [the longest x1 54.4 us: per_device(): lax.psum_scatter(against(grad_pair, w_pair).astype(jnp.bfloat16), 'head',...]
    reduce_sum x14 -> x3, other arithmetic: 51.5 us -> 4.33 us  [the longest x1 3.83 us: per_device(): gg1 = jnp.sum(gh1_full * n1, axis=0)]
    ppermute x0 -> x18, starting transfers between devices: none -> 22.2 us  [exchange(): return lax.ppermute(v, ALL, perm)]
  transfers between devices with their start and end apart: 9 -> 20, of which waited for: 8 -> 7; matrix products, arithmetic and copies ran while one was open for 8% -> 12% of each run, Pallas kernels for 0% -> 18%
where the time goes in v1:
time: 699 us; the launch traced here: 690 us
  Pallas kernels  340 us (49%)
  waiting for transfers between devices  137 us (20%)
  local copies, waits for them, and re-layouts  72.6 us (10%)
  blocking collectives  58.6 us (8%)
  other arithmetic  44 us (6%)
  starting transfers between devices  22.3 us (3%)
  between operations  15.6 us (2%)
    ppermute x18, waiting for transfers between devices, exchange(): return lax.ppermute(v, ALL, perm)  129 us
    pallas_call x1, Pallas kernels, front(): pl.pallas_call(functools.partial(front_kernel, groups), out_shape=outs, i...  117 us
    pallas_call x1, Pallas kernels, mlp(): pl.pallas_call(functools.partial(mlp_kernel, R, NS, FH), grid=(NS,), in_s...  76.8 us
    pallas_call x1, Pallas kernels, att_bwd(): pl.pallas_call(functools.partial(bwd_kernel, BQ, BK), grid=(n,), in_specs...  66.7 us
    psum x1, blocking collectives, per_device(): gains = lax.psum(jnp.stack([gg1, 0.5 * jnp.sum(gg2, axis=0)]), ALL)  58.6 us
    unnamed x71, local copies, waits for them, and re-layouts  42.8 us
    pallas_call x7, Pallas kernels, unpack(): pl.pallas_call(unpack_kernel, grid=(W // 128,), in_specs=[pl.BlockSpec((D...  38.1 us
    ppermute x18, starting transfers between devices, exchange(): return lax.ppermute(v, ALL, perm)  22.2 us
  transfers between devices with their start and end apart: 20, of which 7 were waited for; matrix products, arithmetic and copies ran while one was open for 12% of the time, Pallas kernels for 18%

profile of v1, /device:TPU:0, one launch (start us, length us, event | category | flops | bytes accessed | tf_op | source)
XLA Modules:
  0.0 690.3 jit_solution(1509053921956352510)
XLA Ops:
  10.1 117.2 %front.1 = (bf16[2048,1024]{1,0:T(8,128)(2,1)}, bf16[2048,1024]{1,0:T(8,128)(2,1)}, s32[8,128]{1,0:T(8,128)}, bf16[4,2048,128]{2,1,0:T(8,128)(2,1)}, bf16[4,2048...) custom-call(bf16[1024,1024]{1,0:T(8,128)(2,1)} %tok_h.1, ...), custom_call_target="tpu_custom_call" | custom-call | tf_op jit(solution)/shard_map/front/pallas_call | solution.py:555
  127.3 1.2 slice.60
  128.4 76.8 %mlp_256.1 = (bf16[2048,1024]{1,0:T(8,128)(2,1)}, bf16[2048,1024]{1,0:T(8,128)(2,1)}, bf16[33792,128]{1,0:T(8,128)(2,1)}) custom-call(s32[1]{0:T(128)} %bitcast.2.len_ref, bf16[2048,1024]{1,0:T(8,128)(2,1)} %get-tuple-element.42.t_ref, bf16[2048,1024]{1,0:T(8,128)(2,1)} %get-tuple-element.43.pa_ref, bf16[2048,1024]{1,0:T(8,128)(2,1)} %get-tuple-element.44.pb_ref, ...), custom_call_target="tpu_custom_call" | custom-call | tf_op jit(solution)/shard_map/mlp_256/pallas_call | solution.py:210
  205.5 5.1 constant_dynamic-slice_fusion.2
  210.7 1.6 collective-permute-start.12
  212.3 5.5 fusion.13
  217.8 19.8 %mid_512.1 = (bf16[2048,1024]{1,0:T(8,128)(2,1)}, bf16[2048,512]{1,0:T(8,128)(2,1)}, f32[4,8,2048]{2,1,0:T(8,128)}, bf16[4096,128]{1,0:T(8,128)(2,1)}, f32[8,1024]{1,0:T(8,128)}) custom-call(s32[1]{0:T(128)} %bitcast.2.len_ref, bf16[2048,1024]{1,0:T(8,128)(2,1)} %get-tuple-element.42.t_ref, bf16[2048,1024]{1,0:T(8,128)(2,1)} %get-tuple-element.43.pa_ref, ...), custom_call_target="tpu_custom_call" | custom-call | tf_op jit(solution)/shard_map/mid_512/pallas_call | solution.py:257
  237.6 66.7 %attbwd_512_512.1 = (bf16[2048,512]{1,0:T(8,128)(2,1)}, bf16[2048,512]{1,0:T(8,128)(2,1)}, bf16[2048,512]{1,0:T(8,128)(2,1)}) custom-call(s32[1]{0:T(128)} %bitcast.2.len_ref, bf16[4,2048,128]{2,1,0:T(8,128)(2,1)} %get-tuple-element.55.q_ref, bf16[4,2048,128]{2,1,0:T(8,128)(2,1)} %get-tuple-element.56.k_ref, bf16[4,2048,128]{2,1,0:T(8,128)(2,1)} %get-tuple-element.57.v_ref, ...), custom_call_target="tpu_custom_call" | custom-call | tf_op jit(solution)/shard_map/attbwd_512_512/pallas_call | solution.py:115
  304.3 21.4 %qkvb_512.1 = (bf16[2048,1024]{1,0:T(8,128)(2,1)}, bf16[12288,128]{1,0:T(8,128)(2,1)}) custom-call(bf16[2048,1024]{1,0:T(8,128)(2,1)} %get-tuple-element.42.t_ref, bf16[2048,512]{1,0:T(8,128)(2,1)} %get-tuple-element.61.q_ref, bf16[2048,512]{1,0:T(8,128)(2,1)} %get-tuple-element.62.k_ref, bf16[2048,512]{1,0:T(8,128)(2,1)} %get-tuple-element.63.v_ref, ...), custom_call_target="tpu_custom_call" | custom-call | tf_op jit(solution)/shard_map/qkvb_512/pallas_call | solution.py:285
  325.8 2.3 constant_dynamic-update-slice_fusion
  328.9 3.5 add_convert_fusion
  333.2 42.6 %collective-permute-done.6 = bf16[8192,128]{1,0:T(8,128)(2,1)S(1)} collective-permute-done((bf16[8192,128]{1,0:T(8,128)(2,1)S(1)}, bf16[8192,128]{1,0:T(8,128)(2,1)S(1)}, u32[]{:S(2)}, u32[]{:S(2)}) %collective-permute-start.6) | collective-permute-done | bytes 2097184 | tf_op jit(solution)/shard_map/ppermute | solution.py:558
  376.9 5.7 collective-permute-done.13
  383.2 20.8 %collective-permute-done.7 = bf16[4096,128]{1,0:T(8,128)(2,1)S(1)} collective-permute-done((bf16[4096,128]{1,0:T(8,128)(2,1)S(1)}, bf16[4096,128]{1,0:T(8,128)(2,1)S(1)}, u32[]{:S(2)}, u32[]{:S(2)}) %collective-permute-start.7) | collective-permute-done | bytes 1048608 | tf_op jit(solution)/shard_map/ppermute | solution.py:558
  404.4 4.2 collective-permute-start.8
  409.6 11.8 %collective-permute-done.8 = bf16[2048,128]{1,0:T(8,128)(2,1)S(1)} collective-permute-done((bf16[2048,128]{1,0:T(8,128)(2,1)S(1)}, bf16[2048,128]{1,0:T(8,128)(2,1)S(1)}, u32[]{:S(2)}, u32[]{:S(2)}) %collective-permute-start.8) | collective-permute-done | bytes 524320 | tf_op jit(solution)/shard_map/ppermute | solution.py:558
  421.6 1.5 collective-permute-start.9
  423.1 1.5 constant_dynamic-slice_fusion.8
  424.5 3.2 constant_dynamic-slice_fusion.7
  428.3 19.5 %collective-permute-done.9 = bf16[1024,128]{1,0:T(8,128)(2,1)S(1)} collective-permute-done((bf16[1024,128]{1,0:T(8,128)(2,1)S(1)}, bf16[1024,128]{1,0:T(8,128)(2,1)S(1)}, u32[]{:S(2)}, u32[]{:S(2)}) %collective-permute-start.9) | collective-permute-done | bytes 262176 | tf_op jit(solution)/shard_map/ppermute | solution.py:558
  449.1 2.1 collective-permute-start.5
  451.9 1.7 add_convert_fusion.3
  453.7 3.5 collective-permute-start.15
  457.2 3.8 fusion.8
  461.0 28.5 %collective-permute-done.15 = bf16[2112,128]{1,0:T(8,128)(2,1)S(1)} collective-permute-done((bf16[2112,128]{1,0:T(8,128)(2,1)S(1)}, bf16[2112,128]{1,0:T(8,128)(2,1)S(1)}, u32[]{:S(2)}, u32[]{:S(2)}) %collective-permute-start.15) | collective-permute-done | bytes 540704 | tf_op jit(solution)/shard_map/ppermute | solution.py:558
  490.4 7.3 %fusion.7 = (bf16[1024,1024]{1,0:T(8,128)(2,1)S(1)}, bf16[1024,1024]{1,0:T(8,128)(2,1)}) fusion(bf16[1024,1024]{1,0:T(8,128)(2,1)} %collective-permute-done.3, f32[1024]{0:T(1024)S(1)} %broadcast_multiply_fusion.1, f32[1024]{0:T(1024)S(1)} %copy-done.6, f32[1024]{0:T(1024)S(1)} %add_rsqrt_fusion, bf16[2048,1024]{1,0:T(8,128)(2,1)} %get-tuple-element.54, ...), kind=kLoop, calls=%fused_computation.13 | loop fusion | flops 22020096 | bytes 20983812 | tf_op jit(solution)/shard_map/convert_element_type | solution.py:611
  497.7 2.2 collective-permute-start.1
  499.9 2.0 collective-permute-start.4
  502.7 8.3 %all-gather.5.cloned.1.call-done = bf16[8192,128]{1,0:T(8,128)(2,1)} async-done(((bf16[1024,128]{1,0:T(8,128)(2,1)}), bf16[8192,128]{1,0:T(8,128)(2,1)}) %all-gather.5.cloned.1.call-update) | async-done | bytes 2097168 | tf_op jit(solution)/shard_map/all_gather | solution.py:622
  511.0 1.7 slice_dynamic-update-slice_fusion.46
  512.7 1.7 slice_dynamic-update-slice_fusion.43
  514.3 1.7 slice_dynamic-update-slice_fusion.40
  516.0 1.7 slice_dynamic-update-slice_fusion.37
  517.7 1.7 slice_dynamic-update-slice_fusion.34
  519.3 1.7 slice_dynamic-update-slice_fusion.31
  521.0 1.7 slice_dynamic-update-slice_fusion.28
  522.7 1.7 slice_dynamic-update-slice_fusion.25
  524.5 58.6 %psum.7 = f32[2,1024]{1,0:T(2,128)S(1)} all-reduce(f32[2,1024]{1,0:T(2,128)S(1)} %pad_maximum_fusion), channel_id=1, replica_groups=mesh['zy'=8,'core'=2,'head'=2] {'zy','core','head'}, use_global_device_ids=true, to_apply=%region_4.5 | all-reduce | flops 2048 | bytes 16384 | tf_op jit(solution)/shard_map/psum | solution.py:613
  583.6 3.1 broadcast_select_fusion.2
  586.8 3.1 broadcast_select_fusion.4
  589.9 1.5 broadcast_select_fusion.3
  591.5 3.0 constant_dynamic-update-slice_fusion.3
  605.4 1.9 slice_dynamic-update-slice_fusion.22
  607.3 1.9 slice_dynamic-update-slice_fusion.19
  609.2 1.9 slice_dynamic-update-slice_fusion.16
  611.1 1.9 slice_dynamic-update-slice_fusion.13
  612.9 1.9 slice_dynamic-update-slice_fusion.10
  614.8 1.9 slice_dynamic-update-slice_fusion.7
  616.7 1.9 slice_dynamic-update-slice_fusion.4
  618.6 1.9 slice_dynamic-update-slice_fusion.1
  620.5 1.6 collective-permute-start.17
  622.0 3.0 constant_dynamic-update-slice_fusion.2
  625.0 3.8 broadcast_select_fusion.1.b_ref
  628.9 3.6 unpack_512.3
  632.4 3.6 unpack_512.4
  636.0 3.6 unpack_512.5
  639.6 5.4 unpack_1024.2
  645.0 3.3 constant_dynamic-update-slice_fusion.5
  649.7 3.2 constant_dynamic-update-slice_fusion.4
  652.9 5.1 broadcast_select_fusion.b_ref
  658.0 7.8 %unpack_1408.2 = f32[1024,1408]{1,0:T(8,128)} custom-call(bf16[33792,128]{1,0:T(8,128)(2,1)} %broadcast_select_fusion.b_ref), custom_call_target="tpu_custom_call" | custom-call | tf_op jit(solution)/shard_map/unpack_1408/pallas_call | solution.py:295
  665.8 7.8 %unpack_1408.3 = f32[1024,1408]{1,0:T(8,128)} custom-call(bf16[33792,128]{1,0:T(8,128)(2,1)} %broadcast_select_fusion.b_ref), custom_call_target="tpu_custom_call" | custom-call | tf_op jit(solution)/shard_map/unpack_1408/pallas_call | solution.py:295
  673.5 3.0 slice.114.b_ref
  676.6 6.4 unpack_1024.3
  (115 shorter events, 24.6 us)
Async XLA Ops:
  7.2 503.8 %all-gather.5.cloned.1.call-start = ((), (), s32[]{:S(2)}) async-start(), calls=%async_computation | async-start | bytes 2359296 | tf_op jit(solution)/shard_map/all_gather | solution.py:622
  205.2 12.5 %collective-permute-start.2 = (bf16[2048,1024]{1,0:T(8,128)(2,1)}, bf16[2048,1024]{1,0:T(8,128)(2,1)}, u32[]{:S(2)}, u32[]{:S(2)}) collective-permute-start(bf16[2048,1024]{1,0:T(8,128)(2,1)} %get-tuple-element.51.ga_ref), channel_id=1, source_target_pairs={{0,2},{1,3},{2,0},{3,1},{4,6},{5,7},{6,4},{7,5},{8,10},{9,11},{10,... | collective-permute-start | bytes 12582920 | tf_op jit(solution)/shard_map/ppermute | solution.py:558
  210.7 118.1 %collective-permute-start.12 = (bf16[16896,128]{1,0:T(8,128)(2,1)}, bf16[16896,128]{1,0:T(8,128)(2,1)}, u32[]{:S(2)}, u32[]{:S(2)}) collective-permute-start(bf16[16896,128]{1,0:T(8,128)(2,1)} %constant_dynamic-slice_fusion.2), channel_id=1, source_target_pairs={{0,1},{1,0},{2,3},{3,2},{4,5},{5,4},{6,7},{7,6},{8,9},{9,8},{10,11... | collective-permute-start | bytes 12976136 | tf_op jit(solution)/shard_map/ppermute | solution.py:558
  304.3 21.5 %copy-start.5 = (bf16[4096,128]{1,0:T(8,128)(2,1)S(1)}, bf16[4096,128]{1,0:T(8,128)(2,1)}, u32[]{:S(2)}) copy-start(bf16[4096,128]{1,0:T(8,128)(2,1)} %get-tuple-element.69) | copy-start | bytes 3145732
  304.3 24.4 %slice-start.2 = ((s8[8650752]{0:T(1024)(128)(4,1)}), s8[262144]{0:T(1024)(128)(4,1)S(1)}, s32[]{:S(2)}) async-start(s8[8650752]{0:T(1024)(128)(4,1)} %bitcast.11), calls=%async_computation.4 | async-start | bytes 524288
  304.3 24.4 %slice-start.3 = ((s8[8650752]{0:T(1024)(128)(4,1)}), s8[4194304]{0:T(1024)(128)(4,1)S(1)}, s32[]{:S(2)}) async-start(s8[8650752]{0:T(1024)(128)(4,1)} %bitcast.11), calls=%async_computation.5 | async-start | bytes 8388608
  325.8 3.1 slice-start.4
  328.2 47.5 %collective-permute-start.6 = (bf16[8192,128]{1,0:T(8,128)(2,1)S(1)}, bf16[8192,128]{1,0:T(8,128)(2,1)S(1)}, u32[]{:S(2)}, u32[]{:S(2)}) collective-permute-start(bf16[8192,128]{1,0:T(8,128)(2,1)S(1)} %constant_dynamic-slice_fusion.6), channel_id=1, source_target_pairs={{0,1},{1,0},{2,3},{3,2},{4,5},{5,4},{6,7},{7,6},{8,9},{9,8},{10,11... | collective-permute-start | bytes 6291464 | tf_op jit(solution)/shard_map/ppermute | solution.py:558
  332.6 50.0 %collective-permute-start.13 = (bf16[8448,128]{1,0:T(8,128)(2,1)S(1)}, bf16[8448,128]{1,0:T(8,128)(2,1)S(1)}, u32[]{:S(2)}, u32[]{:S(2)}) collective-permute-start(bf16[8448,128]{1,0:T(8,128)(2,1)S(1)} %constant_dynamic-slice_fusion.1), channel_id=1, source_target_pairs={{0,4},{1,5},{2,6},{3,7},{4,0},{5,1},{6,2},{7,3},{8,12},{9,13},{10,... | collective-permute-start | bytes 6488072 | tf_op jit(solution)/shard_map/ppermute | solution.py:558
  376.4 27.7 %collective-permute-start.7 = (bf16[4096,128]{1,0:T(8,128)(2,1)S(1)}, bf16[4096,128]{1,0:T(8,128)(2,1)S(1)}, u32[]{:S(2)}, u32[]{:S(2)}) collective-permute-start(bf16[4096,128]{1,0:T(8,128)(2,1)S(1)} %constant_dynamic-slice_fusion.5), channel_id=1, source_target_pairs={{0,4},{1,5},{2,6},{3,7},{4,0},{5,1},{6,2},{7,3},{8,12},{9,13},{10,... | collective-permute-start | bytes 3145736 | tf_op jit(solution)/shard_map/ppermute | solution.py:558
  383.2 39.8 %copy-start.4 = (bf16[2048,1024]{1,0:T(8,128)(2,1)S(1)}, bf16[2048,1024]{1,0:T(8,128)(2,1)}, u32[]{:S(2)}) copy-start(bf16[2048,1024]{1,0:T(8,128)(2,1)} %get-tuple-element.50) | copy-start | bytes 12582916
  404.4 17.0 %collective-permute-start.8 = (bf16[2048,128]{1,0:T(8,128)(2,1)S(1)}, bf16[2048,128]{1,0:T(8,128)(2,1)S(1)}, u32[]{:S(2)}, u32[]{:S(2)}) collective-permute-start(bf16[2048,128]{1,0:T(8,128)(2,1)S(1)} %constant_dynamic-slice_fusion.4), channel_id=1, source_target_pairs={{0,8},{1,9},{2,10},{3,11},{4,12},{5,13},{6,14},{7,15},{8,0},{9,1},... | collective-permute-start | bytes 1572872 | tf_op jit(solution)/shard_map/ppermute | solution.py:558
  409.6 42.3 %collective-permute-start.14 = (bf16[4224,128]{1,0:T(8,128)(2,1)}, bf16[4224,128]{1,0:T(8,128)(2,1)}, u32[]{:S(2)}, u32[]{:S(2)}) collective-permute-start(bf16[4224,128]{1,0:T(8,128)(2,1)} %constant_dynamic-slice_fusion), channel_id=1, source_target_pairs={{0,8},{1,9},{2,10},{3,11},{4,12},{5,13},{6,14},{7,15},{8,0},{9,1},... | collective-permute-start | bytes 3244040 | tf_op jit(solution)/shard_map/ppermute | solution.py:558
  421.6 26.2 %collective-permute-start.9 = (bf16[1024,128]{1,0:T(8,128)(2,1)S(1)}, bf16[1024,128]{1,0:T(8,128)(2,1)S(1)}, u32[]{:S(2)}, u32[]{:S(2)}) collective-permute-start(bf16[1024,128]{1,0:T(8,128)(2,1)S(1)} %constant_dynamic-slice_fusion.3), channel_id=1, source_target_pairs={{0,16},{1,17},{2,18},{3,19},{4,20},{5,21},{6,22},{7,23},{8,24},{9,... | collective-permute-start | bytes 786440 | tf_op jit(solution)/shard_map/ppermute | solution.py:558
  424.5 65.8 %collective-permute-start = (bf16[1024,1024]{1,0:T(8,128)(2,1)}, bf16[1024,1024]{1,0:T(8,128)(2,1)}, u32[]{:S(2)}, u32[]{:S(2)}) collective-permute-start(bf16[1024,1024]{1,0:T(8,128)(2,1)} %constant_dynamic-slice_fusion.8), channel_id=1, source_target_pairs={{0,2},{1,3},{2,0},{3,1},{4,6},{5,7},{6,4},{7,5},{8,10},{9,11},{10,... | collective-permute-start | bytes 6291464 | tf_op jit(solution)/shard_map/ppermute | solution.py:558
  424.5 24.0 %copy-start = (bf16[2048,1024]{1,0:T(8,128)(2,1)S(1)}, bf16[2048,1024]{1,0:T(8,128)(2,1)}, u32[]{:S(2)}) copy-start(bf16[2048,1024]{1,0:T(8,128)(2,1)} %get-tuple-element.42.t_ref) | copy-start | bytes 12582916
  427.8 29.4 %copy-start.6 = (f32[1024]{0:T(1024)S(1)}, f32[1024]{0:T(1024)}, u32[]{:S(2)}) copy-start(f32[1024]{0:T(1024)} %param.17) | copy-start | bytes 12292
  427.8 29.4 %collective-permute-start.3 = (bf16[1024,1024]{1,0:T(8,128)(2,1)}, bf16[1024,1024]{1,0:T(8,128)(2,1)}, u32[]{:S(2)}, u32[]{:S(2)}) collective-permute-start(bf16[1024,1024]{1,0:T(8,128)(2,1)} %constant_dynamic-slice_fusion.7), channel_id=1, source_target_pairs={{0,2},{1,3},{2,0},{3,1},{4,6},{5,7},{6,4},{7,5},{8,10},{9,11},{10,... | collective-permute-start | bytes 6291464 | tf_op jit(solution)/shard_map/ppermute | solution.py:558
  447.9 3.3 collective-permute-start.10
  449.1 134.6 %collective-permute-start.5 = (bf16[2048,512]{1,0:T(8,128)(2,1)}, bf16[2048,512]{1,0:T(8,128)(2,1)}, u32[]{:S(2)}, u32[]{:S(2)}) collective-permute-start(bf16[2048,512]{1,0:T(8,128)(2,1)} %get-tuple-element.63.v_ref), channel_id=1, source_target_pairs={{1,2},{2,1},{5,6},{6,5},{9,10},{10,9},{13,14},{14,13},{17,18},{18,... | collective-permute-start | bytes 6291464 | tf_op jit(solution)/shard_map/ppermute | solution.py:558
  451.9 153.5 %all-gather.7.cloned.1.call-start = ((), (), s32[]{:S(2)}) async-start(), calls=%async_computation.1 | async-start | bytes 4866048 | tf_op jit(solution)/shard_map/all_gather | solution.py:622
  451.9 5.2 copy-start.1
  453.7 36.7 %copy-start.2 = (bf16[2048,1024]{1,0:T(8,128)(2,1)S(1)}, bf16[2048,1024]{1,0:T(8,128)(2,1)}, u32[]{:S(2)}) copy-start(bf16[2048,1024]{1,0:T(8,128)(2,1)} %get-tuple-element.43.pa_ref) | copy-start | bytes 12582916
  453.7 35.8 %collective-permute-start.15 = (bf16[2112,128]{1,0:T(8,128)(2,1)S(1)}, bf16[2112,128]{1,0:T(8,128)(2,1)S(1)}, u32[]{:S(2)}, u32[]{:S(2)}) collective-permute-start(bf16[2112,128]{1,0:T(8,128)(2,1)S(1)} %constant_dynamic-slice_fusion.9), channel_id=1, source_target_pairs={{0,16},{1,17},{2,18},{3,19},{4,20},{5,21},{6,22},{7,23},{8,24},{9,... | collective-permute-start | bytes 1622024 | tf_op jit(solution)/shard_map/ppermute | solution.py:558
  489.6 12.2 %collective-permute-start.16 = (bf16[2112,128]{1,0:T(8,128)(2,1)S(1)}, bf16[2112,128]{1,0:T(8,128)(2,1)S(1)}, u32[]{:S(2)}, u32[]{:S(2)}) collective-permute-start(bf16[2112,128]{1,0:T(8,128)(2,1)S(1)} %add_convert_fusion.5), channel_id=1, source_target_pairs={{1,2},{2,1},{5,6},{6,5},{9,10},{10,9},{13,14},{14,13},{17,18},{18,... | collective-permute-start | bytes 1622024 | tf_op jit(solution)/shard_map/ppermute | solution.py:558
  497.7 26.7 %copy-start.7 = (f32[8,1024]{1,0:T(8,128)S(1)}, f32[8,1024]{1,0:T(8,128)}, u32[]{:S(2)}) copy-start(f32[8,1024]{1,0:T(8,128)} %get-tuple-element.68) | copy-start | bytes 98308
  497.7 89.1 %collective-permute-start.1 = (bf16[1024,1024]{1,0:T(8,128)(2,1)}, bf16[1024,1024]{1,0:T(8,128)(2,1)}, u32[]{:S(2)}, u32[]{:S(2)}) collective-permute-start(bf16[1024,1024]{1,0:T(8,128)(2,1)} %get-tuple-element.77), channel_id=1, source_target_pairs={{1,2},{2,1},{5,6},{6,5},{9,10},{10,9},{13,14},{14,13},{17,18},{18,... | collective-permute-start | bytes 6291464 | tf_op jit(solution)/shard_map/ppermute | solution.py:558
  499.9 90.0 %collective-permute-start.4 = (bf16[1024,1024]{1,0:T(8,128)(2,1)S(1)}, bf16[1024,1024]{1,0:T(8,128)(2,1)}, u32[]{:S(2)}, u32[]{:S(2)}) collective-permute-start(bf16[1024,1024]{1,0:T(8,128)(2,1)S(1)} %get-tuple-element.76), channel_id=1, source_target_pairs={{1,2},{2,1},{5,6},{6,5},{9,10},{10,9},{13,14},{14,13},{17,18},{18,... | collective-permute-start | bytes 6291464 | tf_op jit(solution)/shard_map/ppermute | solution.py:558
  524.4 67.1 %collective-permute-start.11 = (bf16[8192,128]{1,0:T(8,128)(2,1)}, bf16[8192,128]{1,0:T(8,128)(2,1)}, u32[]{:S(2)}, u32[]{:S(2)}) collective-permute-start(bf16[8192,128]{1,0:T(8,128)(2,1)} %slice_dynamic-update-slice_fusion.25), channel_id=1, source_target_pairs={{0,2},{1,3},{2,0},{3,1},{4,6},{5,7},{6,4},{7,5},{8,10},{9,11},{10,... | collective-permute-start | bytes 6291464 | tf_op jit(solution)/shard_map/ppermute | solution.py:558
  589.9 4.6 copy-start.3
  620.5 24.6 %collective-permute-start.17 = (bf16[16896,128]{1,0:T(8,128)(2,1)}, bf16[16896,128]{1,0:T(8,128)(2,1)}, u32[]{:S(2)}, u32[]{:S(2)}) collective-permute-start(bf16[16896,128]{1,0:T(8,128)(2,1)} %slice_dynamic-update-slice_fusion.1), channel_id=1, source_target_pairs={{0,2},{1,3},{2,0},{3,1},{4,6},{5,7},{6,4},{7,5},{8,10},{9,11},{10,... | collective-permute-start | bytes 12976136 | tf_op jit(solution)/shard_map/ppermute | solution.py:558
  639.6 8.8 %slice-start = ((s8[4325376]{0:T(1024)(128)(4,1)}), s8[131072]{0:T(1024)(128)(4,1)S(1)}, s32[]{:S(2)}) async-start(s8[4325376]{0:T(1024)(128)(4,1)} %bitcast.9), calls=%async_computation.2 | async-start | bytes 262144
  645.0 3.5 slice-start.1
Sparse Core Ops, SparseCore 0:
  452.0 58.9 all-gather.4
  513.8 73.6 all-gather.6

commit v2 on v1

--- a/solution.py
+++ b/solution.py
@@ -11,114 +11,6 @@
 NN=(((1,),(0,)),((),()))
 def dot(a,b,dims=NN): return lax.dot_general(a,b,dims,preferred_element_type=jnp.float32)
 
-def fwd_kernel(BQ,BK,len_ref,q_ref,k_ref,v_ref,o_ref,lse_ref,kb_ref,s_ref):
-    length=len_ref[0]
-    lane=lax.broadcasted_iota(jnp.int32,(SLOT,128),1)
-    row=lax.broadcasted_iota(jnp.int32,(SLOT,128),0)
-    k=k_ref[...]; v=v_ref[...]
-    vs=[]
-    for h in range(2):
-        mine=(lane//64)==h
-        first=lane==(64*(1-h))
-        bias=jnp.where(first&(row>=length),-1e30,0.0).astype(jnp.bfloat16)
-        kb_ref[h]=jnp.where(mine,k,bias)
-        kb_ref[2+h]=jnp.where(mine,v,jnp.ones_like(v))
-    laneq=lax.broadcasted_iota(jnp.int32,(BQ,128),1)
-    for i in range(SLOT//BQ):
-        rows=slice(i*BQ,(i+1)*BQ)
-        q=q_ref[rows,:]
-        outs=[]
-        for h in range(2):
-            mine=(laneq//64)==h
-            qh=jnp.where(mine,q,jnp.ones_like(q))
-            ext=(i+1)*BQ
-            nb=(ext+BK-1)//BK
-            mx=None
-            for j in range(nb):
-                w=min(BK,ext-j*BK)
-                s=dot(qh,kb_ref[h,pl.ds(j*BK,w),:],NT)
-                if j*BK+w>i*BQ+1:
-                    r=lax.broadcasted_iota(jnp.int32,(BQ,w),0)+i*BQ
-                    c=lax.broadcasted_iota(jnp.int32,(BQ,w),1)+j*BK
-                    s=jnp.where(c<=r,s,-1e30)
-                s_ref[h,:,pl.ds(j*BK,w)]=s
-                m=jnp.max(s,axis=-1,keepdims=True)
-                mx=m if mx is None else jnp.maximum(mx,m)
-            mc=mx*C2
-            acc=None
-            for j in range(nb):
-                w=min(BK,ext-j*BK)
-                p=jnp.exp2(s_ref[h,:,pl.ds(j*BK,w)]*C2-mc).astype(jnp.bfloat16)
-                a=dot(p,kb_ref[2+h,pl.ds(j*BK,w),:])
-                acc=a if acc is None else acc+a
-            other=64*(1-h)
-            l=acc[:,other:other+1]
-            outs.append((acc/l,mc+jnp.log2(l)))
-        o_ref[rows,:]=jnp.where((laneq//64)==0,outs[0][0],outs[1][0]).astype(jnp.bfloat16)
-        lse_ref[0,:,pl.ds(i*BQ,BQ)]=jnp.where(lax.broadcasted_iota(jnp.int32,(BQ,128),1)==0,outs[0][1],outs[1][1]).T[0:8]
-def att_fwd(length,q,k,v,BQ=512,BK=512):
-    W=q.shape[1]; n=W//128
-    blk=pl.BlockSpec((SLOT,128),lambda p:(0,p))
-    return pl.pallas_call(functools.partial(fwd_kernel,BQ,BK),grid=(n,),
-        in_specs=[pl.BlockSpec(memory_space=pltpu.SMEM),blk,blk,blk],
-        out_specs=[blk,pl.BlockSpec((1,8,SLOT),lambda p:(p,0,0))],
-        out_shape=[jax.ShapeDtypeStruct((SLOT,W),jnp.bfloat16),jax.ShapeDtypeStruct((n,8,SLOT),jnp.float32)],
-        scratch_shapes=[pltpu.VMEM((4,SLOT,128),jnp.bfloat16),pltpu.VMEM((2,BQ,SLOT),jnp.float32)],
-        compiler_params=pltpu.CompilerParams(vmem_limit_bytes=56<<20),name="attfwd_%d_%d"%(BQ,BK))(length,q,k,v)
-
-def bwd_kernel(BQ,BK,len_ref,q_ref,k_ref,v_ref,do_ref,lse_ref,dl_ref,cos_ref,sin_ref,dq_ref,dk_ref,dv_ref,qs,ks,vs,dqa):
-    length=len_ref[0]
-    lane=lax.broadcasted_iota(jnp.int32,(SLOT,128),1)
-    row=lax.broadcasted_iota(jnp.int32,(SLOT,128),0)
-    k=k_ref[0]; q=q_ref[0]; do=do_ref[...]
-    for h in range(2):
-        mine=(lane//64)==h
-        first=lane==(64*(1-h))
-        bias=jnp.where(first&(row>=length),-1e30,0.0).astype(jnp.bfloat16)
-        ks[h]=jnp.where(mine,k,bias)
-        ks[2+h]=jnp.where(mine,k,jnp.zeros_like(k))
-        qs[h]=jnp.where(mine,q,jnp.ones_like(q))
-        qs[2+h]=jnp.where(mine,q,jnp.zeros_like(q))
-        vs[h]=jnp.where(mine,do,jnp.zeros_like(do))
-    dqa[...]=jnp.zeros_like(dqa)
-    nq=SLOT//BQ
-    for j in range(SLOT//BK):
-        cols=slice(j*BK,(j+1)*BK)
-        v=v_ref[0,cols,:]
-        dk=dv=None
-        for i in range((j*BK)//BQ,nq):
-            rows=slice(i*BQ,(i+1)*BQ)
-            for h in range(2):
-                st=dot(ks[h,cols,:],qs[h,rows,:],NT)
-                if (j+1)*BK>i*BQ+1:
-                    c=lax.broadcasted_iota(jnp.int32,(BK,BQ),0)+j*BK
-                    r=lax.broadcasted_iota(jnp.int32,(BK,BQ),1)+i*BQ
-                    st=jnp.where(c<=r,st,-1e30)
-                pt=jnp.exp2(st*C2-lse_ref[0,h:h+1,rows])
-                dpt=dot(v,vs[h,rows,:],NT)
-                dst=(pt*(dpt-dl_ref[0,h:h+1,rows])).astype(jnp.bfloat16)
-                a=dot(pt.astype(jnp.bfloat16),vs[h,rows,:])
-                dv=a if dv is None else dv+a
-                b=dot(dst,qs[2+h,rows,:])
-                dk=b if dk is None else dk+b
-                dqa[rows,:]+=dot(dst,ks[2+h,cols,:],TN)
-        lf=(lax.broadcasted_iota(jnp.int32,(BK,128),1)%64)<32
-        dk_ref[cols,:]=rot(dk*0.125,cos_ref[cols,:],-sin_ref[cols,:],lf).astype(dk_ref.dtype)
-        dv_ref[cols,:]=(dv*0.5).astype(dv_ref.dtype)
-    lf=(lax.broadcasted_iota(jnp.int32,(SLOT,128),1)%64)<32
-    dq_ref[...]=rot(dqa[...]*0.125,cos_ref[...],-sin_ref[...],lf).astype(dq_ref.dtype)
-def att_bwd(length,q,k,v,do,lse,delta,cos,sin,BQ=512,BK=512,odt=jnp.bfloat16):
-    tab=pl.BlockSpec((SLOT,128),lambda p:(0,0),pipeline_mode=pl.Buffered(1))
-    n=q.shape[0]; W=n*128
-    blk=pl.BlockSpec((SLOT,128),lambda p:(0,p)); tri=pl.BlockSpec((1,SLOT,128),lambda p:(p,0,0))
-    st=pl.BlockSpec((1,8,SLOT),lambda p:(p,0,0))
-    return pl.pallas_call(functools.partial(bwd_kernel,BQ,BK),grid=(n,),
-        in_specs=[pl.BlockSpec(memory_space=pltpu.SMEM),tri,tri,tri,blk,st,st,tab,tab],
-        out_specs=[blk,blk,blk],
-        out_shape=[jax.ShapeDtypeStruct((SLOT,W),odt)]*3,
-        scratch_shapes=[pltpu.VMEM((4,SLOT,128),jnp.bfloat16),pltpu.VMEM((4,SLOT,128),jnp.bfloat16),pltpu.VMEM((2,SLOT,128),jnp.bfloat16),pltpu.VMEM((SLOT,128),jnp.float32)],
-        compiler_params=pltpu.CompilerParams(vmem_limit_bytes=56<<20),name="attbwd_%d_%d"%(BQ,BK))(length,q,k,v,do,lse,delta,cos,sin)
-
 EPS=1e-5
 R2=256
 def norm_block(x,gain):
@@ -129,27 +21,6 @@
     up=pltpu.roll(x,96,1)
     dn=pltpu.roll(x,32,1)
     return x*cos+jnp.where(lane_first,up,dn)*sin
-
-def qkv_kernel(R,t_ref,f_ref,g_ref,cos_ref,sin_ref,wq,wk,wv,q_ref,k_ref,m_ref):
-    x=t_ref[...].astype(jnp.float32)
-    n,_=norm_block(x,None)
-    h=(n*g_ref[...]).astype(jnp.bfloat16)
-    cos=cos_ref[...]; sin=sin_ref[...]
-    lf=(lax.broadcasted_iota(jnp.int32,(R,128),1)%64)<32
-    for w,o in ((wq,q_ref),(wk,k_ref)):
-        y=dot(h,w[...])
-        for c in range(y.shape[1]//128):
-            o[:,c*128:(c+1)*128]=rot(y[:,c*128:(c+1)*128],cos,sin,lf).astype(jnp.bfloat16)
-    y=dot(h,wv[...])
-    m_ref[...]=(0.5*y+0.5*f_ref[...].astype(jnp.float32)).astype(jnp.bfloat16)
-def qkv_fwd(t,f,gain,cos,sin,wq,wk,wv,R=256):
-    N,D=t.shape; W=wq.shape[1]
-    rb=lambda w:pl.BlockSpec((R,w),lambda i:(i,0))
-    full=lambda a:pl.BlockSpec(a.shape,lambda i:(0,0),pipeline_mode=pl.Buffered(1))
-    return pl.pallas_call(functools.partial(qkv_kernel,R),grid=(N//R,),
-        in_specs=[rb(D),rb(W),full(gain),rb(128),rb(128),full(wq),full(wk),full(wv)],
-        out_specs=[rb(W)]*3,out_shape=[jax.ShapeDtypeStruct((N,W),jnp.bfloat16)]*3,
-        compiler_params=pltpu.CompilerParams(vmem_limit_bytes=56<<20),name="qkvfwd_%d"%R)(t,f,gain,cos,sin,wq,wk,wv)
 
 def mlp_kernel(R,NS,FH,len_ref,t_ref,pa_ref,pb_ref,og_ref,g_ref,wg_h,wu_h,wd_h,wg_f,wu_f,wd_f,
                op_ref,gh_ref,comb_h,
@@ -214,86 +85,6 @@
         scratch_shapes=[pltpu.VMEM((D,2*FH),jnp.bfloat16),pltpu.VMEM((FH,D),jnp.bfloat16),pltpu.VMEM((D,2*FH),jnp.float32),pltpu.VMEM((FH,D),jnp.float32),
             pltpu.VMEM((4,max(D,FH),128),jnp.bfloat16),pltpu.SemaphoreType.DMA((3,)),pltpu.SemaphoreType.DMA((4,))],
         compiler_params=pltpu.CompilerParams(vmem_limit_bytes=60<<20),name="mlp_%d"%R)(length,t,pa,pb,og,gain,wg,wu,wd,wg_f,wu_f,wd_f)
-
-def mid_kernel(R,NS,len_ref,t_ref,pa_ref,pb_ref,og_ref,ga_ref,gb_ref,at_ref,g_ref,wo,
-               gm_ref,gat_ref,dl_ref,gwo_ref,gg_ref,acc):
-    step=pl.program_id(0)
-    x=t_ref[...].astype(jnp.float32)+(pa_ref[...].astype(jnp.float32)+pb_ref[...].astype(jnp.float32))
-    n,r=norm_block(x,None)
-    gh2=ga_ref[...].astype(jnp.float32)+gb_ref[...].astype(jnp.float32)
-    row=lax.broadcasted_iota(jnp.int32,(R,1),0)+step*R
-    mg=jnp.where(row<len_ref[0],og_ref[...].astype(jnp.float32),0.0)
-    gn=gh2*g_ref[...]
-    inner=jnp.mean(gn*n,axis=-1,keepdims=True)
-    gm=(mg+r*(gn-n*inner)).astype(jnp.bfloat16)
-    gm_ref[...]=gm
-    part=jnp.sum((gh2*n).reshape(R//8,8,-1),axis=0)
-    at=at_ref[...]
-    ga=dot(gm,wo[...],NT).astype(jnp.bfloat16)
-    gat_ref[...]=ga
-    xx=ga.astype(jnp.float32)*at.astype(jnp.float32)
-    hi=xx.astype(jnp.bfloat16); lo=(xx-hi.astype(jnp.float32)).astype(jnp.bfloat16)
-    W=at.shape[1]
-    hr=lax.broadcasted_iota(jnp.int32,(8*(W//128),W),0); ln=lax.broadcasted_iota(jnp.int32,(8*(W//128),W),1)
-    ind=((ln//64)==((hr//8)*2+hr%8)) & (hr%8<2)
-    ind=jnp.where(ind,1.0,0.0).astype(jnp.bfloat16)
-    d=dot(ind,hi,NT)+dot(ind,lo,NT)
-    dl_ref[...]=d.reshape(W//128,8,R)
-    w=dot(at,gm,TN)
-    @pl.when(step==0)
-    def _():
-        acc[...]=w; gg_ref[...]=part
-    @pl.when(step>0)
-    def _():
-        acc[...]+=w; gg_ref[...]+=part
-    @pl.when(step==NS-1)
-    def _():
-        for c in range(acc.shape[1]//128):
-            gwo_ref[c*W:(c+1)*W,:]=acc[:,c*128:(c+1)*128].astype(jnp.bfloat16)
-def mid(length,t,pa,pb,og,ga,gb,at,gain,wo,R=256):
-    N,D=t.shape; W=at.shape[1]; NS=N//R
-    rb=lambda w:pl.BlockSpec((R,w),lambda i:(i,0))
-    full=lambda a:pl.BlockSpec(a.shape,lambda i:(0,0),pipeline_mode=pl.Buffered(1))
-    return pl.pallas_call(functools.partial(mid_kernel,R,NS),grid=(NS,),
-        in_specs=[pl.BlockSpec(memory_space=pltpu.SMEM)]+[rb(D)]*6+[rb(W),full(gain),full(wo)],
-        out_specs=[rb(D),rb(W),pl.BlockSpec((W//128,8,R),lambda i:(0,0,i)),pl.BlockSpec((W*D//128,128),lambda i:(0,0)),pl.BlockSpec((8,D),lambda i:(0,0))],
-        out_shape=[jax.ShapeDtypeStruct((N,D),jnp.bfloat16),jax.ShapeDtypeStruct((N,W),jnp.bfloat16),jax.ShapeDtypeStruct((W//128,8,N),jnp.float32),
-            jax.ShapeDtypeStruct((W*D//128,128),jnp.bfloat16),jax.ShapeDtypeStruct((8,D),jnp.float32)],
-        scratch_shapes=[pltpu.VMEM((W,D),jnp.float32)],
-        compiler_params=pltpu.CompilerParams(vmem_limit_bytes=56<<20),name="mid_%d"%R)(length,t,pa,pb,og,ga,gb,at,gain,wo)
-
-def qkvb_kernel(R,NS,t_ref,q_ref,k_ref,v_ref,g_ref,wq,wk,wv,gh_ref,gw_ref,acc):
-    step=pl.program_id(0)
-    x=t_ref[...].astype(jnp.float32)
-    n,_=norm_block(x,None)
-    h=(n*g_ref[...]).astype(jnp.bfloat16)
-    gq=q_ref[...]; gk=k_ref[...]; gv=v_ref[...]
-    gh_ref[...]=(dot(gq,wq[...],NT)+dot(gk,wk[...],NT)+dot(gv,wv[...],NT)).astype(jnp.bfloat16)
-    W=gq.shape[1]; D=x.shape[1]
-    @pl.when(step==0)
-    def _(): acc[...]=jnp.zeros_like(acc)
-    for i,g in enumerate((gq,gk,gv)):
-        acc[:,i*W:(i+1)*W]+=dot(h,g,TN)
-    @pl.when(step==NS-1)
-    def _():
-        for c in range(3*W//128):
-            gw_ref[c*D:(c+1)*D,:]=acc[:,c*128:(c+1)*128].astype(jnp.bfloat16)
-def qkv_bwd(t,gq,gk,gv,gain,wq,wk,wv,R=256):
-    N,D=t.shape; W=wq.shape[1]; NS=N//R
-    rb=lambda w:pl.BlockSpec((R,w),lambda i:(i,0))
-    full=lambda a:pl.BlockSpec(a.shape,lambda i:(0,0),pipeline_mode=pl.Buffered(1))
-    return pl.pallas_call(functools.partial(qkvb_kernel,R,NS),grid=(NS,),
-        in_specs=[rb(D),rb(W),rb(W),rb(W),full(gain),full(wq),full(wk),full(wv)],
-        out_specs=[rb(D),pl.BlockSpec((3*W*D//128,128),lambda i:(0,0))],
-        out_shape=[jax.ShapeDtypeStruct((N,D),jnp.bfloat16),jax.ShapeDtypeStruct((3*W*D//128,128),jnp.bfloat16)],
-        scratch_shapes=[pltpu.VMEM((D,3*W),jnp.float32)],
-        compiler_params=pltpu.CompilerParams(vmem_limit_bytes=56<<20),name="qkvb_%d"%R)(t,gq,gk,gv,gain,wq,wk,wv)
-
-def unpack_kernel(b_ref,o_ref): o_ref[...]=b_ref[...].astype(jnp.float32)
-def unpack(buf,off,D,W):
-    o=off//D
-    return pl.pallas_call(unpack_kernel,grid=(W//128,),in_specs=[pl.BlockSpec((D,128),lambda c:(o+c,0))],
-       out_specs=pl.BlockSpec((D,128),lambda c:(0,c)),out_shape=jax.ShapeDtypeStruct((D,W),jnp.float32),name="unpack_%d"%W)(buf)
 
 
 ALL=("zy","core","head")
@@ -555,30 +346,454 @@
     return pl.pallas_call(functools.partial(front_kernel,groups),out_shape=outs,
         in_specs=[anyb]*4+[vm]*5+[anyb]*7,out_specs=[anyb]*len(outs),scratch_shapes=scratch,
         compiler_params=pltpu.CompilerParams(collective_id=0,has_side_effects=True,vmem_limit_bytes=58<<20),name="front")(tok,fv,og,length,gain,*tables,*ws)
-def exchange(v,perm): return lax.ppermute(v,ALL,perm)
-def halve(buf,perm,bit):
-    half=buf.shape[0]//2
-    keep=lax.dynamic_slice_in_dim(buf,bit*half,half,0)
-    send=lax.dynamic_slice_in_dim(buf,(1-bit)*half,half,0)
-    got=exchange(send,perm)
-    return (keep.astype(jnp.float32)+got.astype(jnp.float32)).astype(jnp.bfloat16)
+
+class Reduce:
+    def __init__(self,links,order,src,offset,rows,recv,recv_at,result,result_at,at,landing=None,held=None):
+        self.links=links; self.order=order; self.rows=rows; self.src=src; self.offset=offset; self.at=at
+        self.levels=len(order); self.bufs=[]; self.sends=[]
+        for level in range(self.levels):
+            size=rows>>(level+1)
+            if level==0 and held is not None: self.bufs.append(held)
+            else: self.bufs.append(recv.at[pl.ds(recv_at,size)]); recv_at+=size
+        self.landing=landing; self.sent1=False
+        self.recv_end=recv_at
+        half=rows//2
+        for level,name in enumerate(order):
+            size=rows>>(level+1)
+            bit=at.bit(name)
+            if level==0:
+                source=src.at[pl.ds(pl.multiple_of(offset+(1-bit)*half,16),half)]
+            else:
+                source=self.bufs[level-1].at[pl.ds(pl.multiple_of((1-bit)*size,16),size)]
+            self.sends.append(links.remote(source,landing if level==0 and landing is not None else self.bufs[level],at.partner(name)))
+        self.result=result; self.result_at=result_at
+        leaf=rows>>self.levels; self.leaf=leaf
+        weight={name:rows>>(i+1) for i,name in enumerate(order)}
+        own=sum(at.bit(name)*weight[name] for name in order)
+        spot=result.at[pl.ds(pl.multiple_of(result_at+own,16),leaf)]
+        self.swap=links.remote(self.bufs[-1],spot,at.swap)
+        self.keep=links.copy(self.bufs[-1],spot)
+        self.gathers=[]; gathered=[]
+        for name in sorted([n for n in order if n!="x"],reverse=True)+["x"]:
+            unit=leaf; apart=[]
+            for w in sorted(gathered):
+                if w==unit: unit*=2
+                else: apart.append(w)
+            base=sum((at.core if n=="x" else at.bit(n))*weight[n] for n in order if weight[n] not in gathered)
+            combos=[0]
+            for w in apart: combos=combos+[c+w for c in combos]
+            device=at.core_dev if name=="x" else at.partner(name)
+            step=[]
+            for c in combos:
+                block=result.at[pl.ds(pl.multiple_of(result_at+base+c,16),unit)]
+                step.append(links.remote(block,block,device))
+            self.gathers.append(step); gathered.append(weight[name])
+    def start(self): self.sends[0].start()
+    def finish(self,level,got=None):
+        if got is None: self.sends[level].wait_recv()
+        size=self.rows>>(level+1)
+        bit=self.at.bit(self.order[level])
+        into=self.bufs[level]
+        if level==0:
+            mine=got if got is not None else self.src.at[pl.ds(pl.multiple_of(self.offset+bit*size,16),size)]
+        else:
+            mine=self.bufs[level-1].at[pl.ds(pl.multiple_of(bit*size,16),size)]
+        step=math.gcd(size,512)
+        def add(i,_):
+            rows=pl.ds(pl.multiple_of(i*step,step),step)
+            into[rows,:]=(into[rows,:].astype(jnp.float32)+mine[rows,:].astype(jnp.float32)).astype(jnp.bfloat16)
+            return 0
+        lax.fori_loop(0,size//step,add,0)
+        if level+1<self.levels: self.sends[level+1].start()
+        else:
+            @pl.when(self.at.off)
+            def _(): self.swap.start()
+            @pl.when(self.at.diag)
+            def _(): self.keep.start()
+    def gather(self,step):
+        if step==0:
+            @pl.when(self.at.off)
+            def _(): self.swap.wait_recv()
+            @pl.when(self.at.diag)
+            def _(): self.keep.wait()
+        else:
+            for c in self.gathers[step-1]: c.wait_recv()
+        for c in self.gathers[step]: c.start()
+    def drain(self):
+        for c in self.gathers[-1]: c.wait_recv()
+        for i,c in enumerate(self.sends):
+            if not (i==1 and self.sent1): c.wait_send()
+        @pl.when(self.at.off)
+        def _(): self.swap.wait_send()
+        for s in self.gathers:
+            for c in s: c.wait_send()
+
+class Place: pass
+def place_of(groups):
+    at=Place()
+    at.zy=lax.axis_index("zy"); at.core=lax.axis_index("core"); at.x=lax.axis_index("head")
+    at.off=at.core!=at.x; at.diag=at.core==at.x
+    at.bit=lambda name: at.x if name=="x" else (at.zy//name)%2
+    at.partner=lambda name: (at.zy,at.core,1-at.x) if name=="x" else (at.zy+name-2*name*((at.zy//name)%2),at.core,at.x)
+    at.swap=(at.zy,1-at.core,1-at.x); at.core_dev=(at.zy,1-at.core,at.x)
+    at.bits=[]
+    b=1
+    while b<groups: at.bits.append(b); b*=2
+    return at
+
+def back_kernel(groups,
+        len_ref,tok_h,pa_h,pb_h,og_h,op_h,gh_h,att_h,comb_h,q_h,k_h,m_h,wq_h,wk_h,wv_h,wo_h,lse_ref,g1_ref,g2_ref,ch_ref,sh_ref,cl_ref,sl_ref,
+        out_o,gt_o,gf_o,res_o,gains_o,land_o,
+        tokb,pab,pbb,ogb,gab,atb,opb,oprv,ghb,h1_v,gm_v,gat_v,dl_v,qd,kd,md,ks,qs,vs,dqa,cos_v,sin_v,wo_v,acc,keep_v,got_v,recv_v,gwo_v,gw_v,gain_v,
+        send_sem,recv_sem,local_sem,blk_sem,free_sem):
+    at=place_of(groups); core=at.core; off=at.off; diag=at.diag
+    L=Links(send_sem,recv_sem,local_sem)
+    MESH=pl.DeviceIdType.MESH
+    N,D=tok_h.shape; half=N//2; W=wo_h.shape[0]; NP=W//128; R=256; NB=N//R
+    bits=at.bits
+    order1=["x"]+bits; order2=bits[:1]+["x"]+bits[1:]; order3=bits[1:2]+bits[:1]+["x"]+bits[2:]
+    total=comb_h.shape[0]; KB=1024; units=total//KB
+    cut=[units//4,units//4,units//4,units-3*(units//4)]
+    runs={}; pos=0; rp=0
+    keep_slot={"A":0,"B":1,"E":0,"F":1}; follows={"E":"A","F":"B"}
+    for name,c,order in (("A",cut[0],order1),("B",cut[3],order2),("E",cut[1],order1),("F",cut[2],order2)):
+        runs[name]=Reduce(L,order,comb_h,pos,c*KB,recv_v,rp,res_o,pos,at,land_o.at[pl.ds(pos//2,c*KB//2)],keep_v.at[keep_slot[name],pl.ds(0,c*KB//2)]); rp=runs[name].recv_end; pos+=c*KB
+    runs["C"]=Reduce(L,order3,gwo_v,0,gwo_v.shape[0],recv_v,rp,res_o,pos,at); rp=runs["C"].recv_end; pos+=gwo_v.shape[0]
+    for p in range(NP):
+        runs[p]=Reduce(L,order3,gw_v.at[p],0,gw_v.shape[1],recv_v,rp,res_o,pos,at); rp=runs[p].recv_end; pos+=gw_v.shape[1]
+    def both_copies(name):
+        r=runs[name]; h=r.rows//2
+        mine=comb_h.at[pl.ds(pl.multiple_of(r.offset+at.bit(r.order[0])*h,16),h)]
+        return (pltpu.make_async_copy(mine,r.bufs[0],blk_sem.at[16]),pltpu.make_async_copy(r.landing,got_v.at[pl.ds(0,h)],blk_sem.at[17]))
+    def prep(name):
+        if name in follows: runs[follows[name]].sends[1].wait_send(); runs[follows[name]].sent1=True
+        runs[name].sends[0].wait_recv()
+        for c in both_copies(name): c.start()
+    def finish0(name):
+        for c in both_copies(name): c.wait()
+        runs[name].finish(0,got_v)
+    first_rows=lambda b:pl.multiple_of(((core*(NB//2)+b)%NB)*R,R)
+    blk=lambda b:pl.ds(first_rows(b),R)
+    theirs=lambda b:pl.ds(pl.multiple_of((((1-core)*(NB//2)+b)%NB)*R,R),R)
+    ex_gh=[L.remote(gh_h.at[theirs(b)],ghb.at[theirs(b)],at.core_dev) for b in range(NB)]
+    ex_op=[L.remote(op_h.at[theirs(b)],oprv.at[pl.ds(b*R,R)],at.core_dev) for b in range(NB//2)]
+    sw_out=[L.remote(opb.at[pl.ds(b*R,R)],out_o.at[pl.ds(b*R,R)],at.swap) for b in range(NB//2)]
+    lo_out=[L.copy(opb.at[pl.ds(b*R,R)],out_o.at[pl.ds(b*R,R)]) for b in range(NB//2)]
+    sw_gf=[L.remote(md.at[p],gf_o.at[:,pl.ds(p*128,128)],at.swap) for p in range(NP)]
+    lo_gf=[L.copy(md.at[p],gf_o.at[:,pl.ds(p*128,128)]) for p in range(NP)]
+    ex_g1=[L.remote(ghb.at[theirs(b)],oprv.at[pl.ds(b*R,R)],at.core_dev) for b in range(NB//2)]
+    sw_gt=[L.remote(gm_v.at[pl.ds(b*R,R)],gt_o.at[pl.ds(b*R,R)],at.swap) for b in range(NB//2)]
+    lo_gt=[L.copy(gm_v.at[pl.ds(b*R,R)],gt_o.at[pl.ds(b*R,R)]) for b in range(NB//2)]
+    names=["c","x"]+bits
+    ex_gain=[L.remote(gain_v.at[0] if i==0 else gain_v.at[2*i],gain_v.at[2*i+1],at.core_dev if n=="c" else at.partner(n)) for i,n in enumerate(names)]
+    loads=[L.copy(a,b) for a,b in ((wo_h,wo_v),(q_h,qd),(k_h,kd),(m_h,md))]
+    proj=[L.copy(w.at[pl.ds(i*256,256)],v.at[i//2,:,pl.ds((i%2)*W,W)]) for w,v in ((wq_h,pab),(wk_h,pbb),(wv_h,ogb)) for i in range(D//256)]
+    barrier=pltpu.get_barrier_semaphore()
+    for d in [at.core_dev]+[at.partner(n) for n in ["x"]+bits]:
+        pl.semaphore_signal(barrier,inc=1,device_id=d,device_id_type=MESH)
+    @pl.when(off)
+    def _():
+        pl.semaphore_signal(barrier,inc=1,device_id=at.swap,device_id_type=MESH)
+        pl.semaphore_wait(barrier,3+len(bits))
+    @pl.when(diag)
+    def _(): pl.semaphore_wait(barrier,2+len(bits))
+    for c in ex_gh[:2]: c.start()
+    ex_op[0].start()
+    for b in range(2,NB): ex_gh[b].start()
+    for c in ex_op[1:]: c.start()
+    runs["A"].start(); runs["B"].start()
+    def block_loads(b):
+        s=b%2
+        pairs=[(tok_h,tokb),(pa_h,pab),(pb_h,pbb),(og_h,ogb),(gh_h,gab),(att_h,atb)]
+        cps=[pltpu.make_async_copy(h.at[blk(b)],v.at[s],blk_sem.at[s*8+i]) for i,(h,v) in enumerate(pairs)]
+        if b<NB//2: cps.append(pltpu.make_async_copy(op_h.at[blk(b)],opb.at[pl.ds(b*R,R)],blk_sem.at[s*8+6]))
+        return cps
+    for c in block_loads(0): c.start()
+    for c in loads: c.start()
+    sign=jnp.where((lax.broadcasted_iota(jnp.int32,(1,128),1)%64)<32,-1.0,1.0)
+    cl=cl_ref[...]; sl=sl_ref[...]
+    def table(a,_):
+        rows=pl.ds(pl.multiple_of(a*32,32),32)
+        ch=ch_ref[pl.ds(a,1),:]; sh=sh_ref[pl.ds(a,1),:]
+        cos_v[rows,:]=ch*cl-sh*sl
+        sin_v[rows,:]=(sh*cl+ch*sl)*sign
+        return 0
+    lax.fori_loop(0,N//32,table,0)
+    g1=g1_ref[...]; g2=g2_ref[...]
+    length=len_ref[0:1,0:1]
+    hr=lax.broadcasted_iota(jnp.int32,(8*NP,W),0); ln=lax.broadcasted_iota(jnp.int32,(8*NP,W),1)
+    ind=jnp.where(((ln//64)==((hr//8)*2+hr%8))&(hr%8<2),1.0,0.0).astype(jnp.bfloat16)
+    loads[0].wait()
+    gsum=None
+    plan={}
+    todo=lambda t,*acts: plan.setdefault(t,[]).extend(acts)
+    for k,v in make_schedule(1+len(bits),NP).items():
+        for name,what,*arg in v:
+            if what=="start": todo(k,runs[name].start)
+            elif what=="prep": todo(k,functools.partial(prep,name))
+            elif what=="f": todo(k,functools.partial(finish0,name) if (arg[0]==0 and name in keep_slot) else functools.partial(runs[name].finish,arg[0]))
+            elif what=="g": todo(k,functools.partial(runs[name].gather,arg[0]))
+    for b in range(NB):
+        for a in plan.get(("m",b),[]): a()
+        if b+1<NB:
+            for c in block_loads(b+1): c.start()
+        for c in block_loads(b): c.wait()
+        ex_gh[b].wait_recv()
+        s=b%2; r0=first_rows(b)
+        t=tokb[s].astype(jnp.float32)
+        n1,_=norm_block(t,None)
+        h1_v[blk(b),:]=(n1*g1).astype(jnp.bfloat16)
+        mid=t+(pab[s].astype(jnp.float32)+pbb[s].astype(jnp.float32))
+        n,r=norm_block(mid,None)
+        gh2=gab[s].astype(jnp.float32)+ghb[blk(b),:].astype(jnp.float32)
+        row=lax.broadcasted_iota(jnp.int32,(R,1),0)+r0
+        mg=jnp.where(row<length,ogb[s].astype(jnp.float32),0.0)
+        gn=gh2*g2
+        inner=jnp.mean(gn*n,axis=-1,keepdims=True)
+        gm=(mg+r*(gn-n*inner)).astype(jnp.bfloat16)
+        part=jnp.sum((gh2*n).reshape(R//8,8,D),axis=0)
+        gsum=part if gsum is None else gsum+part
+        if b<NB//2:
+            gm_v[b*R:(b+1)*R,:]=gm
+            ex_op[b].wait_recv()
+            mine=slice(b*R,(b+1)*R)
+            opb[mine,:]=(mid+(opb[mine,:].astype(jnp.float32)+oprv[mine,:].astype(jnp.float32))).astype(jnp.bfloat16)
+        at_b=atb[s]
+        ga=dot(gm,wo_v[...],NT).astype(jnp.bfloat16)
+        for p in range(NP): gat_v[p,blk(b),:]=ga[:,p*128:(p+1)*128]
+        xx=ga.astype(jnp.float32)*at_b.astype(jnp.float32)
+        hi=xx.astype(jnp.bfloat16); lo=(xx-hi.astype(jnp.float32)).astype(jnp.bfloat16)
+        dl_v[:,:,blk(b)]=(dot(ind,hi,NT)+dot(ind,lo,NT)).reshape(NP,8,R)
+        w=dot(at_b,gm,TN)
+        if b==0: acc[...]=w
+        else: acc[...]+=w
+    for c in range(D//128): gwo_v[c*W:(c+1)*W,:]=acc[:,c*128:(c+1)*128].astype(jnp.bfloat16)
+    gain_v[0,8:16,:]=gsum*0.5
+    runs["C"].start()
+    pl.semaphore_signal(free_sem,inc=1,device_id=at.core_dev,device_id_type=MESH)
+    for c in proj: c.start()
+    for c in loads[1:]: c.wait()
+    BQ=BK=512
+    lane=lax.broadcasted_iota(jnp.int32,(N,128),1)
+    rowi=lax.broadcasted_iota(jnp.int32,(N,128),0)
+    lf=(lax.broadcasted_iota(jnp.int32,(BK,128),1)%64)<32
+    def pair(p,_):
+        k=kd[p]; q=qd[p]; do=gat_v[p]
+        for h in range(2):
+            own=(lane//64)==h
+            first=lane==(64*(1-h))
+            bias=jnp.where(first&(rowi>=length),-1e30,0.0).astype(jnp.bfloat16)
+            ks[h]=jnp.where(own,k,bias)
+            ks[2+h]=jnp.where(own,k,jnp.zeros_like(k))
+            qs[h]=jnp.where(own,q,jnp.ones_like(q))
+            qs[2+h]=jnp.where(own,q,jnp.zeros_like(q))
+            vs[h]=jnp.where(own,do,jnp.zeros_like(do))
+        dqa[...]=jnp.zeros_like(dqa)
+        hook=0
+        for j in range(N//BK):
+            cols=slice(j*BK,(j+1)*BK)
+            v=md[p,cols,:]
+            dk=dv=None
+            for i in range(j,N//BQ):
+                for P_ in range(NP):
+                    acts=plan.get((P_,hook))
+                    if acts:
+                        @pl.when(p==P_)
+                        def _():
+                            for a in acts: a()
+                hook+=1
+                rows=slice(i*BQ,(i+1)*BQ)
+                for h in range(2):
+                    st=dot(ks[h,cols,:],qs[h,rows,:],NT)
+                    if i==j:
+                        c=lax.broadcasted_iota(jnp.int32,(BK,BQ),0); r=lax.broadcasted_iota(jnp.int32,(BK,BQ),1)
+                        st=jnp.where(c<=r,st,-1e30)
+                    pt=jnp.exp2(st*C2-lse_ref[p,h:h+1,rows])
+                    dpt=dot(v,vs[h,rows,:],NT)
+                    dst=(pt*(dpt-dl_v[p,h:h+1,rows])).astype(jnp.bfloat16)
+                    a=dot(pt.astype(jnp.bfloat16),vs[h,rows,:])
+                    dv=a if dv is None else dv+a
+                    b_=dot(dst,qs[2+h,rows,:])
+                    dk=b_ if dk is None else dk+b_
+                    dqa[rows,:]+=dot(dst,ks[2+h,cols,:],TN)
+            kd[p,cols,:]=rot(dk*0.125,cos_v[cols,:],-sin_v[cols,:],lf).astype(jnp.bfloat16)
+            md[p,cols,:]=(dv*0.5).astype(jnp.bfloat16)
+        for j in range(N//BK):
+            cols=slice(j*BK,(j+1)*BK)
+            qd[p,cols,:]=rot(dqa[cols,:]*0.125,cos_v[cols,:],-sin_v[cols,:],lf).astype(jnp.bfloat16)
+        joint=jnp.concatenate([qd[p],kd[p],md[p]],axis=1)
+        g=dot(h1_v[...],joint,TN)
+        for c in range(3): gw_v[p,c*D:(c+1)*D,:]=g[:,c*128:(c+1)*128].astype(jnp.bfloat16)
+        for P_ in range(NP):
+            @pl.when(p==P_)
+            def _():
+                runs[P_].start()
+                @pl.when(off)
+                def _(): sw_gf[P_].start()
+                @pl.when(diag)
+                def _(): lo_gf[P_].start()
+                if P_==0:
+                    @pl.when(off)
+                    def _():
+                        for c in sw_out: c.start()
+                    @pl.when(diag)
+                    def _():
+                        for c in lo_out: c.start()
+        return 0
+    lax.fori_loop(0,NP,pair,0)
+    for c in proj: c.wait()
+    pl.semaphore_wait(free_sem,1)
+    def tok_load(b): return pltpu.make_async_copy(tok_h.at[blk(b)],tokb.at[b%2],blk_sem.at[b%2])
+    tok_load(0).start(); tok_load(1).start()
+    def input_grad(b,rows):
+        gs=[jnp.concatenate([d[p,rows,:] for p in range(NP)],axis=1) for d in (qd,kd,md)]
+        out=[]
+        for i in range(D//256):
+            ws=[v[i//2,:,(i%2)*W:(i%2+1)*W] for v in (pab,pbb,ogb)]
+            out.append(dot(gs[0],ws[0],NT)+dot(gs[1],ws[1],NT)+dot(gs[2],ws[2],NT))
+        return jnp.concatenate(out,axis=1)
+    for b in range(NB//2):
+        ghb[theirs(b),:]=input_grad(b,theirs(b)).astype(jnp.bfloat16)
+        ex_g1[b].start()
+        for a in plan.get(("t",b),[]): a()
+    gsum=None
+    for b in range(NB//2):
+        mine=input_grad(b,blk(b)).astype(jnp.bfloat16).astype(jnp.float32)
+        for a in plan.get(("u",b),[]): a()
+        ex_g1[b].wait_recv()
+        gh=mine+oprv[b*R:(b+1)*R,:].astype(jnp.float32)
+        tok_load(b).wait()
+        t=tokb[b%2].astype(jnp.float32)
+        n,r=norm_block(t,None)
+        gn=gh*g1
+        part=jnp.sum((gh*n).reshape(R//8,8,D),axis=0)
+        gsum=part if gsum is None else gsum+part
+        gm_v[b*R:(b+1)*R,:]=(gm_v[b*R:(b+1)*R,:].astype(jnp.float32)+r*(gn-n*jnp.mean(gn*n,axis=-1,keepdims=True))).astype(jnp.bfloat16)
+        if b+2<NB//2: tok_load(b+2).start()
+        @pl.when(off)
+        def _(): sw_gt[b].start()
+        @pl.when(diag)
+        def _(): lo_gt[b].start()
+    gain_v[0,0:8,:]=gsum
+    ex_gain[0].start()
+    last=plan.get("end",[])
+    gain_steps=len(names)
+    def gain_step(i):
+        ex_gain[i].wait_recv()
+        prev=gain_v[0] if i==0 else gain_v[2*i]
+        gain_v[2*i+2]=prev+gain_v[2*i+1]
+        if i+1<gain_steps: ex_gain[i+1].start()
+    gi=0
+    for i,a in enumerate(last):
+        a()
+        if i%3==2 and gi<gain_steps: gain_step(gi); gi+=1
+    while gi<gain_steps: gain_step(gi); gi+=1
+    gout=pltpu.make_async_copy(gain_v.at[2*gain_steps],gains_o,blk_sem.at[0])
+    gout.start()
+    for r in runs.values(): r.drain()
+    gout.wait()
+    for c in ex_gh+ex_op+ex_g1+ex_gain: c.wait_send()
+    @pl.when(off)
+    def _():
+        for c in sw_out+sw_gf+sw_gt: c.wait()
+    @pl.when(diag)
+    def _():
+        for c in lo_out+lo_gf+lo_gt: c.wait()
+
+def back(groups,length8,tok,pa,pb,og,op,gh,att,comb,q,k,m,wq,wk,wv,wo,lse,g1,g2,tables):
+    bf=jnp.bfloat16; f32=jnp.float32; S=jax.ShapeDtypeStruct; V=pltpu.VMEM
+    N,D=tok.shape; half=N//2; W=wo.shape[0]; NP=W//128; R=256
+    KB=1024; units=comb.shape[0]//KB
+    rows=comb.shape[0]+W*D//128+3*W*D//128
+    levels=1+int(math.log2(groups))
+    per=lambda n:sum(n>>(l+1) for l in range(levels))
+    cut=[units//4]*3+[units-3*(units//4)]
+    recv=sum(per(c*KB)-c*KB//2 for c in cut)+per(W*D//128)+NP*per(3*D)
+    anyb=pl.BlockSpec(memory_space=pl.ANY); vm=pl.BlockSpec(memory_space=pltpu.VMEM)
+    outs=[S((half,D),bf),S((half,D),bf),S((N,W),bf),S((rows,128),bf),S((16,D),f32),S((comb.shape[0]//2,128),bf)]
+    gains=2*(2+levels-1)+1
+    scratch=[V((2,R,D),bf)]*5+[V((2,R,W),bf),V((half,D),bf),V((half,D),bf),V((N,D),bf),V((N,D),bf),V((half,D),bf),V((NP,N,128),bf),V((NP,8,N),f32),
+        V((NP,N,128),bf),V((NP,N,128),bf),V((NP,N,128),bf),V((4,N,128),bf),V((4,N,128),bf),V((2,N,128),bf),V((N,128),f32),V((N,128),f32),V((N,128),f32),
+        V((W,D),bf),V((W,D),f32),V((2,max(cut)*KB//2,128),bf),V((max(cut)*KB//2,128),bf),V((recv,128),bf),V((W*D//128,128),bf),V((NP,3*D,128),bf),V((gains,16,D),f32),
+        pltpu.SemaphoreType.DMA((160,)),pltpu.SemaphoreType.DMA((160,)),pltpu.SemaphoreType.DMA((48,)),pltpu.SemaphoreType.DMA((18,)),pltpu.SemaphoreType.REGULAR]
+    return pl.pallas_call(functools.partial(back_kernel,groups),out_shape=outs,
+        in_specs=[vm]+[anyb]*15+[vm]*7,out_specs=[anyb]*6,scratch_shapes=scratch,
+        compiler_params=pltpu.CompilerParams(collective_id=1,has_side_effects=True,vmem_limit_bytes=63<<20),name="back")(
+        length8,tok,pa,pb,og,op,gh,att,comb,q,k,m,wq,wk,wv,wo,lse,g1,g2,*tables)
+
+def make_schedule(levels,pairs):
+    plan={}
+    def put(key,*what): plan.setdefault(key,[]).append(what)
+    put(("m",5),"E","start"); put(("m",5),"F","start")
+    put((0,0),"A","prep"); put((0,1),"A","f",0); put((0,1),"B","prep"); put((0,2),"B","f",0)
+    put((1,4),"E","prep"); put((1,5),"E","f",0); put((1,5),"F","prep"); put((1,6),"F","f",0)
+    late={"A":[(1,2),(1,8),(2,2)],"B":[(1,3),(1,9),(2,3)],"E":[(2,2),(2,7),(3,0)],"F":[(2,3),(2,8),(3,1)],
+          "C":[(0,6),(1,0),(1,4),(1,7)],0:[(1,8),(2,1),(2,5),(2,9)],1:[(2,6),(3,0),(3,4),(3,7)],2:[(3,5),(3,9),("t",1),("u",0)]}
+    gather={"A":[(2,6),(3,0),(3,3),(3,9)],"B":[(2,7),(3,1),(3,4),("t",0)],"C":[(2,4),(2,8),(3,2),(3,6)],
+            "E":[(3,4),(3,8),("t",1),("u",2)],"F":[(3,5),(3,9),("t",2),("u",3)],0:[(3,3),(3,7),("t",0),("u",0)],1:[("t",0),("t",3),("u",1)]}
+    rest=[]
+    for name in ["C","A","B",0,"E","F",1,2,3]:
+        first=1 if name in ("A","B","E","F") else 0
+        keys=late.get(name,[])
+        more=levels-first-len(keys)
+        for i in range(levels-first):
+            if i<len(keys): put(keys[i],name,"f",first+i)
+            else: rest.append((name,"f",first+i))
+        keys=gather.get(name,[]) if more<=0 else []
+        for i in range(levels):
+            if i<len(keys): put(keys[i],name,"g",i)
+            else: rest.append((name,"g",i))
+    queues={}
+    for r in rest: queues.setdefault(r[0],[]).append(r)
+    while queues:
+        for n in list(queues):
+            put("end",*queues[n].pop(0))
+            if not queues[n]: del queues[n]
+    return plan
+
+def unpack_kernel(jobs,slots,*refs):
+    src=refs[0]; n=max(j[2] for j in jobs)+1
+    outs=refs[4:4+n]; raw,wide,in_sem,out_sem,r0,r1,r2,row_in,row_out=refs[4+n+3:]
+    rows_in=[pltpu.make_async_copy(a,b,row_in.at[i]) for i,(a,b) in enumerate(zip(refs[1:4],(r0,r1,r2)))]
+    rows_out=[pltpu.make_async_copy(b,a,row_out.at[i]) for i,(a,b) in enumerate(zip(refs[4+n:4+n+3],(r0,r1,r2)))]
+    for c in rows_in: c.start()
+    load=lambda i:pltpu.make_async_copy(src.at[pl.ds(jobs[i][0],jobs[i][1])],raw.at[i%slots,pl.ds(0,jobs[i][1])],in_sem.at[i%slots])
+    def store(i):
+        _,rows,out,row,col=jobs[i]
+        return pltpu.make_async_copy(wide.at[i%slots,pl.ds(0,rows)],outs[out].at[pl.ds(row,rows),pl.ds(col*128,128)],out_sem.at[i%slots])
+    for i in range(min(slots,len(jobs))): load(i).start()
+    for i in range(len(jobs)):
+        rows=jobs[i][1]
+        load(i).wait()
+        if i>=slots: store(i-slots).wait()
+        wide[i%slots,0:rows,:]=raw[i%slots,0:rows,:].astype(jnp.float32)
+        store(i).start()
+        if i+slots<len(jobs): load(i+slots).start()
+        if i==len(jobs)//4:
+            for a,b in zip(rows_in,rows_out): a.wait(); b.start()
+    for i in range(max(0,len(jobs)-slots),len(jobs)): store(i).wait()
+    for c in rows_out: c.wait()
+
+def unpack_all(buf,rows,D,FH,W):
+    t=FH//128; n=W//128; d=D//128; slots=8
+    jobs=[(c*D,D,0,0,c) for c in range(t)]+[((t+c)*D,D,1,0,c) for c in range(t)]
+    pos=2*t*D
+    jobs+=[(pos+c*FH,FH,2,0,c) for c in range(d)]; pos+=d*FH
+    jobs+=[(pos+c*W,W,3,0,c) for c in range(d)]; pos+=d*W
+    jobs+=[(pos+(p*3+j)*D,D,4+j,0,p) for p in range(n) for j in range(3)]
+    shapes=[(D,FH),(D,FH),(FH,D),(W,D),(D,W),(D,W),(D,W)]
+    most=max(j[1] for j in jobs)
+    anyb=pl.BlockSpec(memory_space=pl.ANY)
+    return pl.pallas_call(functools.partial(unpack_kernel,jobs,slots),in_specs=[anyb]*4,out_specs=[anyb]*10,
+        out_shape=[jax.ShapeDtypeStruct(s,jnp.float32) for s in shapes]+[jax.ShapeDtypeStruct(r.shape,r.dtype) for r in rows],
+        scratch_shapes=[pltpu.VMEM((slots,most,128),jnp.bfloat16),pltpu.VMEM((slots,most,128),jnp.float32),pltpu.SemaphoreType.DMA((slots,)),pltpu.SemaphoreType.DMA((slots,))]
+            +[pltpu.VMEM(r.shape,r.dtype) for r in rows]+[pltpu.SemaphoreType.DMA((3,)),pltpu.SemaphoreType.DMA((3,))],
+        compiler_params=pltpu.CompilerParams(vmem_limit_bytes=60<<20),name="unpack")(buf,*rows)
 
 def per_device(groups,tokens,first_values,out_grad,lengths,gain_attn,gain_mlp,w_query,w_key,w_value,w_out,w_gate,w_up,w_down):
     bf=jnp.bfloat16; f32=jnp.float32
     n=groups
-    lin=lambda i,c,x:(i*2+c)*2+x
-    each=lambda fn:[(lin(i,c,x),lin(*fn(i,c,x))) for i in range(n) for c in range(2) for x in range(2)]
-    swap=each(lambda i,c,x:(i,x,c))
-    swap_some=[p for p in swap if p[0]!=p[1]]
-    over_core=each(lambda i,c,x:(i,1-c,x))
-    over_x=each(lambda i,c,x:(i,c,1-x))
-    zy=lax.axis_index("zy"); core=lax.axis_index("core"); x_at=lax.axis_index("head")
-    half=tokens.shape[0]
     D=tokens.shape[1]
-    def mine_of(v): return lax.dynamic_slice_in_dim(v,core*half,half,0)
-    def other_of(v): return lax.dynamic_slice_in_dim(v,(1-core)*half,half,0)
-    def home(v):
-        return jnp.where(core==x_at,v,exchange(v,swap_some))
     g1=gain_attn.reshape(1,D); g2=gain_mlp.reshape(1,D)
     lanes=jnp.arange(128)%(HEAD_DIM//2)
     frequency=jnp.exp(lanes.astype(f32)*(-2.0*math.log(10000.0)/HEAD_DIM))
@@ -588,51 +803,12 @@
     length8=jnp.broadcast_to(lengths.reshape(1,1),(8,128))
     (tok,og,len_full,q,k,mixed,att,lse,pa,pb,w_q,w_k,w_v,w_o,w_g,w_u,w_d)=front(n,tokens,first_values,out_grad,length8,g1,tables,(w_query,w_key,w_value,w_out,w_gate,w_up,w_down))
     length=len_full[0,:1]
-    tok_half=mine_of(tok)
-    angles=jnp.arange(SLOT).astype(f32)[:,None]*frequency[None,:]
-    cos=jnp.cos(angles); sin=jnp.sin(angles)*jnp.where((jnp.arange(128)%64)<32,-1.0,1.0)
     op,gh2a,comb=mlp(length,tok,pa,pb,og,g2,w_gate,w_up,w_down,w_g,w_u,w_d)
-    op_recv=exchange(other_of(op),over_core)
-    middle=tok_half.astype(f32)+(mine_of(pa).astype(f32)+mine_of(pb).astype(f32))
-    out=(middle+(mine_of(op).astype(f32)+op_recv.astype(f32))).astype(bf)
-    out=home(out)
-    gh2b=exchange(gh2a,over_core)
-    gm,gat,delta,gwo,gg2=mid(length,tok,pa,pb,og,gh2a,gh2b,att,g2,w_o,512)
-    dq,dk,dv=att_bwd(length,q,k,mixed,gat,lse,delta,cos,sin)
-    grad_first=home(dv)
-    gh1,gwqkv=qkv_bwd(tok,dq,dk,dv,g1,w_q,w_k,w_v,512)
-    gh1_recv=exchange(other_of(gh1),over_core)
-    gh1_full=mine_of(gh1).astype(f32)+gh1_recv.astype(f32)
-    xt=tok_half.astype(f32)
-    r1=lax.rsqrt(jnp.mean(xt*xt,axis=-1,keepdims=True)+EPS)
-    n1=xt*r1
-    gn=gh1_full*g1
-    gt=mine_of(gm).astype(f32)+r1*(gn-n1*jnp.mean(gn*n1,axis=-1,keepdims=True))
-    grad_tokens=home(gt.astype(bf))
-    gg1=jnp.sum(gh1_full*n1,axis=0)
-    gains=lax.psum(jnp.stack([gg1,0.5*jnp.sum(gg2,axis=0)]),ALL)
-    bits=[]
-    b=1
-    while b<n:
-        bits.append((each(lambda i,c,x,b=b:(i^b,c,x)),(zy//b)%2,b)); b*=2
-    def reduce_all(buf):
-        buf=halve(buf,over_x,x_at)
-        for perm,bit,_ in bits: buf=halve(buf,perm,bit)
-        piece=home(buf)
-        got=lax.all_gather(piece,"zy",axis=0,tiled=False)
-        order=[int(format(i,"0%db"%len(bits))[::-1],2) for i in range(n)]
-        got=jnp.concatenate([got[o] for o in order],0)
-        other=exchange(got,over_core)
-        return jnp.where(core==0,jnp.concatenate([got,other],0),jnp.concatenate([other,got],0))
+    out,grad_tokens,grad_first,packed,gains,_=back(n,len_full,tok,pa,pb,og,op,gh2a,att,comb,q,k,mixed,w_q,w_k,w_v,w_o,lse,g1,g2,tables)
+    gains=jnp.sum(gains.reshape(2,8,D),axis=1)
     FH=w_gate.shape[1]; W=w_query.shape[1]
-    cut=(2*FH//128)*D
-    cs=reduce_all(comb)
-    os=reduce_all(jnp.concatenate([gwo,gwqkv],0))
-    gwg=unpack(cs,0,D,FH); gwu=unpack(cs,cut//2,D,FH); gwd=unpack(cs[cut:],0,FH,D)
-    rest=os.shape[0]-gwqkv.shape[0]
-    gwo_=unpack(os,0,W,D)
-    gq,gk,gv=[unpack(os,rest+j*(W//128)*D,D,W) for j in range(3)]
-    return (out,grad_tokens,grad_first,gains[0],gains[1],gq,gk,gv,gwo_,gwg,gwu,gwd)
+    gwg,gwu,gwd,gwo,gwq,gwk,gwv,out,grad_tokens,grad_first=unpack_all(packed,(out,grad_tokens,grad_first),D,FH,W)
+    return (out,grad_tokens,grad_first,gains[0],gains[1],gwq,gwk,gwv,gwo,gwg,gwu,gwd)
 
 def solution(mesh):
     fine=Mesh(mesh.devices.reshape(-1,2,2),ALL)

time: 699 us -> 477 us (0.68)
  waiting for transfers between devices: 137 us -> 0 us
  Pallas kernels: 340 us -> 463 us
  local copies, waits for them, and re-layouts: 72.6 us -> 2.4 us
  blocking collectives: 58.6 us -> 0 us
  other arithmetic: 44 us -> 2.46 us
  starting transfers between devices: 22.3 us -> 0 us
  between operations: 15.6 us -> 1.55 us
    ppermute x18 -> x0, waiting for transfers between devices: 129 us -> none  [exchange(): return lax.ppermute(v, ALL, perm)]
    pallas_call x10 -> x2, Pallas kernels: 146 us -> 269 us  [the longest x1 253 us: back(): pl.pallas_call(functools.partial(back_kernel, groups), out_shape=outs, in...]
    psum x1 -> x0, blocking collectives: 58.6 us -> none  [per_device(): gains = lax.psum(jnp.stack([gg1, 0.5 * jnp.sum(gg2, axis=0)]), ALL)]
    unnamed x71 -> x0, local copies, waits for them, and re-layouts: 42.8 us -> none
    ppermute x18 -> x0, starting transfers between devices: 22.2 us -> none  [exchange(): return lax.ppermute(v, ALL, perm)]
    select_n x8 -> x0, other arithmetic: 18.3 us -> none  [the longest x5 9.39 us: home(): return jnp.where(core == x_at, v, exchange(v, swap_some))]
    convert_element_type x10 -> x0, other arithmetic: 14.3 us -> none  [the longest x1 7.33 us: per_device(): grad_tokens = home(gt.astype(bf))]
    concatenate x7 -> x0, local copies, waits for them, and re-layouts: 13 us -> none  [the longest x2 6.23 us: reduce_all(): jnp.concatenate([got, other], 0)]
  transfers between devices with their start and end apart: 20 -> 0, of which waited for: 7 -> 0; matrix products, arithmetic and copies ran while one was open for 12% -> 0% of each run, Pallas kernels for 18% -> 0%
where the time goes in v2:
time: 477 us; the launch traced here: 470 us
  Pallas kernels  463 us (97%)
    pallas_call x1, Pallas kernels, back(): pl.pallas_call(functools.partial(back_kernel, groups), out_shape=outs, in...  253 us
    pallas_call x1, Pallas kernels, front(): pl.pallas_call(functools.partial(front_kernel, groups), out_shape=outs, i...  117 us
    pallas_call x1, Pallas kernels, mlp(): pl.pallas_call(functools.partial(mlp_kernel, R, NS, FH), grid=(NS,), in_s...  76.8 us
    pallas_call x1, Pallas kernels, unpack_all(): pl.pallas_call(functools.partial(unpack_kernel, jobs, slots), in_specs=[a...  16.7 us

profile of v2, /device:TPU:0, one launch (start us, length us, event | category | flops | bytes accessed | tf_op | source)
XLA Modules:
  0.0 469.6 jit_solution(12994485842725610053)
XLA Ops:
  1.3 0.6 broadcast_in_dim.5.len_h
  1.9 0.8 multiply_sine_fusion.1
  2.7 0.8 multiply_sine_fusion
  3.5 117.2 %front.1 = (bf16[2048,1024]{1,0:T(8,128)(2,1)}, bf16[2048,1024]{1,0:T(8,128)(2,1)}, s32[8,128]{1,0:T(8,128)}, bf16[4,2048,128]{2,1,0:T(8,128)(2,1)}, bf16[4,2048...) custom-call(bf16[1024,1024]{1,0:T(8,128)(2,1)} %tok_h.1, ...), custom_call_target="tpu_custom_call" | custom-call | tf_op jit(solution)/shard_map/front/pallas_call | solution.py:346
  120.7 1.2 slice.9
  121.9 76.8 %mlp_256.1 = (bf16[2048,1024]{1,0:T(8,128)(2,1)}, bf16[2048,1024]{1,0:T(8,128)(2,1)}, bf16[33792,128]{1,0:T(8,128)(2,1)}) custom-call(s32[1]{0:T(128)} %bitcast.2.len_ref, bf16[2048,1024]{1,0:T(8,128)(2,1)} %get-tuple-element.48.t_ref.tok_h, bf16[2048,1024]{1,0:T(8,128)(2,1)} %get-tuple-element.49.pa_ref.pa_h, ...), custom_call_target="tpu_custom_call" | custom-call | tf_op jit(solution)/shard_map/mlp_256/pallas_call | solution.py:81
  198.7 252.5 %back.1 = (bf16[1024,1024]{1,0:T(8,128)(2,1)}, bf16[1024,1024]{1,0:T(8,128)(2,1)}, bf16[2048,512]{1,0:T(8,128)(2,1)}, bf16[50176,128]{1,0:T(8,128)(2,1)}, f32[16...) custom-call(s32[8,128]{1,0:T(8,128)} %get-tuple-element.47.len_ref, bf16[2048,1024]{1,0:T(8,128)(2,1)} %get-tuple-element.48.t_ref.tok_h, ...), custom_call_target="tpu_custom_call" | custom-call | tf_op jit(solution)/shard_map/back/pallas_call | solution.py:719
  451.2 0.9 bitcast_reduce_fusion
  452.1 0.6 fusion.3
  452.7 16.7 %unpack.1 = (f32[1024,1408]{1,0:T(8,128)}, f32[1024,1408]{1,0:T(8,128)}, f32[1408,1024]{1,0:T(8,128)}, f32[512,1024]{1,0:T(8,128)}, f32[1024,512]{1,0:T(8,128)},...) custom-call(bf16[50176,128]{1,0:T(8,128)(2,1)} %get-tuple-element.67, ...), custom_call_target="tpu_custom_call" | custom-call | tf_op jit(solution)/shard_map/unpack/pallas_call | solution.py:787
  (3 shorter events, 0.0 us)

commit v3 on v2

--- a/solution.py
+++ b/solution.py
@@ -21,70 +21,6 @@
     up=pltpu.roll(x,96,1)
     dn=pltpu.roll(x,32,1)
     return x*cos+jnp.where(lane_first,up,dn)*sin
-
-def mlp_kernel(R,NS,FH,len_ref,t_ref,pa_ref,pb_ref,og_ref,g_ref,wg_h,wu_h,wd_h,wg_f,wu_f,wd_f,
-               op_ref,gh_ref,comb_h,
-               wgu,wd,agu,ad,stage,wsem,ssem):
-    step=pl.program_id(0)
-    D=t_ref.shape[1]
-    diag=lax.axis_index("core")==lax.axis_index("head")
-    load=lambda a,b,c:[pltpu.make_async_copy(a,wgu.at[:,pl.ds(0,FH)],wsem.at[0]),
-         pltpu.make_async_copy(b,wgu.at[:,pl.ds(FH,FH)],wsem.at[1]),
-         pltpu.make_async_copy(c,wd,wsem.at[2])]
-    cps=load(wg_h,wu_h,wd_h); far=load(wg_f,wu_f,wd_f)
-    @pl.when(step==0)
-    def _():
-        @pl.when(diag)
-        def _():
-            for c in cps: c.start()
-        @pl.when(jnp.logical_not(diag))
-        def _():
-            for c in far: c.start()
-        agu[...]=jnp.zeros_like(agu)
-        ad[...]=jnp.zeros_like(ad)
-        for c in cps: c.wait()
-    x=t_ref[...].astype(jnp.float32)+(pa_ref[...].astype(jnp.float32)+pb_ref[...].astype(jnp.float32))
-    n,_=norm_block(x,None)
-    h=(n*g_ref[...]).astype(jnp.bfloat16)
-    row=lax.broadcasted_iota(jnp.int32,(R,1),0)+step*R
-    g=jnp.where(row<len_ref[0],og_ref[...],jnp.zeros((),jnp.bfloat16))
-    gu=dot(h,wgu[...])
-    gate=gu[:,:FH]; up=gu[:,FH:]
-    gh=dot(g,wd[...],NT)
-    sg=0.5*jnp.tanh(0.5*gate)+0.5
-    silu=gate*sg
-    hid=(silu*up).astype(jnp.bfloat16)
-    gu_=(gh*silu).astype(jnp.bfloat16)
-    gg_=(gh*up*(sg*(1.0+gate*(1.0-sg)))).astype(jnp.bfloat16)
-    op_ref[...]=dot(hid,wd[...]).astype(jnp.bfloat16)
-    gh_ref[...]=(dot(gg_,wgu[:,:FH],NT)+dot(gu_,wgu[:,FH:],NT)).astype(jnp.bfloat16)
-    ad[...]+=dot(hid,g,TN)
-    agu[:,:FH]+=dot(h,gg_,TN)
-    agu[:,FH:]+=dot(h,gu_,TN)
-    @pl.when(step==NS-1)
-    def _():
-        tiles=[(agu,c,c*D,D) for c in range(2*FH//128)]+[(ad,c,(2*FH//128)*D+c*FH,FH) for c in range(D//128)]
-        pend=[None]*4
-        for i,(a,c,off,ln) in enumerate(tiles):
-            s=i%4
-            if pend[s] is not None: pend[s].wait()
-            stage[s,0:ln,:]=a[:,c*128:(c+1)*128].astype(jnp.bfloat16)
-            cp=pltpu.make_async_copy(stage.at[s,pl.ds(0,ln)],comb_h.at[pl.ds(off,ln)],ssem.at[s])
-            cp.start(); pend[s]=cp
-        for p in pend: p.wait()
-def mlp(length,t,pa,pb,og,gain,wg,wu,wd,wg_f,wu_f,wd_f,R=256):
-    N,D=t.shape; FH=wg.shape[1]; NS=N//R
-    rb=pl.BlockSpec((R,D),lambda i:(i,0))
-    anyb=pl.BlockSpec(memory_space=pl.ANY)
-    full=lambda a:pl.BlockSpec(a.shape,lambda i:(0,0),pipeline_mode=pl.Buffered(1))
-    rows=(2*FH//128)*D+(D//128)*FH
-    return pl.pallas_call(functools.partial(mlp_kernel,R,NS,FH),grid=(NS,),
-        in_specs=[pl.BlockSpec(memory_space=pltpu.SMEM),rb,rb,rb,rb,full(gain)]+[anyb]*6,
-        out_specs=[rb,rb,anyb],
-        out_shape=[jax.ShapeDtypeStruct((N,D),jnp.bfloat16)]*2+[jax.ShapeDtypeStruct((rows,128),jnp.bfloat16)],
-        scratch_shapes=[pltpu.VMEM((D,2*FH),jnp.bfloat16),pltpu.VMEM((FH,D),jnp.bfloat16),pltpu.VMEM((D,2*FH),jnp.float32),pltpu.VMEM((FH,D),jnp.float32),
-            pltpu.VMEM((4,max(D,FH),128),jnp.bfloat16),pltpu.SemaphoreType.DMA((3,)),pltpu.SemaphoreType.DMA((4,))],
-        compiler_params=pltpu.CompilerParams(vmem_limit_bytes=60<<20),name="mlp_%d"%R)(length,t,pa,pb,og,gain,wg,wu,wd,wg_f,wu_f,wd_f)
 
 
 ALL=("zy","core","head")
@@ -348,34 +284,46 @@
         compiler_params=pltpu.CompilerParams(collective_id=0,has_side_effects=True,vmem_limit_bytes=58<<20),name="front")(tok,fv,og,length,gain,*tables,*ws)
 
 class Reduce:
-    def __init__(self,links,order,src,offset,rows,recv,recv_at,result,result_at,at,landing=None,held=None):
-        self.links=links; self.order=order; self.rows=rows; self.src=src; self.offset=offset; self.at=at
-        self.levels=len(order); self.bufs=[]; self.sends=[]
-        for level in range(self.levels):
-            size=rows>>(level+1)
-            if level==0 and held is not None: self.bufs.append(held)
-            else: self.bufs.append(recv.at[pl.ds(recv_at,size)]); recv_at+=size
-        self.landing=landing; self.sent1=False
+    def __init__(self,links,order,src,offset,rows,recv,recv_at,at,keep=None):
+        self.order=order; self.rows=rows; self.offset=offset; self.at=at; self.then=None
+        self.keep=src if keep is None else keep
+        self.levels=len(order); self.leaf=rows>>self.levels; self.bufs=[]; self.sends=[]
+        for level,name in enumerate(order):
+            size=rows>>(level+1); bit=at.bit(name)
+            self.bufs.append(recv.at[pl.ds(recv_at,size)]); recv_at+=size
+            if level==0: source=src.at[pl.ds(pl.multiple_of(offset+(1-bit)*size,16),size)]
+            else: source=self.bufs[level-1].at[pl.ds(pl.multiple_of((1-bit)*size,16),size)]
+            self.sends.append(links.remote(source,self.bufs[level],at.partner(name)))
         self.recv_end=recv_at
-        half=rows//2
-        for level,name in enumerate(order):
-            size=rows>>(level+1)
-            bit=at.bit(name)
-            if level==0:
-                source=src.at[pl.ds(pl.multiple_of(offset+(1-bit)*half,16),half)]
-            else:
-                source=self.bufs[level-1].at[pl.ds(pl.multiple_of((1-bit)*size,16),size)]
-            self.sends.append(links.remote(source,landing if level==0 and landing is not None else self.bufs[level],at.partner(name)))
-        self.result=result; self.result_at=result_at
-        leaf=rows>>self.levels; self.leaf=leaf
+    def start(self): self.sends[0].start()
+    def finish(self,level):
+        self.sends[level].wait_recv()
+        size=self.rows>>(level+1); bit=self.at.bit(self.order[level])
+        into=self.bufs[level]
+        if level==0: mine=self.keep.at[pl.ds(pl.multiple_of(self.offset+bit*size,16),size)]
+        else: mine=self.bufs[level-1].at[pl.ds(pl.multiple_of(bit*size,16),size)]
+        step=math.gcd(size,512)
+        def add(i,_):
+            rows=pl.ds(pl.multiple_of(i*step,step),step)
+            into[rows,:]=(into[rows,:].astype(jnp.float32)+mine[rows,:].astype(jnp.float32)).astype(jnp.bfloat16)
+            return 0
+        lax.fori_loop(0,size//step,add,0)
+        if level+1<self.levels: self.sends[level+1].start()
+        elif self.then is not None: self.then()
+    def drain_sends(self):
+        for c in self.sends: c.wait_send()
+
+class Gather:
+    def __init__(self,links,order,leaf,rows,result,result_at,at):
+        self.at=at; self.steps=len(order); size=rows>>self.steps
         weight={name:rows>>(i+1) for i,name in enumerate(order)}
         own=sum(at.bit(name)*weight[name] for name in order)
-        spot=result.at[pl.ds(pl.multiple_of(result_at+own,16),leaf)]
-        self.swap=links.remote(self.bufs[-1],spot,at.swap)
-        self.keep=links.copy(self.bufs[-1],spot)
+        spot=result.at[pl.ds(pl.multiple_of(result_at+own,16),size)]
+        self.swap=links.remote(leaf,spot,at.swap)
+        self.keep=links.copy(leaf,spot)
         self.gathers=[]; gathered=[]
         for name in sorted([n for n in order if n!="x"],reverse=True)+["x"]:
-            unit=leaf; apart=[]
+            unit=size; apart=[]
             for w in sorted(gathered):
                 if w==unit: unit*=2
                 else: apart.append(w)
@@ -388,29 +336,12 @@
                 block=result.at[pl.ds(pl.multiple_of(result_at+base+c,16),unit)]
                 step.append(links.remote(block,block,device))
             self.gathers.append(step); gathered.append(weight[name])
-    def start(self): self.sends[0].start()
-    def finish(self,level,got=None):
-        if got is None: self.sends[level].wait_recv()
-        size=self.rows>>(level+1)
-        bit=self.at.bit(self.order[level])
-        into=self.bufs[level]
-        if level==0:
-            mine=got if got is not None else self.src.at[pl.ds(pl.multiple_of(self.offset+bit*size,16),size)]
-        else:
-            mine=self.bufs[level-1].at[pl.ds(pl.multiple_of(bit*size,16),size)]
-        step=math.gcd(size,512)
-        def add(i,_):
-            rows=pl.ds(pl.multiple_of(i*step,step),step)
-            into[rows,:]=(into[rows,:].astype(jnp.float32)+mine[rows,:].astype(jnp.float32)).astype(jnp.bfloat16)
-            return 0
-        lax.fori_loop(0,size//step,add,0)
-        if level+1<self.levels: self.sends[level+1].start()
-        else:
-            @pl.when(self.at.off)
-            def _(): self.swap.start()
-            @pl.when(self.at.diag)
-            def _(): self.keep.start()
-    def gather(self,step):
+    def begin(self):
+        @pl.when(self.at.off)
+        def _(): self.swap.start()
+        @pl.when(self.at.diag)
+        def _(): self.keep.start()
+    def go(self,step):
         if step==0:
             @pl.when(self.at.off)
             def _(): self.swap.wait_recv()
@@ -421,8 +352,6 @@
         for c in self.gathers[step]: c.start()
     def drain(self):
         for c in self.gathers[-1]: c.wait_recv()
-        for i,c in enumerate(self.sends):
-            if not (i==1 and self.sent1): c.wait_send()
         @pl.when(self.at.off)
         def _(): self.swap.wait_send()
         for s in self.gathers:
@@ -441,47 +370,223 @@
     while b<groups: at.bits.append(b); b*=2
     return at
 
+def passes_of(tiles):
+    a=(4*tiles+10)//11; b=(3*tiles+10)//11; c=(tiles-a-b+1)//2
+    return (a,b,c,tiles-a-b-c)
+def runs_of(tiles,d_tiles):
+    KB=1024; pos=0; out=[]
+    for t,n in enumerate(passes_of(tiles)):
+        units=(2*n*d_tiles*128+d_tiles*128*n)//KB
+        parts=[[units//2,units-units//2],[units//3,units//3,units-2*(units//3)],[units],[0,units]][t]
+        for i,u in enumerate(parts):
+            if u: out.append((t,"abc"[i]+str(t),i,pos,u*KB))
+            pos+=u*KB
+    return out
+def orders_of(bits):
+    return [["x"]+bits,bits[:1]+["x"]+bits[1:],bits[1:2]+bits[:1]+["x"]+bits[2:]]
+
+MLP_PLAN={
+    (2, 0):[('a0',0),('b0',0)],
+    (2, 6):[('a1',0),('b1',0),('c1',0)],
+    (3, 2):[('a0',1),('b0',1)],
+    (3, 4):[('a1',1),('b1',1)],
+    (3, 5):[('c1',1),('a0',2)],
+    (3, 7):[('b0',2)],
+}
+def mlp_kernel(groups,len_ref,tok_h,pa_h,pb_h,og_h,g_ref,wg_h,wu_h,wd_h,wg_f,wu_f,wd_f,
+        op_o,opr_o,gh_o,ghr_o,rest_o,leaf_o,
+        tokb,pab,pbb,h_v,g_v,oacc,gacc,wgu,wd,agu,ad,comb,recv_v,
+        send_sem,recv_sem,local_sem,blk_sem,w_sem,out_sem,ex_send,ex_recv):
+    at=place_of(groups); core=at.core; diag=at.diag
+    MESH=pl.DeviceIdType.MESH
+    N,D=tok_h.shape; FH=wg_h.shape[1]; R=256; NB=N//R
+    passes=passes_of(FH//128); T=len(passes)
+    L=Links(send_sem,recv_sem,local_sem)
+    orders=orders_of(at.bits)
+    runs={}; rp=0; lp=0; leaves=[]
+    for t,name,kind,pos,rows in runs_of(FH//128,D//128):
+        if t<2:
+            r=Reduce(L,orders[kind],comb,pos,rows,recv_v,rp,at); rp=r.recv_end
+            runs[name]=(t,r)
+            leaves.append(L.copy(r.bufs[-1],leaf_o.at[pl.ds(lp,r.leaf)])); lp+=r.leaf
+    out_rest=L.copy(comb.at[pl.ds(comb.shape[0]-rest_o.shape[0],rest_o.shape[0])],rest_o)
+    barrier=pltpu.get_barrier_semaphore()
+    partners=[at.core_dev]+[at.partner(n) for n in ["x"]+at.bits]
+    for d in partners: pl.semaphore_signal(barrier,inc=1,device_id=d,device_id_type=MESH)
+    pl.semaphore_wait(barrier,len(partners))
+    firsts=[sum(passes[:t]) for t in range(T)]
+    def w_copies(t,src):
+        n=passes[t]*128; f=firsts[t]*128; s=t%2
+        a,b,c=src
+        return [pltpu.make_async_copy(a.at[:,pl.ds(f,n)],wgu.at[s,:,pl.ds(0,n)],w_sem.at[0]),
+            pltpu.make_async_copy(b.at[:,pl.ds(f,n)],wgu.at[s,:,pl.ds(n,n)],w_sem.at[1]),
+            pltpu.make_async_copy(c.at[pl.ds(f,n)],wd.at[s,pl.ds(0,n)],w_sem.at[2])]
+    def w_start(t):
+        @pl.when(diag)
+        def _():
+            for c in w_copies(t,(wg_h,wu_h,wd_h)): c.start()
+        @pl.when(at.off)
+        def _():
+            for c in w_copies(t,(wg_f,wu_f,wd_f)): c.start()
+    def w_wait(t):
+        for c in w_copies(t,(wg_h,wu_h,wd_h)): c.wait()
+    w_start(0)
+    rowsof=lambda b:pl.ds(pl.multiple_of(((core*(NB//2)+b)%NB)*R,R),R)
+    def loads(b):
+        s=b%2
+        return [pltpu.make_async_copy(h.at[rowsof(b)],v.at[s],blk_sem.at[s,i]) for i,(h,v) in enumerate(((tok_h,tokb),(pa_h,pab),(pb_h,pbb)))]+[
+            pltpu.make_async_copy(og_h.at[rowsof(b)],g_v.at[rowsof(b)],blk_sem.at[s,3])]
+    for c in loads(0): c.start()
+    w_wait(0)
+    gain=g_ref[...]; length=len_ref[0:1,0:1]
+    def to_partner(b):
+        send=[pltpu.make_async_remote_copy(src_ref=g_v.at[rowsof(b)],dst_ref=ghr_o.at[rowsof(b)],send_sem=ex_send.at[0,b],recv_sem=ex_recv.at[0,b],device_id=at.core_dev,device_id_type=MESH)]
+        k=b-NB//2
+        last=pltpu.make_async_remote_copy(src_ref=h_v.at[rowsof(b)],dst_ref=opr_o.at[pl.ds(pl.multiple_of(k*R,R),R)],send_sem=ex_send.at[1,b],recv_sem=ex_recv.at[1,b],device_id=at.core_dev,device_id_type=MESH)
+        return send,last
+    def outs(b): return [pltpu.make_async_copy(h_v.at[rowsof(b)],op_o.at[rowsof(b)],out_sem.at[0,b]),pltpu.make_async_copy(g_v.at[rowsof(b)],gh_o.at[rowsof(b)],out_sem.at[1,b])]
+    for t,n in enumerate(passes):
+        s=t%2; w=n*128
+        def block(b,_):
+            for B in range(NB):
+                acts=MLP_PLAN.get((t,B))
+                if acts:
+                    @pl.when(b==B)
+                    def _():
+                        for name,level in acts:
+                            if name in runs and level<runs[name][1].levels: runs[name][1].finish(level)
+            rows=rowsof(b)
+            if t==0:
+                @pl.when(b+1<NB)
+                def _():
+                    for c in loads(b+1): c.start()
+                for c in loads(b): c.wait()
+                i=b%2
+                x=tokb[i].astype(jnp.float32)+(pab[i].astype(jnp.float32)+pbb[i].astype(jnp.float32))
+                nn,_=norm_block(x,None)
+                h=(nn*gain).astype(jnp.bfloat16)
+                h_v[rows,:]=h
+                row=lax.broadcasted_iota(jnp.int32,(R,1),0)+((core*(NB//2)+b)%NB)*R
+                g=jnp.where(row<length,g_v[rows,:],jnp.zeros((),jnp.bfloat16))
+                g_v[rows,:]=g
+            else:
+                h=h_v[rows,:]; g=g_v[rows,:]
+            gu=dot(h,wgu[s,:,0:2*w])
+            gate=gu[:,:w]; up=gu[:,w:]
+            gh=dot(g,wd[s,0:w,:],NT)
+            sg=0.5*jnp.tanh(0.5*gate)+0.5
+            silu=gate*sg
+            hid=(silu*up).astype(jnp.bfloat16)
+            both=jnp.concatenate([(gh*up*(sg*(1.0+gate*(1.0-sg)))).astype(jnp.bfloat16),(gh*silu).astype(jnp.bfloat16)],axis=1)
+            o=dot(hid,wd[s,0:w,:])
+            q=dot(both,wgu[s,:,0:2*w],NT)
+            da=dot(hid,g,TN); dg=dot(h,both,TN)
+            if t==0: oacc[rows,:]=o; gacc[rows,:]=q
+            elif t<T-1: oacc[rows,:]+=o; gacc[rows,:]+=q
+            else:
+                h_v[rows,:]=(oacc[rows,:]+o).astype(jnp.bfloat16)
+                g_v[rows,:]=(gacc[rows,:]+q).astype(jnp.bfloat16)
+                for c in outs(b): c.start()
+                send,last=to_partner(b)
+                for c in send: c.start()
+                @pl.when(b>=NB//2)
+                def _(): last.start()
+            @pl.when(b==0)
+            def _(): ad[0:w,:]=da; agu[:,0:2*w]=dg
+            @pl.when(b>0)
+            def _(): ad[0:w,:]+=da; agu[:,0:2*w]+=dg
+            if t+1<T:
+                @pl.when(b==NB-2)
+                def _(): w_start(t+1)
+            return 0
+        lax.fori_loop(0,NB,block,0)
+        base=firsts[t]*(2*D+D)
+        for c in range(2*n): comb[base+c*D:base+(c+1)*D,:]=agu[:,c*128:(c+1)*128].astype(jnp.bfloat16)
+        base+=2*n*D
+        for c in range(D//128): comb[base+c*w:base+(c+1)*w,:]=ad[0:w,c*128:(c+1)*128].astype(jnp.bfloat16)
+        for name,(rt,r) in runs.items():
+            if rt==t: r.start()
+        if t+1<T: w_wait(t+1)
+    out_rest.start()
+    planned={(a,l) for v in MLP_PLAN.values() for a,l in v}
+    queues=[[(r,l) for l in range(r.levels) if (name,l) not in planned] for name,(rt,r) in runs.items()]
+    while any(queues):
+        for q in queues:
+            if q:
+                r,l=q.pop(0); r.finish(l)
+    for c in leaves: c.start()
+    def settle(b,_):
+        for c in outs(b): c.wait()
+        send,last=to_partner(b)
+        for c in send: c.wait()
+        @pl.when(b>=NB//2)
+        def _(): last.wait()
+        return 0
+    lax.fori_loop(0,NB,settle,0)
+    for c in leaves: c.wait()
+    out_rest.wait()
+    for _,r in runs.values(): r.drain_sends()
+
+def mlp(groups,length8,tok,pa,pb,og,gain,ws,full):
+    bf=jnp.bfloat16; f32=jnp.float32; S=jax.ShapeDtypeStruct; V=pltpu.VMEM
+    N,D=tok.shape; FH=ws[0].shape[1]; R=256
+    anyb=pl.BlockSpec(memory_space=pl.ANY); vm=pl.BlockSpec(memory_space=pltpu.VMEM)
+    levels=1+int(math.log2(groups))
+    all_runs=runs_of(FH//128,D//128)
+    early=[r for r in all_runs if r[0]<2]
+    recv=sum(r[4]>>(l+1) for r in early for l in range(levels))
+    leaf=sum(r[4]>>levels for r in early)
+    total=sum(r[4] for r in all_runs); rest=sum(r[4] for r in all_runs if r[0]>=2)
+    w=max(passes_of(FH//128))*128
+    outs=[S((N,D),bf),S((N//2,D),bf),S((N,D),bf),S((N,D),bf),S((rest,128),bf),S((leaf,128),bf)]
+    DM=pltpu.SemaphoreType.DMA
+    return pl.pallas_call(functools.partial(mlp_kernel,groups),out_shape=outs,in_specs=[vm]+[anyb]*4+[vm]+[anyb]*6,out_specs=[anyb]*6,
+        scratch_shapes=[V((2,R,D),bf)]*3+[V((N,D),bf),V((N,D),bf),V((N,D),f32),V((N,D),f32),V((2,D,2*w),bf),V((2,w,D),bf),V((D,2*w),f32),V((w,D),f32),V((total,128),bf),V((recv,128),bf),
+            DM((48,)),DM((48,)),DM((16,)),DM((2,4)),DM((3,)),DM((2,N//R)),DM((2,N//R)),DM((2,N//R))],
+        compiler_params=pltpu.CompilerParams(collective_id=2,has_side_effects=True,vmem_limit_bytes=63<<20),name="mlp")(length8,tok,pa,pb,og,gain,*ws,*full)
+
 def back_kernel(groups,
-        len_ref,tok_h,pa_h,pb_h,og_h,op_h,gh_h,att_h,comb_h,q_h,k_h,m_h,wq_h,wk_h,wv_h,wo_h,lse_ref,g1_ref,g2_ref,ch_ref,sh_ref,cl_ref,sl_ref,
-        out_o,gt_o,gf_o,res_o,gains_o,land_o,
-        tokb,pab,pbb,ogb,gab,atb,opb,oprv,ghb,h1_v,gm_v,gat_v,dl_v,qd,kd,md,ks,qs,vs,dqa,cos_v,sin_v,wo_v,acc,keep_v,got_v,recv_v,gwo_v,gw_v,gain_v,
-        send_sem,recv_sem,local_sem,blk_sem,free_sem):
+        len_ref,tok_h,pa_h,pb_h,og_h,op_h,opr_h,gh_h,ghr_h,att_h,rest_h,leaf_h,q_h,k_h,m_h,wq_h,wk_h,wv_h,wo_h,lse_ref,g1_ref,g2_ref,ch_ref,sh_ref,cl_ref,sl_ref,
+        out_o,gt_o,gf_o,res_o,gains_o,
+        tokb,pab,pbb,ogb,gab,grb,orb,atb,opb,oprv,ghb,h1_v,gm_v,gat_v,dl_v,qd,kd,md,ks,qs,vs,dqa,cos_v,sin_v,wo_v,acc,src_v,leaf_v,recv_v,gwo_v,gw_v,gain_v,
+        send_sem,recv_sem,local_sem,blk_sem):
     at=place_of(groups); core=at.core; off=at.off; diag=at.diag
     L=Links(send_sem,recv_sem,local_sem)
     MESH=pl.DeviceIdType.MESH
     N,D=tok_h.shape; half=N//2; W=wo_h.shape[0]; NP=W//128; R=256; NB=N//R
     bits=at.bits
-    order1=["x"]+bits; order2=bits[:1]+["x"]+bits[1:]; order3=bits[1:2]+bits[:1]+["x"]+bits[2:]
-    total=comb_h.shape[0]; KB=1024; units=total//KB
-    cut=[units//4,units//4,units//4,units-3*(units//4)]
-    runs={}; pos=0; rp=0
-    keep_slot={"A":0,"B":1,"E":0,"F":1}; follows={"E":"A","F":"B"}
-    for name,c,order in (("A",cut[0],order1),("B",cut[3],order2),("E",cut[1],order1),("F",cut[2],order2)):
-        runs[name]=Reduce(L,order,comb_h,pos,c*KB,recv_v,rp,res_o,pos,at,land_o.at[pl.ds(pos//2,c*KB//2)],keep_v.at[keep_slot[name],pl.ds(0,c*KB//2)]); rp=runs[name].recv_end; pos+=c*KB
-    runs["C"]=Reduce(L,order3,gwo_v,0,gwo_v.shape[0],recv_v,rp,res_o,pos,at); rp=runs["C"].recv_end; pos+=gwo_v.shape[0]
-    for p in range(NP):
-        runs[p]=Reduce(L,order3,gw_v.at[p],0,gw_v.shape[1],recv_v,rp,res_o,pos,at); rp=runs[p].recv_end; pos+=gw_v.shape[1]
-    def both_copies(name):
-        r=runs[name]; h=r.rows//2
-        mine=comb_h.at[pl.ds(pl.multiple_of(r.offset+at.bit(r.order[0])*h,16),h)]
-        return (pltpu.make_async_copy(mine,r.bufs[0],blk_sem.at[16]),pltpu.make_async_copy(r.landing,got_v.at[pl.ds(0,h)],blk_sem.at[17]))
-    def prep(name):
-        if name in follows: runs[follows[name]].sends[1].wait_send(); runs[follows[name]].sent1=True
-        runs[name].sends[0].wait_recv()
-        for c in both_copies(name): c.start()
-    def finish0(name):
-        for c in both_copies(name): c.wait()
-        runs[name].finish(0,got_v)
+    orders=orders_of(bits); FH=rest_h.shape[0]; all_runs=runs_of(FF_TILES(res_o.shape[0],W,D),D//128)
+    total=sum(r[4] for r in all_runs); rest_at=total-rest_h.shape[0]
+    runs={}; gathers={}; rp=0; lp=0
+    for t,name,kind,pos,rows in all_runs:
+        if t<2:
+            size=rows>>(1+len(bits))
+            gathers[name]=Gather(L,orders[kind],leaf_v.at[pl.ds(lp,size)],rows,res_o,pos,at); lp+=size
+        else: runs[name]=Reduce(L,orders[kind],rest_h,pos-rest_at,rows,recv_v,rp,at,keep=src_v); rp=runs[name].recv_end
+    early=list(gathers); late=list(runs)
+    runs["C"]=Reduce(L,orders[2],gwo_v,0,gwo_v.shape[0],recv_v,rp,at); rp=runs["C"].recv_end
+    for p in range(NP): runs[p]=Reduce(L,orders[2],gw_v.at[p],0,gw_v.shape[1],recv_v,rp,at); rp=runs[p].recv_end
+    places={name:(orders[kind],rows,pos) for t,name,kind,pos,rows in all_runs}
+    places["C"]=(orders[2],gwo_v.shape[0],total)
+    for p in range(NP): places[p]=(orders[2],gw_v.shape[1],total+gwo_v.shape[0]+p*gw_v.shape[1])
+    for name,r in runs.items():
+        order,rows,pos=places[name]
+        gathers[name]=Gather(L,order,r.bufs[-1],rows,res_o,pos,at); r.then=gathers[name].begin
     first_rows=lambda b:pl.multiple_of(((core*(NB//2)+b)%NB)*R,R)
     blk=lambda b:pl.ds(first_rows(b),R)
     theirs=lambda b:pl.ds(pl.multiple_of((((1-core)*(NB//2)+b)%NB)*R,R),R)
-    ex_gh=[L.remote(gh_h.at[theirs(b)],ghb.at[theirs(b)],at.core_dev) for b in range(NB)]
-    ex_op=[L.remote(op_h.at[theirs(b)],oprv.at[pl.ds(b*R,R)],at.core_dev) for b in range(NB//2)]
-    sw_out=[L.remote(opb.at[pl.ds(b*R,R)],out_o.at[pl.ds(b*R,R)],at.swap) for b in range(NB//2)]
-    lo_out=[L.copy(opb.at[pl.ds(b*R,R)],out_o.at[pl.ds(b*R,R)]) for b in range(NB//2)]
-    sw_gf=[L.remote(md.at[p],gf_o.at[:,pl.ds(p*128,128)],at.swap) for p in range(NP)]
-    lo_gf=[L.copy(md.at[p],gf_o.at[:,pl.ds(p*128,128)]) for p in range(NP)]
-    ex_g1=[L.remote(ghb.at[theirs(b)],oprv.at[pl.ds(b*R,R)],at.core_dev) for b in range(NB//2)]
+    piece=half//8
+    sw_out=[L.remote(opb.at[pl.ds(i*piece,piece)],out_o.at[pl.ds(i*piece,piece)],at.swap) for i in range(8)]
+    lo_out=[L.copy(opb.at[pl.ds(i*piece,piece)],out_o.at[pl.ds(i*piece,piece)]) for i in range(8)]
+    sw_gf=[[L.remote(md.at[p,pl.ds(i*half,half)],gf_o.at[pl.ds(i*half,half),pl.ds(p*128,128)],at.swap) for i in range(2)] for p in range(NP)]
+    lo_gf=[[L.copy(md.at[p,pl.ds(i*half,half)],gf_o.at[pl.ds(i*half,half),pl.ds(p*128,128)]) for i in range(2)] for p in range(NP)]
+    def home(name,i):
+        a,b=(sw_out[i],lo_out[i]) if name=="out" else (sw_gf[name[1]][i],lo_gf[name[1]][i])
+        @pl.when(off)
+        def _(): a.start()
+        @pl.when(diag)
+        def _(): b.start()
+    ex_g1=[L.remote(ghb.at[pl.ds(b*R,R)],oprv.at[pl.ds(b*R,R)],at.core_dev) for b in range(NB//2)]
     sw_gt=[L.remote(gm_v.at[pl.ds(b*R,R)],gt_o.at[pl.ds(b*R,R)],at.swap) for b in range(NB//2)]
     lo_gt=[L.copy(gm_v.at[pl.ds(b*R,R)],gt_o.at[pl.ds(b*R,R)]) for b in range(NB//2)]
     names=["c","x"]+bits
@@ -497,19 +602,22 @@
         pl.semaphore_wait(barrier,3+len(bits))
     @pl.when(diag)
     def _(): pl.semaphore_wait(barrier,2+len(bits))
-    for c in ex_gh[:2]: c.start()
-    ex_op[0].start()
-    for b in range(2,NB): ex_gh[b].start()
-    for c in ex_op[1:]: c.start()
-    runs["A"].start(); runs["B"].start()
+    for name in late: runs[name].start()
+    own_rest=L.copy(rest_h,src_v); own_leaf=L.copy(leaf_h,leaf_v)
+    own_leaf.start()
     def block_loads(b):
         s=b%2
-        pairs=[(tok_h,tokb),(pa_h,pab),(pb_h,pbb),(og_h,ogb),(gh_h,gab),(att_h,atb)]
-        cps=[pltpu.make_async_copy(h.at[blk(b)],v.at[s],blk_sem.at[s*8+i]) for i,(h,v) in enumerate(pairs)]
-        if b<NB//2: cps.append(pltpu.make_async_copy(op_h.at[blk(b)],opb.at[pl.ds(b*R,R)],blk_sem.at[s*8+6]))
+        pairs=[(tok_h,tokb),(pa_h,pab),(pb_h,pbb),(og_h,ogb),(gh_h,gab),(ghr_h,grb),(att_h,atb)]
+        cps=[pltpu.make_async_copy(h.at[blk(b)],v.at[s],blk_sem.at[s*9+i]) for i,(h,v) in enumerate(pairs)]
+        if b<NB//2:
+            cps.append(pltpu.make_async_copy(op_h.at[blk(b)],opb.at[pl.ds(b*R,R)],blk_sem.at[s*9+7]))
+            cps.append(pltpu.make_async_copy(opr_h.at[pl.ds(b*R,R)],orb.at[s],blk_sem.at[s*9+8]))
         return cps
     for c in block_loads(0): c.start()
     for c in loads: c.start()
+    own_rest.start()
+    own_leaf.wait()
+    for name in early: gathers[name].begin()
     sign=jnp.where((lax.broadcasted_iota(jnp.int32,(1,128),1)%64)<32,-1.0,1.0)
     cl=cl_ref[...]; sl=sl_ref[...]
     def table(a,_):
@@ -523,29 +631,38 @@
     length=len_ref[0:1,0:1]
     hr=lax.broadcasted_iota(jnp.int32,(8*NP,W),0); ln=lax.broadcasted_iota(jnp.int32,(8*NP,W),1)
     ind=jnp.where(((ln//64)==((hr//8)*2+hr%8))&(hr%8<2),1.0,0.0).astype(jnp.bfloat16)
-    loads[0].wait()
+    loads[0].wait(); own_rest.wait()
     gsum=None
     plan={}
     todo=lambda t,*acts: plan.setdefault(t,[]).extend(acts)
-    for k,v in make_schedule(1+len(bits),NP).items():
-        for name,what,*arg in v:
-            if what=="start": todo(k,runs[name].start)
-            elif what=="prep": todo(k,functools.partial(prep,name))
-            elif what=="f": todo(k,functools.partial(finish0,name) if (arg[0]==0 and name in keep_slot) else functools.partial(runs[name].finish,arg[0]))
-            elif what=="g": todo(k,functools.partial(runs[name].gather,arg[0]))
+    def action(name,what,level): return functools.partial(runs[name].finish if what=="f" else gathers[name].go,level)
+    done=set()
+    levels=1+len(bits)
+    for key,items in BACK_PLAN.items():
+        for item in items:
+            if item[1]=="s": todo(key,functools.partial(home,item[0],item[2])); done.add(item)
+            elif levels==4 or item[1]=="f": todo(key,action(*item)); done.add(item)
+    left=[i for i in BACK_END if levels==4 and i not in done]
+    done.update(left)
+    for i in range(2*levels):
+        for name in list(gathers):
+            what,level=("f",i) if i<levels else ("g",i-levels)
+            if (what=="g" or name in runs) and (name,what,level) not in done: left.append((name,what,level))
+    for item in left: todo("end",action(*item))
+    for name,i in [("out",i) for i in range(8)]+[(("gf",p),i) for p in range(NP) for i in range(2)]:
+        if (name,"s",i) not in done: todo(("u",0),functools.partial(home,name,i))
     for b in range(NB):
         for a in plan.get(("m",b),[]): a()
         if b+1<NB:
             for c in block_loads(b+1): c.start()
         for c in block_loads(b): c.wait()
-        ex_gh[b].wait_recv()
         s=b%2; r0=first_rows(b)
         t=tokb[s].astype(jnp.float32)
         n1,_=norm_block(t,None)
         h1_v[blk(b),:]=(n1*g1).astype(jnp.bfloat16)
         mid=t+(pab[s].astype(jnp.float32)+pbb[s].astype(jnp.float32))
         n,r=norm_block(mid,None)
-        gh2=gab[s].astype(jnp.float32)+ghb[blk(b),:].astype(jnp.float32)
+        gh2=gab[s].astype(jnp.float32)+grb[s].astype(jnp.float32)
         row=lax.broadcasted_iota(jnp.int32,(R,1),0)+r0
         mg=jnp.where(row<length,ogb[s].astype(jnp.float32),0.0)
         gn=gh2*g2
@@ -555,9 +672,8 @@
         gsum=part if gsum is None else gsum+part
         if b<NB//2:
             gm_v[b*R:(b+1)*R,:]=gm
-            ex_op[b].wait_recv()
             mine=slice(b*R,(b+1)*R)
-            opb[mine,:]=(mid+(opb[mine,:].astype(jnp.float32)+oprv[mine,:].astype(jnp.float32))).astype(jnp.bfloat16)
+            opb[mine,:]=(mid+(opb[mine,:].astype(jnp.float32)+orb[s].astype(jnp.float32))).astype(jnp.bfloat16)
         at_b=atb[s]
         ga=dot(gm,wo_v[...],NT).astype(jnp.bfloat16)
         for p in range(NP): gat_v[p,blk(b),:]=ga[:,p*128:(p+1)*128]
@@ -570,7 +686,6 @@
     for c in range(D//128): gwo_v[c*W:(c+1)*W,:]=acc[:,c*128:(c+1)*128].astype(jnp.bfloat16)
     gain_v[0,8:16,:]=gsum*0.5
     runs["C"].start()
-    pl.semaphore_signal(free_sem,inc=1,device_id=at.core_dev,device_id_type=MESH)
     for c in proj: c.start()
     for c in loads[1:]: c.wait()
     BQ=BK=512
@@ -628,21 +743,9 @@
             @pl.when(p==P_)
             def _():
                 runs[P_].start()
-                @pl.when(off)
-                def _(): sw_gf[P_].start()
-                @pl.when(diag)
-                def _(): lo_gf[P_].start()
-                if P_==0:
-                    @pl.when(off)
-                    def _():
-                        for c in sw_out: c.start()
-                    @pl.when(diag)
-                    def _():
-                        for c in lo_out: c.start()
         return 0
     lax.fori_loop(0,NP,pair,0)
     for c in proj: c.wait()
-    pl.semaphore_wait(free_sem,1)
     def tok_load(b): return pltpu.make_async_copy(tok_h.at[blk(b)],tokb.at[b%2],blk_sem.at[b%2])
     tok_load(0).start(); tok_load(1).start()
     def input_grad(b,rows):
@@ -653,7 +756,7 @@
             out.append(dot(gs[0],ws[0],NT)+dot(gs[1],ws[1],NT)+dot(gs[2],ws[2],NT))
         return jnp.concatenate(out,axis=1)
     for b in range(NB//2):
-        ghb[theirs(b),:]=input_grad(b,theirs(b)).astype(jnp.bfloat16)
+        ghb[b*R:(b+1)*R,:]=input_grad(b,theirs(b)).astype(jnp.bfloat16)
         ex_g1[b].start()
         for a in plan.get(("t",b),[]): a()
     gsum=None
@@ -690,66 +793,82 @@
     while gi<gain_steps: gain_step(gi); gi+=1
     gout=pltpu.make_async_copy(gain_v.at[2*gain_steps],gains_o,blk_sem.at[0])
     gout.start()
-    for r in runs.values(): r.drain()
+    for g in gathers.values(): g.drain()
+    for r in runs.values(): r.drain_sends()
     gout.wait()
-    for c in ex_gh+ex_op+ex_g1+ex_gain: c.wait_send()
+    for c in ex_g1+ex_gain: c.wait_send()
     @pl.when(off)
     def _():
-        for c in sw_out+sw_gf+sw_gt: c.wait()
+        for c in sw_out+sum(sw_gf,[])+sw_gt: c.wait()
     @pl.when(diag)
     def _():
-        for c in lo_out+lo_gf+lo_gt: c.wait()
-
-def back(groups,length8,tok,pa,pb,og,op,gh,att,comb,q,k,m,wq,wk,wv,wo,lse,g1,g2,tables):
+        for c in lo_out+sum(lo_gf,[])+lo_gt: c.wait()
+
+def FF_TILES(rows,W,D):
+    return (rows-4*W*D//128)//(3*D)
+
+def back(groups,length8,tok,pa,pb,og,op,opr,gh,ghr,att,rest,leaf,q,k,m,wq,wk,wv,wo,lse,g1,g2,tables,tiles):
     bf=jnp.bfloat16; f32=jnp.float32; S=jax.ShapeDtypeStruct; V=pltpu.VMEM
     N,D=tok.shape; half=N//2; W=wo.shape[0]; NP=W//128; R=256
-    KB=1024; units=comb.shape[0]//KB
-    rows=comb.shape[0]+W*D//128+3*W*D//128
+    rows=3*tiles*D+W*D//128+3*W*D//128
     levels=1+int(math.log2(groups))
     per=lambda n:sum(n>>(l+1) for l in range(levels))
-    cut=[units//4]*3+[units-3*(units//4)]
-    recv=sum(per(c*KB)-c*KB//2 for c in cut)+per(W*D//128)+NP*per(3*D)
+    recv=sum(per(r[4]) for r in runs_of(tiles,D//128) if r[0]>=2)+per(W*D//128)+NP*per(3*D)
     anyb=pl.BlockSpec(memory_space=pl.ANY); vm=pl.BlockSpec(memory_space=pltpu.VMEM)
-    outs=[S((half,D),bf),S((half,D),bf),S((N,W),bf),S((rows,128),bf),S((16,D),f32),S((comb.shape[0]//2,128),bf)]
+    outs=[S((half,D),bf),S((half,D),bf),S((N,W),bf),S((rows,128),bf),S((16,D),f32)]
     gains=2*(2+levels-1)+1
-    scratch=[V((2,R,D),bf)]*5+[V((2,R,W),bf),V((half,D),bf),V((half,D),bf),V((N,D),bf),V((N,D),bf),V((half,D),bf),V((NP,N,128),bf),V((NP,8,N),f32),
+    scratch=[V((2,R,D),bf)]*7+[V((2,R,W),bf),V((half,D),bf),V((half,D),bf),V((half,D),bf),V((N,D),bf),V((half,D),bf),V((NP,N,128),bf),V((NP,8,N),f32),
         V((NP,N,128),bf),V((NP,N,128),bf),V((NP,N,128),bf),V((4,N,128),bf),V((4,N,128),bf),V((2,N,128),bf),V((N,128),f32),V((N,128),f32),V((N,128),f32),
-        V((W,D),bf),V((W,D),f32),V((2,max(cut)*KB//2,128),bf),V((max(cut)*KB//2,128),bf),V((recv,128),bf),V((W*D//128,128),bf),V((NP,3*D,128),bf),V((gains,16,D),f32),
-        pltpu.SemaphoreType.DMA((160,)),pltpu.SemaphoreType.DMA((160,)),pltpu.SemaphoreType.DMA((48,)),pltpu.SemaphoreType.DMA((18,)),pltpu.SemaphoreType.REGULAR]
+        V((W,D),bf),V((W,D),f32),V(rest.shape,bf),V(leaf.shape,bf),V((recv,128),bf),V((W*D//128,128),bf),V((NP,3*D,128),bf),V((gains,16,D),f32),
+        pltpu.SemaphoreType.DMA((192,)),pltpu.SemaphoreType.DMA((192,)),pltpu.SemaphoreType.DMA((64,)),pltpu.SemaphoreType.DMA((18,))]
     return pl.pallas_call(functools.partial(back_kernel,groups),out_shape=outs,
-        in_specs=[vm]+[anyb]*15+[vm]*7,out_specs=[anyb]*6,scratch_shapes=scratch,
+        in_specs=[vm]+[anyb]*18+[vm]*7,out_specs=[anyb]*5,scratch_shapes=scratch,
         compiler_params=pltpu.CompilerParams(collective_id=1,has_side_effects=True,vmem_limit_bytes=63<<20),name="back")(
-        length8,tok,pa,pb,og,op,gh,att,comb,q,k,m,wq,wk,wv,wo,lse,g1,g2,*tables)
-
-def make_schedule(levels,pairs):
-    plan={}
-    def put(key,*what): plan.setdefault(key,[]).append(what)
-    put(("m",5),"E","start"); put(("m",5),"F","start")
-    put((0,0),"A","prep"); put((0,1),"A","f",0); put((0,1),"B","prep"); put((0,2),"B","f",0)
-    put((1,4),"E","prep"); put((1,5),"E","f",0); put((1,5),"F","prep"); put((1,6),"F","f",0)
-    late={"A":[(1,2),(1,8),(2,2)],"B":[(1,3),(1,9),(2,3)],"E":[(2,2),(2,7),(3,0)],"F":[(2,3),(2,8),(3,1)],
-          "C":[(0,6),(1,0),(1,4),(1,7)],0:[(1,8),(2,1),(2,5),(2,9)],1:[(2,6),(3,0),(3,4),(3,7)],2:[(3,5),(3,9),("t",1),("u",0)]}
-    gather={"A":[(2,6),(3,0),(3,3),(3,9)],"B":[(2,7),(3,1),(3,4),("t",0)],"C":[(2,4),(2,8),(3,2),(3,6)],
-            "E":[(3,4),(3,8),("t",1),("u",2)],"F":[(3,5),(3,9),("t",2),("u",3)],0:[(3,3),(3,7),("t",0),("u",0)],1:[("t",0),("t",3),("u",1)]}
-    rest=[]
-    for name in ["C","A","B",0,"E","F",1,2,3]:
-        first=1 if name in ("A","B","E","F") else 0
-        keys=late.get(name,[])
-        more=levels-first-len(keys)
-        for i in range(levels-first):
-            if i<len(keys): put(keys[i],name,"f",first+i)
-            else: rest.append((name,"f",first+i))
-        keys=gather.get(name,[]) if more<=0 else []
-        for i in range(levels):
-            if i<len(keys): put(keys[i],name,"g",i)
-            else: rest.append((name,"g",i))
-    queues={}
-    for r in rest: queues.setdefault(r[0],[]).append(r)
-    while queues:
-        for n in list(queues):
-            put("end",*queues[n].pop(0))
-            if not queues[n]: del queues[n]
-    return plan
+        length8,tok,pa,pb,og,op,opr,gh,ghr,att,rest,leaf,q,k,m,wq,wk,wv,wo,lse,g1,g2,*tables)
+
+BACK_PLAN={
+    ('m', 7):[('c1','g',0)],
+    (0, 0):[('a2','f',0),('b3','f',0),('a0','g',0),('a1','g',0),('b0','g',0)],
+    (0, 3):[('b1','g',0),('out','s',0)],
+    (0, 4):[('out','s',1)],
+    (0, 5):[('out','s',2)],
+    (0, 6):[('b3','f',1),('out','s',3)],
+    (0, 7):[('C','f',0),('out','s',4)],
+    (0, 8):[('a0','g',1),('out','s',5)],
+    (0, 9):[('b0','g',1),('out','s',6)],
+    (1, 0):[('C','f',1),('a2','f',1),('a1','g',1),('out','s',7)],
+    (1, 1):[('b1','g',1),(('gf',0),'s',0)],
+    (1, 2):[('a0','g',2),(('gf',0),'s',1)],
+    (1, 3):[('b3','f',2)],
+    (1, 4):[('c1','g',1)],
+    (1, 6):[('C','f',2)],
+    (1, 7):[('b0','g',2),('a0','g',3)],
+    (1, 9):[('a2','f',2)],
+    (2, 1):[(0,'f',0),('b0','g',3),(('gf',1),'s',0)],
+    (2, 2):[(('gf',1),'s',1)],
+    (2, 3):[('b1','g',2),('c1','g',2)],
+    (2, 4):[(0,'f',1),('a2','f',3)],
+    (2, 5):[('b3','f',3),('a1','g',2)],
+    (2, 6):[('C','f',3),('a2','g',0)],
+    (2, 7):[(0,'f',2),('b3','g',0),('b1','g',3),('c1','g',3)],
+    (2, 8):[('C','g',0),('a1','g',3)],
+    (3, 0):[(1,'f',0)],
+    (3, 1):[(0,'f',3),(0,'g',0),('b3','g',1),(('gf',2),'s',0)],
+    (3, 2):[('a2','g',1),(('gf',2),'s',1)],
+    (3, 3):[('C','g',1)],
+    (3, 5):[(1,'f',1),(1,'f',2)],
+    (3, 8):[(2,'f',0)],
+    ('t', 0):[(0,'g',1),('a2','g',2),('b3','g',2),(('gf',3),'s',0)],
+    ('t', 1):[(2,'f',1),(('gf',3),'s',1)],
+    ('t', 3):[('C','g',2)],
+    ('u', 1):[(2,'f',2),(1,'f',3),('a2','g',3)],
+    ('u', 3):[(1,'g',0)],
+}
+BACK_END=[
+    ('b3','g',3),(3,'f',0),(0,'g',2),('C','g',3),(2,'f',3),(1,'g',1),(3,'f',1),(1,'g',2),
+    (0,'g',3),(1,'g',3),(2,'g',0),(3,'f',2),(2,'g',1),(3,'f',3),(3,'g',0),(2,'g',2),
+    (3,'g',1),(2,'g',3),(3,'g',2),(3,'g',3),
+]
 
 def unpack_kernel(jobs,slots,*refs):
     src=refs[0]; n=max(j[2] for j in jobs)+1
@@ -776,9 +895,11 @@
 
 def unpack_all(buf,rows,D,FH,W):
     t=FH//128; n=W//128; d=D//128; slots=8
-    jobs=[(c*D,D,0,0,c) for c in range(t)]+[((t+c)*D,D,1,0,c) for c in range(t)]
-    pos=2*t*D
-    jobs+=[(pos+c*FH,FH,2,0,c) for c in range(d)]; pos+=d*FH
+    jobs=[]; pos=0; first=0
+    for m in passes_of(t):
+        jobs+=[(pos+(j*m+c)*D,D,j,0,first+c) for j in range(2) for c in range(m)]; pos+=2*m*D
+        jobs+=[(pos+c*128*m,128*m,2,first*128,c) for c in range(d)]; pos+=d*128*m
+        first+=m
     jobs+=[(pos+c*W,W,3,0,c) for c in range(d)]; pos+=d*W
     jobs+=[(pos+(p*3+j)*D,D,4+j,0,p) for p in range(n) for j in range(3)]
     shapes=[(D,FH),(D,FH),(FH,D),(W,D),(D,W),(D,W),(D,W)]
@@ -802,9 +923,8 @@
     tables=(jnp.cos(coarse),jnp.sin(coarse),jnp.cos(fine),jnp.sin(fine))
     length8=jnp.broadcast_to(lengths.reshape(1,1),(8,128))
     (tok,og,len_full,q,k,mixed,att,lse,pa,pb,w_q,w_k,w_v,w_o,w_g,w_u,w_d)=front(n,tokens,first_values,out_grad,length8,g1,tables,(w_query,w_key,w_value,w_out,w_gate,w_up,w_down))
-    length=len_full[0,:1]
-    op,gh2a,comb=mlp(length,tok,pa,pb,og,g2,w_gate,w_up,w_down,w_g,w_u,w_d)
-    out,grad_tokens,grad_first,packed,gains,_=back(n,len_full,tok,pa,pb,og,op,gh2a,att,comb,q,k,mixed,w_q,w_k,w_v,w_o,lse,g1,g2,tables)
+    op,opr,gh,ghr,rest,leaf=mlp(n,len_full,tok,pa,pb,og,g2,(w_gate,w_up,w_down),(w_g,w_u,w_d))
+    out,grad_tokens,grad_first,packed,gains=back(n,len_full,tok,pa,pb,og,op,opr,gh,ghr,att,rest,leaf,q,k,mixed,w_q,w_k,w_v,w_o,lse,g1,g2,tables,w_gate.shape[1]//128)
     gains=jnp.sum(gains.reshape(2,8,D),axis=1)
     FH=w_gate.shape[1]; W=w_query.shape[1]
     gwg,gwu,gwd,gwo,gwq,gwk,gwv,out,grad_tokens,grad_first=unpack_all(packed,(out,grad_tokens,grad_first),D,FH,W)

time: 477 us -> 453 us (0.950)
  Pallas kernels: 463 us -> 440 us
    pallas_call x1, Pallas kernels: 253 us -> 197 us  [back(): pl.pallas_call(functools.partial(back_kernel, groups), out_shape=outs, in...]
    pallas_call x1, Pallas kernels: 76.8 us -> 108 us  [mlp(): pl.pallas_call(functools.partial(mlp_kernel, groups), out_shape=outs, in_...]
where the time goes in v3:
time: 453 us; the launch traced here: 445 us
  Pallas kernels  440 us (97%)
    pallas_call x1, Pallas kernels, back(): pl.pallas_call(functools.partial(back_kernel, groups), out_shape=outs, in...  197 us
    pallas_call x1, Pallas kernels, front(): pl.pallas_call(functools.partial(front_kernel, groups), out_shape=outs, i...  118 us
    pallas_call x1, Pallas kernels, mlp(): pl.pallas_call(functools.partial(mlp_kernel, groups), out_shape=outs, in_...  108 us
    pallas_call x1, Pallas kernels, unpack_all(): pl.pallas_call(functools.partial(unpack_kernel, jobs, slots), in_specs=[a...  18 us

profile of v3, /device:TPU:0, one launch (start us, length us, event | category | flops | bytes accessed | tf_op | source)
XLA Modules:
  0.0 445.4 jit_solution(16161672757131384270)
XLA Ops:
  1.3 0.6 broadcast_in_dim.5.len_h
  1.9 0.8 multiply_sine_fusion.1
  2.7 0.8 multiply_sine_fusion
  3.5 117.6 %front.1 = (bf16[2048,1024]{1,0:T(8,128)(2,1)}, bf16[2048,1024]{1,0:T(8,128)(2,1)}, s32[8,128]{1,0:T(8,128)}, bf16[4,2048,128]{2,1,0:T(8,128)(2,1)}, bf16[4,2048...) custom-call(bf16[1024,1024]{1,0:T(8,128)(2,1)} %tok_h.1, ...), custom_call_target="tpu_custom_call" | custom-call | tf_op jit(solution)/shard_map/front/pallas_call | solution.py:282
  121.1 107.7 %mlp.1 = (bf16[2048,1024]{1,0:T(8,128)(2,1)}, bf16[1024,1024]{1,0:T(8,128)(2,1)}, bf16[2048,1024]{1,0:T(8,128)(2,1)}, bf16[2048,1024]{1,0:T(8,128)(2,1)}, bf16[1...) custom-call(s32[8,128]{1,0:T(8,128)} %get-tuple-element.50.len_ref, bf16[2048,1024]{1,0:T(8,128)(2,1)} %get-tuple-element.51.tok_h, ...), custom_call_target="tpu_custom_call" | custom-call | tf_op jit(solution)/shard_map/mlp/pallas_call | solution.py:543
  228.9 196.8 %back.1 = (bf16[1024,1024]{1,0:T(8,128)(2,1)}, bf16[1024,1024]{1,0:T(8,128)(2,1)}, bf16[2048,512]{1,0:T(8,128)(2,1)}, bf16[50176,128]{1,0:T(8,128)(2,1)}, f32[16,1024]{1,0:T(8,128)}) custom-call(s32[8,128]{1,0:T(8,128)} %get-tuple-element.50.len_ref, bf16[2048,1024]{1,0:T(8,128)(2,1)} %get-tuple-element.51.tok_h, bf16[2048,1024]{1,0:T(8,128)(2,1)} %get-tuple-element.52.pa_h, ...), custom_call_target="tpu_custom_call" | custom-call | tf_op jit(solution)/shard_map/back/pallas_call | solution.py:824
  425.7 0.9 bitcast_reduce_fusion
  426.6 0.6 fusion.3
  427.2 18.0 %unpack.1 = (f32[1024,1408]{1,0:T(8,128)}, f32[1024,1408]{1,0:T(8,128)}, f32[1408,1024]{1,0:T(8,128)}, f32[512,1024]{1,0:T(8,128)}, f32[1024,512]{1,0:T(8,128)},...) custom-call(bf16[50176,128]{1,0:T(8,128)(2,1)} %get-tuple-element.73, ...), custom_call_target="tpu_custom_call" | custom-call | tf_op jit(solution)/shard_map/unpack/pallas_call | solution.py:908
  (3 shorter events, 0.0 us)

commit v4 on v3

--- a/solution.py
+++ b/solution.py
@@ -101,8 +101,11 @@
         pl.semaphore_signal(barrier,inc=1,device_id=swap_dev,device_id_type=MESH)
         for b in bits: pl.semaphore_signal(barrier,inc=1,device_id=peer(b),device_id_type=MESH)
         pl.semaphore_wait(barrier,2+len(bits))
-        for n in "qkvog": sp[n].steps[0].start()
+        for n in "qkvg": sp[n].steps[0].start()
         swap_len.start()
+        for c in swap_tok: c.start()
+        for n in "oud": sp[n].steps[0].start()
+        for c in swap_fv+swap_og: c.start()
     @pl.when(diag)
     def _():
         pl.semaphore_wait(barrier,1)
@@ -125,13 +128,11 @@
     lax.fori_loop(0,SLOT//32,table,0)
     nl=len(bits)
     def advance(n,level):
-        sp[n].steps[level].wait_recv(); sp[n].steps[level+1].start()
+        if level<nl:
+            sp[n].steps[level].wait_recv(); sp[n].steps[level+1].start()
     @pl.when(off)
     def _():
-        for level in range(nl):
-            for n in ("qkvog" if level<max(nl-1,1) else "qkv"): advance(n,level)
-            if level==0:
-                for k in range(NC): swap_tok[k].start()
+        for n,level in (("q",0),("k",0),("v",0),("q",1),("k",1),("g",0),("v",1),("q",2),("k",2),("v",2),("g",1)): advance(n,level)
         swap_len.wait_recv()
     @pl.when(diag)
     def _():
@@ -162,30 +163,24 @@
         project(x*NC+k)
         @pl.when(off)
         def _():
-            if k==0: sp["u"].steps[0].start(); swap_fv[0].start()
-            if k==1 and nl>1: advance("o",nl-1)
-            if k==2 and nl>1: advance("g",nl-1)
-            if k==3: advance("u",0)
+            if k==0: advance("g",2)
+            if k==1: advance("u",0); advance("o",0)
+            if k==3: advance("d",0)
     for k in range(NC):
         @pl.when(off)
         def _():
             swap_tok[k].wait_recv()
             core_tok[k].start()
-            if k==1: swap_fv[1].start(); sp["d"].steps[0].start()
+            if k==3: advance("u",1)
         @pl.when(diag)
         def _():
             core_tok[k].wait_recv()
         project((1-x)*NC+k)
-    @pl.when(off)
-    def _():
-        swap_fv[2].start(); swap_fv[3].start()
     for c in outs: c.start()
     plan={}
     todo=lambda slot,act: plan.setdefault(slot,[]).append(act)
-    for level in range(1,nl): todo(4*(level-1),functools.partial(advance,"u",level))
-    for level in range(nl): todo(3+4*level if level<2 else 10,functools.partial(advance,"d",level))
-    todo(4,swap_og[0].start); todo(7,swap_og[1].start)
-    todo(12,lambda:(swap_og[0].wait_recv(),core_og[0].start()))
+    for slot,n,level in ((0,"o",1),(2,"d",1),(4,"u",2),(5,"o",2),(8,"d",2)): todo(slot,functools.partial(advance,n,level))
+    todo(11,lambda:(swap_og[0].wait_recv(),core_og[0].start()))
     BQ,BK=512,512
     laneq=lax.broadcasted_iota(jnp.int32,(BQ,128),1)
     lane=lax.broadcasted_iota(jnp.int32,(SLOT,128),1)
@@ -377,7 +372,7 @@
     KB=1024; pos=0; out=[]
     for t,n in enumerate(passes_of(tiles)):
         units=(2*n*d_tiles*128+d_tiles*128*n)//KB
-        parts=[[units//2,units-units//2],[units//3,units//3,units-2*(units//3)],[units],[0,units]][t]
+        parts=[[units//3,units//3,units-2*(units//3)],[units//3,units//3,units-2*(units//3)],[units],[0,units]][t]
         for i,u in enumerate(parts):
             if u: out.append((t,"abc"[i]+str(t),i,pos,u*KB))
             pos+=u*KB
@@ -386,12 +381,19 @@
     return [["x"]+bits,bits[:1]+["x"]+bits[1:],bits[1:2]+bits[:1]+["x"]+bits[2:]]
 
 MLP_PLAN={
-    (2, 0):[('a0',0),('b0',0)],
-    (2, 6):[('a1',0),('b1',0),('c1',0)],
-    (3, 2):[('a0',1),('b0',1)],
-    (3, 4):[('a1',1),('b1',1)],
-    (3, 5):[('c1',1),('a0',2)],
-    (3, 7):[('b0',2)],
+    (1, 6):[('a0',0),('b0',0),('c0',0)],
+    (2, 1):[('a0',1),('b0',1)],
+    (2, 4):[('c0',1)],
+    (2, 6):[('a1',0),('c1',0)],
+    (2, 7):[('b1',0),('a0',2),('c0',2)],
+    (3, 0):[('b0',2)],
+    (3, 1):[('a1',1),('a0',3)],
+    (3, 2):[('b1',1)],
+    (3, 3):[('c1',1),('c0',3)],
+    (3, 4):[('b0',3)],
+    (3, 5):[('a1',2)],
+    (3, 6):[('b1',2),('c1',2)],
+    (3, 7):[('a1',3)],
 }
 def mlp_kernel(groups,len_ref,tok_h,pa_h,pb_h,og_h,g_ref,wg_h,wu_h,wd_h,wg_f,wu_f,wd_f,
         op_o,opr_o,gh_o,ghr_o,rest_o,leaf_o,
@@ -827,47 +829,51 @@
         length8,tok,pa,pb,og,op,opr,gh,ghr,att,rest,leaf,q,k,m,wq,wk,wv,wo,lse,g1,g2,*tables)
 
 BACK_PLAN={
-    ('m', 7):[('c1','g',0)],
-    (0, 0):[('a2','f',0),('b3','f',0),('a0','g',0),('a1','g',0),('b0','g',0)],
-    (0, 3):[('b1','g',0),('out','s',0)],
+    ('m', 6):[('a0','g',0)],
+    (0, 0):[('a2','f',0),('b3','f',0),('b0','g',0),('c0','g',0)],
+    (0, 1):[('c1','g',0)],
+    (0, 2):[('b1','g',0)],
+    (0, 3):[('out','s',0)],
     (0, 4):[('out','s',1)],
     (0, 5):[('out','s',2)],
-    (0, 6):[('b3','f',1),('out','s',3)],
-    (0, 7):[('C','f',0),('out','s',4)],
-    (0, 8):[('a0','g',1),('out','s',5)],
-    (0, 9):[('b0','g',1),('out','s',6)],
-    (1, 0):[('C','f',1),('a2','f',1),('a1','g',1),('out','s',7)],
-    (1, 1):[('b1','g',1),(('gf',0),'s',0)],
+    (0, 6):[('b3','f',1),('a0','g',1),('out','s',3)],
+    (0, 7):[('C','f',0),('a1','g',0),('out','s',4)],
+    (0, 8):[('b0','g',1),('out','s',5)],
+    (0, 9):[('c0','g',1),('out','s',6)],
+    (1, 0):[('C','f',1),('c1','g',1),('out','s',7)],
+    (1, 1):[(('gf',0),'s',0)],
     (1, 2):[('a0','g',2),(('gf',0),'s',1)],
-    (1, 3):[('b3','f',2)],
-    (1, 4):[('c1','g',1)],
+    (1, 3):[('b3','f',2),('a1','g',1),('b1','g',1)],
+    (1, 4):[('a2','f',1)],
+    (1, 5):[('b0','g',2),('a0','g',3)],
     (1, 6):[('C','f',2)],
-    (1, 7):[('b0','g',2),('a0','g',3)],
-    (1, 9):[('a2','f',2)],
-    (2, 1):[(0,'f',0),('b0','g',3),(('gf',1),'s',0)],
-    (2, 2):[(('gf',1),'s',1)],
-    (2, 3):[('b1','g',2),('c1','g',2)],
-    (2, 4):[(0,'f',1),('a2','f',3)],
-    (2, 5):[('b3','f',3),('a1','g',2)],
-    (2, 6):[('C','f',3),('a2','g',0)],
-    (2, 7):[(0,'f',2),('b3','g',0),('b1','g',3),('c1','g',3)],
-    (2, 8):[('C','g',0),('a1','g',3)],
+    (1, 9):[('b0','g',3)],
+    (2, 1):[(0,'f',0),('c0','g',2),(('gf',1),'s',0)],
+    (2, 2):[('a2','f',2),(('gf',1),'s',1)],
+    (2, 5):[('b3','f',3),('c1','g',2),('c0','g',3)],
+    (2, 6):[('C','f',3),('b1','g',2)],
+    (2, 7):[('a2','f',3),('b3','g',0)],
+    (2, 8):[(0,'f',1),('C','g',0),('a1','g',2)],
+    (2, 9):[('a2','g',0),('c1','g',3)],
     (3, 0):[(1,'f',0)],
-    (3, 1):[(0,'f',3),(0,'g',0),('b3','g',1),(('gf',2),'s',0)],
-    (3, 2):[('a2','g',1),(('gf',2),'s',1)],
-    (3, 3):[('C','g',1)],
-    (3, 5):[(1,'f',1),(1,'f',2)],
+    (3, 1):[('a1','g',3),(('gf',2),'s',0)],
+    (3, 2):[(0,'f',2),('b1','g',3),(('gf',2),'s',1)],
+    (3, 3):[(1,'f',1),('C','g',1),('b3','g',1)],
+    (3, 5):[('a2','g',1)],
+    (3, 7):[(1,'f',2)],
     (3, 8):[(2,'f',0)],
-    ('t', 0):[(0,'g',1),('a2','g',2),('b3','g',2),(('gf',3),'s',0)],
-    ('t', 1):[(2,'f',1),(('gf',3),'s',1)],
+    ('t', 0):[(2,'f',1),(0,'f',3),('b3','g',2),(('gf',3),'s',0)],
+    ('t', 1):[(1,'f',3),(('gf',3),'s',1)],
+    ('t', 2):[(0,'g',0)],
     ('t', 3):[('C','g',2)],
-    ('u', 1):[(2,'f',2),(1,'f',3),('a2','g',3)],
-    ('u', 3):[(1,'g',0)],
+    ('u', 0):[(2,'f',2)],
+    ('u', 2):[('a2','g',2)],
+    ('u', 3):[(0,'g',1)],
 }
 BACK_END=[
-    ('b3','g',3),(3,'f',0),(0,'g',2),('C','g',3),(2,'f',3),(1,'g',1),(3,'f',1),(1,'g',2),
-    (0,'g',3),(1,'g',3),(2,'g',0),(3,'f',2),(2,'g',1),(3,'f',3),(3,'g',0),(2,'g',2),
-    (3,'g',1),(2,'g',3),(3,'g',2),(3,'g',3),
+    ('b3','g',3),(3,'f',0),(0,'g',2),('C','g',3),(1,'g',0),(1,'g',1),(2,'f',3),(3,'f',1),
+    (0,'g',3),(1,'g',2),(2,'g',0),(1,'g',3),(3,'f',2),(2,'g',1),(3,'f',3),(3,'g',0),
+    (2,'g',2),(3,'g',1),(2,'g',3),(3,'g',2),('a2','g',3),(3,'g',3),
 ]
 
 def unpack_kernel(jobs,slots,*refs):

time: 453 us -> 433 us (0.956)
  Pallas kernels: 440 us -> 422 us
    pallas_call x1, Pallas kernels: 108 us -> 97.6 us  [mlp(): pl.pallas_call(functools.partial(mlp_kernel, groups), out_shape=outs, in_...]
    pallas_call x1, Pallas kernels: 118 us -> 113 us  [front(): pl.pallas_call(functools.partial(front_kernel, groups), out_shape=outs, i...]
where the time goes in v4:
time: 433 us; the launch traced here: 427 us
  Pallas kernels  422 us (97%)
    pallas_call x1, Pallas kernels, back(): pl.pallas_call(functools.partial(back_kernel, groups), out_shape=outs, in...  194 us
    pallas_call x1, Pallas kernels, front(): pl.pallas_call(functools.partial(front_kernel, groups), out_shape=outs, i...  113 us
    pallas_call x1, Pallas kernels, mlp(): pl.pallas_call(functools.partial(mlp_kernel, groups), out_shape=outs, in_...  97.6 us
    pallas_call x1, Pallas kernels, unpack_all(): pl.pallas_call(functools.partial(unpack_kernel, jobs, slots), in_specs=[a...  18 us

profile of v4, /device:TPU:0, one launch (start us, length us, event | category | flops | bytes accessed | tf_op | source)
XLA Modules:
  0.0 427.3 jit_solution(17118569145828587836)
XLA Ops:
  1.3 0.6 broadcast_in_dim.5.len_h
  1.9 0.8 multiply_sine_fusion.1
  2.7 0.8 multiply_sine_fusion
  3.5 112.6 %front.1 = (bf16[2048,1024]{1,0:T(8,128)(2,1)}, bf16[2048,1024]{1,0:T(8,128)(2,1)}, s32[8,128]{1,0:T(8,128)}, bf16[4,2048,128]{2,1,0:T(8,128)(2,1)}, bf16[4,2048...) custom-call(bf16[1024,1024]{1,0:T(8,128)(2,1)} %tok_h.1, ...), custom_call_target="tpu_custom_call" | custom-call | tf_op jit(solution)/shard_map/front/pallas_call | solution.py:277
  116.1 97.6 %mlp.1 = (bf16[2048,1024]{1,0:T(8,128)(2,1)}, bf16[1024,1024]{1,0:T(8,128)(2,1)}, bf16[2048,1024]{1,0:T(8,128)(2,1)}, bf16[2048,1024]{1,0:T(8,128)(2,1)}, bf16[1...) custom-call(s32[8,128]{1,0:T(8,128)} %get-tuple-element.50.len_ref, bf16[2048,1024]{1,0:T(8,128)(2,1)} %get-tuple-element.51.tok_h, ...), custom_call_target="tpu_custom_call" | custom-call | tf_op jit(solution)/shard_map/mlp/pallas_call | solution.py:545
  213.7 193.8 %back.1 = (bf16[1024,1024]{1,0:T(8,128)(2,1)}, bf16[1024,1024]{1,0:T(8,128)(2,1)}, bf16[2048,512]{1,0:T(8,128)(2,1)}, bf16[50176,128]{1,0:T(8,128)(2,1)}, f32[16,1024]{1,0:T(8,128)}) custom-call(s32[8,128]{1,0:T(8,128)} %get-tuple-element.50.len_ref, bf16[2048,1024]{1,0:T(8,128)(2,1)} %get-tuple-element.51.tok_h, bf16[2048,1024]{1,0:T(8,128)(2,1)} %get-tuple-element.52.pa_h, ...), custom_call_target="tpu_custom_call" | custom-call | tf_op jit(solution)/shard_map/back/pallas_call | solution.py:826
  407.6 0.9 bitcast_reduce_fusion
  408.4 0.6 fusion.3
  409.0 18.0 %unpack.1 = (f32[1024,1408]{1,0:T(8,128)}, f32[1024,1408]{1,0:T(8,128)}, f32[1408,1024]{1,0:T(8,128)}, f32[512,1024]{1,0:T(8,128)}, f32[1024,512]{1,0:T(8,128)},...) custom-call(bf16[50176,128]{1,0:T(8,128)(2,1)} %get-tuple-element.73, ...), custom_call_target="tpu_custom_call" | custom-call | tf_op jit(solution)/shard_map/unpack/pallas_call | solution.py:914
  (3 shorter events, 0.0 us)
